TPU v7x, 128 devices: a whole 4x4x4 slice. The times are simulated.
128 devices in a mesh: dp: 32 (over x, y_lo, z), tensor: 4 (over y_hi, core).
Axes of the slice: x: 4, y: 4 (y_hi: 2, y_lo: 2; y = y_hi * 2 + y_lo), z: 4, core: 2. Of those that a mesh axis runs over, the one named last changes fastest.
Arguments:
- tokens: bfloat16 [32768, 1536], P('dp'), may hold values from -6 to 6
- segment: int32 [32, 1024], P('dp'), may hold values from 0 to 3, never falling along the last dimension, each value on 1 to 512 neighbouring positions
- gate_proj: bfloat16 [1536, 3072], P(None, 'tensor'), may hold values from -0.15625 to 0.15625
- value_proj: bfloat16 [1536, 3072], P(None, 'tensor'), may hold values from -0.15625 to 0.15625
- state_proj: bfloat16 [1536, 256], replicated, may hold values from -0.15625 to 0.15625
- step_proj: bfloat16 [1536, 48], P(None, 'tensor'), may hold values from -0.15625 to 0.15625
- value_conv: float32 [4, 3072], P(None, 'tensor'), may hold values from -3 to 3
- value_conv_bias: float32 [3072], P('tensor'), may hold values from -3 to 3
- state_conv: float32 [4, 256], replicated, may hold values from -3 to 3
- state_conv_bias: float32 [256], replicated, may hold values from -3 to 3
- step_bias: float32 [48], P('tensor'), may hold values from -7 to -3
- log_rate: float32 [48], P('tensor'), may hold values from 0 to 2.3
- bypass_gain: float32 [48], P('tensor'), may hold values from 0.5 to 1.5
- norm_gain: float32 [1536], replicated, may hold values from 0.5 to 1.5
- gated_norm_gain: float32 [3072], P('tensor'), may hold values from 0.5 to 1.5
- out_proj: bfloat16 [3072, 1536], P('tensor'), may hold values from -0.109375 to 0.109375
- cotangent: bfloat16 [32768, 1536], P('dp'), may hold values from -6 to 6
Outputs:
- mixed_out: bfloat16 [32768, 1536], P('dp')
- grad_tokens: float32 [32768, 1536], P('dp')
- grad_gate_proj: float32 [1536, 3072], P(None, 'tensor')
- grad_value_proj: float32 [1536, 3072], P(None, 'tensor')
- grad_state_proj: float32 [1536, 256], replicated
- grad_step_proj: float32 [1536, 48], P(None, 'tensor')
- grad_value_conv: float32 [4, 3072], P(None, 'tensor')
- grad_value_conv_bias: float32 [3072], P('tensor')
- grad_state_conv: float32 [4, 256], replicated
- grad_state_conv_bias: float32 [256], replicated
- grad_step_bias: float32 [48], P('tensor')
- grad_log_rate: float32 [48], P('tensor')
- gradient_bypass_gain: float32 [48], P('tensor')
- grad_norm_gain: float32 [1536], replicated
- grad_mixer_gain: float32 [3072], P('tensor')
- grad_out_proj: float32 [3072, 1536], P('tensor')
Inputs may be any that keep to these rules, and one draw needn't show every extreme that they name: `segment`: within each row of 1024 tokens the numbers never fall; each document has 1 to 512 tokens, and one has exactly that many.
All inputs are finite; a program needn't handle non-finite values.
Results may differ from a plain program's by a relative error of at most 0.025.
Values may be sent and summed in bfloat16 or wider, within the bound.
A program may use at most 192 MiB of HBM per device.

v0:
```python
import jax
import jax.numpy as jnp
from jax import lax
from jax.sharding import PartitionSpec as P

H = 48
P_SIZE = 64
SPAN = 256


EPS = 1e-05
HIGH_ACCURACY = lax.Precision.HIGHEST


def sent_to_all(shard, axis):
    copies = jnp.broadcast_to(shard, (lax.axis_size(axis), *shard.shape))
    return lax.all_to_all(copies, axis, split_axis=0, concat_axis=0, tiled=True)


def over_copies(shard, axis):
    everything = sent_to_all(shard, axis)
    return jnp.sum(everything, axis=0)


def in_blocks_2(shard, dim, count):
    lengths = shard.shape
    pieces = shard.reshape(*lengths[:dim], count, lengths[dim] // count, *lengths[dim + 1 :])
    return jnp.moveaxis(pieces, dim, 0)


def sum_at_owner(shard, axis, dim):
    pieces = in_blocks_2(shard, dim, lax.axis_size(axis))
    arrived = lax.all_to_all(pieces, axis, split_axis=0, concat_axis=0, tiled=True)
    return arrived.astype(jnp.float32).sum(axis=0)


def taken_together(shard, axis):
    return sent_to_all(shard, axis).astype(jnp.float32).sum(axis=0)


def causal_conv(values, kernel, offset, segment):
    length = values.shape[0]
    summed = offset + kernel[0] * values
    for lag_count in range(1, kernel.shape[0]):
        shifted = jnp.pad(values, ((lag_count, 0), (0, 0)))[:length]
        earlier = jnp.pad(segment, (lag_count, 0), constant_values=-1)[:length]
        keeper = (earlier == segment).astype(jnp.float32)[:, None]
        summed = summed + kernel[lag_count] * shifted * keeper
    return jax.nn.silu(summed)


def state_space(values, step_sizes, decay_rate, in_state, final_state, segment):
    length, head_count, head_dim = values.shape
    blocks = length // SPAN
    blocked = values.reshape(blocks, SPAN, head_count, head_dim)
    step_blocks = jnp.transpose(step_sizes.reshape(blocks, SPAN, head_count), (0, 2, 1))
    log_decay = step_blocks * decay_rate[None, :, None]
    row_index = lax.broadcasted_iota(jnp.int32, (SPAN, SPAN), 0)
    column_position = lax.broadcasted_iota(jnp.int32, (SPAN, SPAN), 1)
    lower_ones = (row_index >= column_position).astype(jnp.float32)
    cumulative = jnp.einsum("khs,ts->kht", log_decay, lower_ones, precision=HIGH_ACCURACY)
    seg_blocks = segment.reshape(blocks, SPAN)
    same_doc = (seg_blocks[:, :, None] == seg_blocks[:, None, :]) & (row_index >= column_position)[
        None
    ]
    log_gap = cumulative[:, :, :, None] - cumulative[:, :, None, :]
    decay_mat = jnp.exp(jnp.where(same_doc[:, None], log_gap, -1e30))
    in_blocks = in_state.reshape(blocks, SPAN, -1)
    out_blocks = final_state.reshape(blocks, SPAN, -1)
    scores = jnp.einsum("ktn,ksn->kts", out_blocks, in_blocks, precision=HIGH_ACCURACY)
    weights = scores[:, None] * decay_mat * step_blocks[:, :, None, :]
    inside = jnp.einsum("khts,kshp->kthp", weights, blocked, precision=HIGH_ACCURACY)
    last_doc = seg_blocks[:, -1]
    keep_end = (seg_blocks == last_doc[:, None]).astype(jnp.float32)
    tail_weight = jnp.exp(cumulative[:, :, -1:] - cumulative) * step_blocks * keep_end[:, None, :]
    states = jnp.einsum(
        "khs,kshp,ksn->khpn", tail_weight, blocked, in_blocks, precision=HIGH_ACCURACY
    )
    through = jnp.exp(cumulative[:, :, -1])
    carried = jnp.zeros((head_count, head_dim, in_state.shape[1]), jnp.float32)
    entering = []
    for block_id in range(blocks):
        entering.append(carried)
        if block_id == 0:
            carried = states[0]
        else:
            continues = last_doc[block_id] == last_doc[block_id - 1]
            carried = states[block_id] + jnp.where(
                continues, through[block_id][:, None, None] * carried, 0.0
            )
    before = jnp.stack(entering)
    prev_last = jnp.concatenate([jnp.full((1,), -1, jnp.int32), last_doc[:-1]])
    keep_start = (seg_blocks == prev_last[:, None]).astype(jnp.float32)
    growth = jnp.exp(cumulative) * keep_start[:, None, :]
    outside = jnp.einsum("ktn,khpn,kht->kthp", out_blocks, before, growth, precision=HIGH_ACCURACY)
    return (inside + outside).reshape(length, head_count, head_dim)


def mixer(
    value_in,
    state_in,
    step_in,
    value_kernel,
    value_offset,
    state_kernel,
    state_offset,
    step_offset,
    rate_log,
    skip_weight,
    segment,
):
    length = value_in.shape[0]
    conv_values = causal_conv(value_in, value_kernel, value_offset, segment)
    conv_state = causal_conv(state_in, state_kernel, state_offset, segment)
    head_count = step_offset.shape[0]
    state_size = conv_state.shape[1] // 2
    step_sizes = jax.nn.softplus(step_in + step_offset)
    decay_rate = -jnp.exp(rate_log)
    heads_view = conv_values.reshape(length, head_count, -1)
    result = state_space(
        heads_view,
        step_sizes,
        decay_rate,
        conv_state[:, :state_size],
        conv_state[:, state_size:],
        segment,
    )
    result = result + skip_weight[None, :, None] * heads_view
    return result.reshape(length, -1)


def apply_mixer(
    value_in,
    state_in,
    step_in,
    value_kernel,
    value_offset,
    state_kernel,
    state_offset,
    step_offset,
    rate_log,
    skip_weight,
    segment,
):
    mapped = jax.vmap(mixer, in_axes=(0, 0, 0, None, None, None, None, None, None, None, 0))
    return mapped(
        value_in,
        state_in,
        step_in,
        value_kernel,
        value_offset,
        state_kernel,
        state_offset,
        step_offset,
        rate_log,
        skip_weight,
        segment,
    )


def local(
    tokens,
    segment,
    gate_proj,
    value_proj,
    state_proj,
    step_proj,
    value_conv,
    value_conv_bias,
    state_conv,
    state_conv_bias,
    step_bias,
    log_rate,
    bypass_gain,
    norm_gain,
    gated_norm_gain,
    out_proj,
    cotangent,
):
    seq_count, length = segment.shape
    row_count, model_width = tokens.shape
    inner_width = H * P_SIZE
    hidden = tokens.astype(jnp.float32)
    inverse = lax.rsqrt(jnp.mean(hidden * hidden, -1, keepdims=True) + EPS)
    normed = (hidden * inverse * norm_gain).astype(jnp.bfloat16)
    gate_raw = jnp.dot(normed, gate_proj, preferred_element_type=jnp.float32)
    value_raw = jnp.dot(normed, value_proj, preferred_element_type=jnp.float32)
    state_raw = jnp.dot(normed, state_proj, preferred_element_type=jnp.float32)
    step_raw = jnp.dot(normed, step_proj, preferred_element_type=jnp.float32)

    def run_mixer(
        value_in,
        state_in,
        step_in,
        value_kernel,
        value_offset,
        state_kernel,
        state_offset,
        step_offset,
        rate_log,
        skip_weight,
    ):
        return apply_mixer(
            value_in,
            state_in,
            step_in,
            value_kernel,
            value_offset,
            state_kernel,
            state_offset,
            step_offset,
            rate_log,
            skip_weight,
            segment,
        )

    mixed_y, pull_mixer = jax.vjp(
        run_mixer,
        value_raw.reshape(seq_count, length, -1),
        state_raw.reshape(seq_count, length, -1),
        step_raw.reshape(seq_count, length, -1),
        value_conv,
        value_conv_bias,
        state_conv,
        state_conv_bias,
        step_bias,
        log_rate,
        bypass_gain,
    )
    mixed_y = mixed_y.reshape(row_count, -1)
    gate_act = jax.nn.silu(gate_raw)
    gated = mixed_y * gate_act
    squares = over_copies(jnp.sum(gated * gated, -1), "tensor")
    gate_scale = lax.rsqrt(squares[:, None] / inner_width + EPS)
    gate_normed = (gated * gate_scale * gated_norm_gain).astype(jnp.bfloat16)
    branch_part = jnp.dot(gate_normed, out_proj, preferred_element_type=jnp.float32)
    shared = sum_at_owner(branch_part.astype(jnp.bfloat16), "tensor", 0)
    share_rows = shared.shape[0]
    own_rows = lax.dynamic_slice_in_dim(
        hidden, lax.axis_index("tensor") * share_rows, share_rows, 0
    )
    mixed_out = lax.all_gather(
        (own_rows + shared).astype(jnp.bfloat16), "tensor", axis=0, tiled=True
    )
    upstream = cotangent.astype(jnp.float32)
    grad_out_proj = jnp.dot(gate_normed.T, cotangent, preferred_element_type=jnp.float32)
    grad_gate_normed = jnp.dot(cotangent, out_proj.T, preferred_element_type=jnp.float32)
    grad_mixer_gain = jnp.sum(grad_gate_normed * gated * gate_scale, 0)
    scaled = grad_gate_normed * gated_norm_gain
    cross = over_copies(jnp.sum(scaled * gated, -1), "tensor")
    grad_gated = (
        gate_scale * scaled
        - gated * gate_scale * gate_scale * gate_scale * cross[:, None] / inner_width
    )
    grad_y = grad_gated * gate_act
    logistic = jax.nn.sigmoid(gate_raw)
    grad_gate_raw = grad_gated * mixed_y * logistic * (1.0 + gate_raw * (1.0 - logistic))
    pulled = pull_mixer(grad_y.reshape(seq_count, length, -1))
    grad_value_raw, grad_state_part, grad_step_raw = (pulled[0], pulled[1], pulled[2])
    grad_value_conv, grad_value_conv_bias = (pulled[3], pulled[4])
    grad_step_bias, grad_log_rate, gradient_bypass_gain = (pulled[7], pulled[8], pulled[9])
    grad_state_raw, grad_state_conv, grad_state_conv_bias = (
        taken_together(
            grad_state_part.reshape(row_count, -1).astype(jnp.bfloat16), "tensor"
        ).astype(jnp.float32),
        taken_together(pulled[5].astype(jnp.bfloat16), "tensor").astype(jnp.float32),
        taken_together(pulled[6].astype(jnp.bfloat16), "tensor").astype(jnp.float32),
    )
    gate_low = grad_gate_raw.astype(jnp.bfloat16)
    value_low = grad_value_raw.reshape(row_count, -1).astype(jnp.bfloat16)
    state_low = grad_state_raw.astype(jnp.bfloat16)
    step_low = grad_step_raw.reshape(row_count, -1).astype(jnp.bfloat16)
    grad_gate_proj = jnp.dot(normed.T, gate_low, preferred_element_type=jnp.float32)
    grad_value_proj = jnp.dot(normed.T, value_low, preferred_element_type=jnp.float32)
    grad_state_proj = jnp.dot(normed.T, state_low, preferred_element_type=jnp.float32)
    grad_step_proj = jnp.dot(normed.T, step_low, preferred_element_type=jnp.float32)
    normed_part = jnp.dot(gate_low, gate_proj.T, preferred_element_type=jnp.float32)
    normed_part = normed_part + jnp.dot(value_low, value_proj.T, preferred_element_type=jnp.float32)
    normed_part = normed_part + jnp.dot(step_low, step_proj.T, preferred_element_type=jnp.float32)
    grad_normed = lax.psum(normed_part.astype(jnp.bfloat16), "tensor").astype(
        jnp.float32
    ) + jnp.dot(state_low, state_proj.T, preferred_element_type=jnp.float32)
    grad_norm_gain = jnp.sum(grad_normed * hidden * inverse, 0)
    scaled_in = grad_normed * norm_gain
    grad_tokens = (
        upstream
        + inverse * scaled_in
        - hidden
        * inverse
        * inverse
        * inverse
        * jnp.sum(scaled_in * hidden, -1, keepdims=True)
        / model_width
    )
    summed = (
        lax.psum(grad_gate_proj.astype(jnp.bfloat16), "dp").astype(jnp.float32),
        lax.psum(grad_value_proj.astype(jnp.bfloat16), "dp").astype(jnp.float32),
        lax.psum(grad_state_proj.astype(jnp.bfloat16), "dp").astype(jnp.float32),
        lax.psum(grad_step_proj.astype(jnp.bfloat16), "dp").astype(jnp.float32),
        lax.psum(grad_value_conv.astype(jnp.bfloat16), "dp").astype(jnp.float32),
        lax.psum(grad_value_conv_bias.astype(jnp.bfloat16), "dp").astype(jnp.float32),
        lax.psum(grad_state_conv.astype(jnp.bfloat16), "dp").astype(jnp.float32),
        lax.psum(grad_state_conv_bias.astype(jnp.bfloat16), "dp").astype(jnp.float32),
        lax.psum(grad_step_bias.astype(jnp.bfloat16), "dp").astype(jnp.float32),
        lax.psum(grad_log_rate.astype(jnp.bfloat16), "dp").astype(jnp.float32),
        lax.psum(gradient_bypass_gain.astype(jnp.bfloat16), "dp").astype(jnp.float32),
        lax.psum(grad_norm_gain.astype(jnp.bfloat16), "dp").astype(jnp.float32),
        lax.psum(grad_mixer_gain.astype(jnp.bfloat16), "dp").astype(jnp.float32),
        lax.psum(grad_out_proj.astype(jnp.bfloat16), "dp").astype(jnp.float32),
    )
    return (
        mixed_out,
        grad_tokens,
        summed[0],
        summed[1],
        summed[2],
        summed[3],
        summed[4],
        summed[5],
        summed[6],
        summed[7],
        summed[8],
        summed[9],
        summed[10],
        summed[11],
        summed[12],
        summed[13],
    )


def solution(mesh):
    placed = (
        P("dp", None),
        P("dp", None),
        P(None, "tensor"),
        P(None, "tensor"),
        P(),
        P(None, "tensor"),
        P(None, "tensor"),
        P("tensor"),
        P(),
        P(),
        P("tensor"),
        P("tensor"),
        P("tensor"),
        P(),
        P("tensor"),
        P("tensor", None),
        P("dp", None),
    )
    return jax.shard_map(
        local,
        mesh=mesh,
        in_specs=placed,
        out_specs=(
            P("dp", None),
            P("dp", None),
            P(None, "tensor"),
            P(None, "tensor"),
            P(),
            P(None, "tensor"),
            P(None, "tensor"),
            P("tensor"),
            P(),
            P(),
            P("tensor"),
            P("tensor"),
            P("tensor"),
            P(),
            P("tensor"),
            P("tensor", None),
        ),
        check_vma=False,
    )
```

profile of v0, /device:TPU:0, one launch (start us, length us, event | category | flops | bytes accessed | tf_op | source)
XLA Modules:
  0.0 721.4 jit_solution(6264149762450902058)
XLA Ops:
  17.6 5.2 fusion.161
  31.0 5.1 reshape.708
  53.2 15.3 %bitcast_add_fusion.1 = f32[1,4,256,12,64]{2,4,3,1,0:T(8,128)S(1)} fusion(f32[4,12,64,256]{3,2,1,0:T(8,128)S(1)} %fusion.86, f32[4,12,256]{2,1,0:T(8,128)S(1)} %bitcast.434, f32[4,12,256]{2,1,0:T(8,128)S(1)} %fusion.106, f32[4,256,256]{2,1,0:T(8,128)S(1)} %fusion.163, pred[4,256,256]{2,1,0:T(8,128)(4,1)S(1)} %compare_and_fusion, ...), kind=kOutput, calls=%fused_computation.49 | convolution fusion | flops 2430074880 | bytes 10895360 | tf_op jit(solution)/shard_map/jvp(vmap(khts,kshp->kthp))/dot_general | solution.py:72
  76.6 9.8 %multiply_reduce_fusion.12 = (f32[1024]{0:T(1024)S(1)}, f32[1024,768]{1,0:T(8,128)}, f32[1024,768]{1,0:T(8,128)}) fusion(f32[1024,768]{1,0:T(8,128)} %copy.117, f32[1,1024,768]{2,1,0:T(8,128)} %get-tuple-element.69, f32[768]{0:T(1024)S(1)} %mul.787, bf16[1024,1536]{1,0:T(8,128)(2,1)} %copy-done.2, bf16[1536,768]{1,0:T(8,128)(2,1)S(1)} %copy-done), kind=kOutput, calls=%fused_computation.76 | convolution fusion | flops 2426141696 | bytes 18095104 | tf_op jit(solution)/shard_map/dot_general | solution.py:186
  86.4 9.7 %all_to_all.33 = f32[4,1,1024]{2,1,0:T(1,128)S(1)} all-to-all(f32[4,1,1024]{2,1,0:T(1,128)S(1)} %broadcast_in_dim.73), channel_id=1, replica_groups=mesh['dp'=32,'tensor'=4] {'tensor'}, dimensions={0} | all-to-all | bytes 32768 | tf_op jit(solution)/shard_map/all_to_all | solution.py:17
  97.4 8.5 %multiply_reduce_fusion.6 = (bf16[768]{0:T(1024)(128)(2,1)}, f32[1024]{0:T(1024)S(1)}, f32[1024,768]{1,0:T(8,128)}) fusion(f32[1024,768]{1,0:T(8,128)} %get-tuple-element.65, f32[1024]{0:T(1024)S(1)} %add_rsqrt_fusion, f32[768]{0:T(1024)} %param.31, bf16[1024,1536]{1,0:T(8,128)(2,1)} %param.33, bf16[768,1536]{1,0:T(8,128)(2,1)} %param.32), kind=kOutput, calls=%fused_computation.67 | convolution fusion | flops 2420635904 | bytes 11809280 | tf_op jit(solution)/shard_map/dot_general | solution.py:247
  109.8 7.0 convolution_convert_fusion
  122.1 9.3 %fusion.31 = (f32[768]{0:T(1024)}, f32[1024,768]{1,0:T(8,128)}, bf16[1024,768]{1,0:T(8,128)(2,1)}) fusion(f32[1,1024,768]{2,1,0:T(8,128)} %get-tuple-element.69, f32[1024,768]{1,0:T(8,128)} %get-tuple-element.101, f32[1024]{0:T(1024)} %reduce_sum.316, f32[1024,768]{1,0:T(8,128)} %get-tuple-element.65, f32[1024,768]{1,0:T(8,128)} %get-tuple-element.102, ...), kind=kLoop, calls=%fused_computation.59 | loop fusion | flops 22019328 | bytes 20464640 | tf_op jit(solution)/shard_map/transpose(jvp(vmap()))/reduce_sum | solution.py:128
  135.0 5.1 reshape.720
  140.1 5.2 reshape_reshape.4
  145.3 5.4 fusion.69
  153.0 21.2 %fusion.7 = (f32[4,12,256]{2,1,0:T(8,128)}, f32[4,12,256]{2,1,0:T(8,128)}, f32[4,12,256]{2,1,0:T(8,128)}, f32[4,256,256]{2,1,0:T(8,128)}) fusion(f32[4,12,256]{2,1,0:T(8,128)S(1)} %bitcast.435, f32[4,12,256]{2,1,0:T(8,128)S(1)} %fusion.106, f32[4,256,256]{2,1,0:T(8,128)S(1)} %copy-done.36, pred[4,256,256]{2,1,0:T(8,128)(4,1)S(1)} %copy-done.43, ...), kind=kOutput, calls=%fused_computation.9 | convolution fusion | flops 2456514560 | bytes 8896512 | tf_op jit(solution)/shard_map/transpose(jvp(vmap(khts,kshp->kthp)))/dot_general | solution.py:72
  177.0 11.8 %bitcast_add_fusion = f32[1,4,256,12,64]{2,4,3,1,0:T(8,128)S(1)} fusion(f32[4,256,12,64]{1,3,2,0:T(8,128)S(1)} %convolution_bitcast_fusion, f32[4,12,256]{2,1,0:T(8,128)S(1)} %bitcast.436, f32[4,12,256]{2,1,0:T(8,128)S(1)} %fusion.106, f32[4,256,256]{2,1,0:T(8,128)S(1)} %copy-done.36, pred[4,256,256]{2,1,0:T(8,128)(4,1)S(1)} %copy-done.43, ...), kind=kOutput, calls=%fused_computation.48 | convolution fusion | flops 2430074880 | bytes 10895360 | tf_op jit(solution)/shard_map/transpose(jvp(vmap(khts,kshp->kthp)))/dot_general | solution.py:72
  201.5 12.1 %multiply_reduce_fusion.10 = (f32[768]{0:T(1024)}, f32[768]{0:T(1024)}, f32[768]{0:T(1024)}, bf16[768]{0:T(1024)(128)(2,1)}, f32[768]{0:T(1024)}, /*index=5*/f32[1,1024,768]{2,1,0:T(8,128)}) fusion(f32[1,1024,768]{2,1,0:T(8,128)} %bitcast.392, f32[1024]{0:T(1024)S(1)} %bitcast.429, f32[1024]{0:T(1024)S(1)} %bitcast.423, f32[1024]{0:T(1024)S(1)} %bitcast.417, ...), kind=kLoop, calls=%fused_computation.71 | loop fusion | flops 18084096 | bytes 18903552 | tf_op jit(solution)/shard_map/transpose(jvp(vmap()))/reduce_sum | solution.py:48
  230.4 5.5 convert_element_type.172
  243.9 5.7 fusion.77
  251.6 7.7 %fusion.82 = f32[4,256,128]{2,1,0:T(8,128)S(1)} fusion(f32[4,256,12,64]{1,0,3,2:T(4,128)} %reshape.720, f32[4,256,12]{1,2,0:T(8,128)} %copy-done.45, f32[1,1,12,64,128]{4,3,2,1,0:T(8,128)} %copy-done.30, f32[1,1,12,64,128]{4,3,2,1,0:T(8,128)} %copy-done.31, f32[1,1,12,64,128]{4,3,2,1,0:T(8,128)} %copy-done.32, f32[1,1,12,64,128]{4,3,2,1,0:T(8,128)} %copy-done.29), kind=kOutput, calls=%fused_computation.119 | convolution fusion | flops 1209925632 | bytes 5292032 | tf_op jit(solution)/shard_map/transpose(jvp(vmap(ktn,khpn,kht->kthp)))/dot_general | solution.py:95
  269.3 7.3 %convolution_convert_fusion.1 = bf16[768,1536]{1,0:T(8,128)(2,1)} fusion(bf16[1024,1536]{1,0:T(8,128)(2,1)} %param.33, f32[1024,768]{1,0:T(8,128)} %get-tuple-element.65, f32[768]{0:T(1024)S(1)} %copy-done.91, f32[1024]{0:T(1024)S(1)} %copy-done.73), kind=kOutput, calls=%fused_computation.33 | convolution fusion | flops 2419458048 | bytes 8657920 | tf_op jit(solution)/shard_map/dot_general | solution.py:246
  284.5 25.1 %all-to-all-done.3 = bf16[4,1024,256]{2,1,0:T(8,128)(2,1)} async-done(((bf16[4,1024,256]{2,1,0:T(8,128)(2,1)}), bf16[4,1024,256]{2,1,0:T(8,128)(2,1)}, u32[]{:S(2)}, u32[]{:S(2)}) %all-to-all-start.3) | async-done | bytes 2097184 | tf_op jit(solution)/shard_map/all_to_all | solution.py:17
  330.0 5.0 all-to-all-done.4
  335.1 6.2 multiply_reduce_fusion.2
  341.4 159.6 %all-reduce.32 = (bf16[1536,12]{0,1:T(8,128)(2,1)S(1)}, bf16[4,768]{1,0:T(4,128)(2,1)S(1)}, bf16[768]{0:T(1024)(128)(2,1)S(1)}, bf16[4,256]{1,0:T(4,128)(2,1)S(1...) all-reduce(bf16[1536,12]{0,1:T(8,128)(2,1)S(1)} %convolution_conver, ...), channel_id=1, replica_groups=mesh['dp'=32,'tensor'=4] {'dp'}, use_global_device_ids=true, to_apply=%region_19.20 | all-reduce | flops 25892 | bytes 103568 | tf_op jit(solution)/shard_map/psum | solution.py:299
  506.7 7.6 %multiply_subtract_fusion = f32[1024,1536]{1,0:T(8,128)} fusion(bf16[1024,1536]{1,0:T(8,128)(2,1)} %param.33, bf16[1024,1536]{1,0:T(8,128)(2,1)} %param.17, f32[1024,1536]{1,0:T(8,128)} %get-tuple-element.103, f32[1024]{0:T(1024)S(1)} %get-tuple-element.21, f32[1536]{0:T(1024)S(1)} %copy-done.65, f32[1024]{0:T(1024)S(1)} %copy-done.63), kind=kLoop, calls=%fused_computation.11 | loop fusion | flops 17301504 | bytes 18888704 | tf_op jit(solution)/shard_map/sub | solution.py:286
  514.4 187.3 %all-reduce.39.cloned.1.call-done = (bf16[1536,768]{1,0:T(8,128)(2,1)}, bf16[1536,768]{1,0:T(8,128)(2,1)}, bf16[1536,256]{1,0:T(8,128)(2,1)}, bf16[768,1536]{1,0:T(8,128)(2,1)}) async-done(((bf16[1536,768]{1,0:T(8,128)(2,1)}, bf16[1536,768]{1,0:T(8,128)(2,1)}, bf16[1536,256]{1,0:T(8,128)(2,1)}, bf16[768,1536]{1,0:T(8,128)(2,1)}), (bf16[1536,768]{1,0:T(8,128)(2,1)}, bf16[1536,768]{1,0:T(8,128)(2,1)}, ...) | async-done | bytes 7864336 | tf_op jit(solution)/shard_map/psum | solution.py:296
  (337 shorter events, 154.7 us)
Async XLA Ops:
  7.2 69.4 %copy-start = (bf16[1536,768]{1,0:T(8,128)(2,1)S(1)}, bf16[1536,768]{1,0:T(8,128)(2,1)}, u32[]{:S(2)}) copy-start(bf16[1536,768]{1,0:T(8,128)(2,1)} %param.19) | copy-start | bytes 7077892
  16.1 25.3 %copy-start.74 = (f32[4,12]{1,0:T(4,128)}, f32[4,12]{1,0:T(4,128)S(1)}, u32[]{:S(2)}) copy-start(f32[4,12]{1,0:T(4,128)S(1)} %get-tuple-element.36) | copy-start | bytes 580
  16.1 29.5 %copy-start.66 = (f32[4,12]{1,0:T(4,128)}, f32[4,12]{1,0:T(4,128)S(1)}, u32[]{:S(2)}) copy-start(f32[4,12]{1,0:T(4,128)S(1)} %get-tuple-element.37) | copy-start | bytes 580
  53.1 15.3 %copy-start.13 = (f32[4,12,64,256]{3,2,1,0:T(8,128)}, f32[4,12,64,256]{3,2,1,0:T(8,128)S(1)}, u32[]{:S(2)}) copy-start(f32[4,12,64,256]{3,2,1,0:T(8,128)S(1)} %fusion.86) | copy-start | bytes 9437188
  106.5 10.2 %all-to-all-start.2 = ((f32[4,1,1024]{2,1,0:T(1,128)}), f32[4,1,1024]{2,1,0:T(1,128)S(1)}, u32[]{:S(2)}, u32[]{:S(2)}) async-start(f32[4,1,1024]{2,1,0:T(1,128)} %broadcast_in_dim.74), calls=%async_computation.2 | async-start | bytes 32768 | tf_op jit(solution)/shard_map/all_to_all | solution.py:17
  116.7 119.1 %all-to-all-start.1 = ((bf16[4,256,1536]{2,1,0:T(8,128)(2,1)}), bf16[4,256,1536]{2,1,0:T(8,128)(2,1)}, u32[]{:S(2)}, u32[]{:S(2)}) async-start(bf16[4,256,1536]{2,1,0:T(8,128)(2,1)} %bitcast.407), calls=%async_computation.1 | async-start | bytes 6291456 | tf_op jit(solution)/shard_map/all_to_all | solution.py:33
  121.5 213.6 %all-reduce.37.cloned.1.call-start = ((), (), s32[]{:S(2)}) async-start(), calls=%async_computation.7 | async-start | bytes 6291456 | tf_op jit(solution)/shard_map/psum | solution.py:280
  150.9 23.4 %copy-start.19 = (f32[1,1,12,64,128]{4,3,2,1,0:T(8,128)}, f32[1,1,12,64,128]{4,3,2,1,0:T(8,128)S(1)}, u32[]{:S(2)}) copy-start(f32[1,1,12,64,128]{4,3,2,1,0:T(8,128)S(1)} %get-tuple-element.62) | copy-start | bytes 1179652
  150.9 23.3 %copy-start.20 = (f32[1,1,12,64,128]{4,3,2,1,0:T(8,128)}, f32[1,1,12,64,128]{4,3,2,1,0:T(8,128)S(1)}, u32[]{:S(2)}) copy-start(f32[1,1,12,64,128]{4,3,2,1,0:T(8,128)S(1)} %get-tuple-element.63) | copy-start | bytes 1179652
  150.9 23.3 %copy-start.21 = (f32[1,1,12,64,128]{4,3,2,1,0:T(8,128)}, f32[1,1,12,64,128]{4,3,2,1,0:T(8,128)S(1)}, u32[]{:S(2)}) copy-start(f32[1,1,12,64,128]{4,3,2,1,0:T(8,128)S(1)} %get-tuple-element.76) | copy-start | bytes 1179652
  153.0 21.2 %copy-start.10 = (f32[1,1024,128]{2,1,0:T(8,128)S(1)}, f32[1,1024,128]{2,1,0:T(8,128)}, u32[]{:S(2)}) copy-start(f32[1,1024,128]{2,1,0:T(8,128)} %copy-done.9) | copy-start | bytes 1572868
  201.5 12.2 %copy-start.75 = (f32[4,12]{1,0:T(4,128)S(1)}, f32[4,12]{1,0:T(4,128)}, u32[]{:S(2)}) copy-start(f32[4,12]{1,0:T(4,128)} %copy-done.74) | copy-start | bytes 580
  201.5 12.2 %copy-start.94 = (f32[12]{0:T(128)S(1)}, f32[12]{0:T(128)}, u32[]{:S(2)}) copy-start(f32[12]{0:T(128)} %get-tuple-element.29) | copy-start | bytes 148
  201.5 16.1 %copy-start.51 = (f32[768]{0:T(1024)S(1)}, f32[768]{0:T(1024)}, u32[]{:S(2)}) copy-start(f32[768]{0:T(1024)} %copy-done.50) | copy-start | bytes 9220
  201.5 16.1 %copy-start.53 = (f32[768]{0:T(1024)S(1)}, f32[768]{0:T(1024)}, u32[]{:S(2)}) copy-start(f32[768]{0:T(1024)} %copy-done.52) | copy-start | bytes 9220
  201.5 16.1 %copy-start.55 = (f32[768]{0:T(1024)S(1)}, f32[768]{0:T(1024)}, u32[]{:S(2)}) copy-start(f32[768]{0:T(1024)} %copy-done.54) | copy-start | bytes 9220
  230.3 284.1 %all-gather.2.cloned.1.call-start = ((), (), s32[]{:S(2)}) async-start(), calls=%async_computation.6 | async-start | bytes 3932160 | tf_op jit(solution)/shard_map/all_gather | solution.py:242
  264.6 45.0 %all-to-all-start.3 = ((bf16[4,1024,256]{2,1,0:T(8,128)(2,1)}), bf16[4,1024,256]{2,1,0:T(8,128)(2,1)}, u32[]{:S(2)}, u32[]{:S(2)}) async-start(bf16[4,1024,256]{2,1,0:T(8,128)(2,1)} %broadcast_in_dim.146), calls=%async_computation.3 | async-start | bytes 4194304 | tf_op jit(solution)/shard_map/all_to_all | solution.py:17
  269.3 432.5 %all-reduce.39.cloned.1.call-start = ((), (), s32[]{:S(2)}) async-start(), calls=%async_computation.8 | async-start | bytes 15728640 | tf_op jit(solution)/shard_map/psum | solution.py:296
  315.7 14.1 %copy-start.67 = (f32[768]{0:T(1024)S(1)}, f32[768]{0:T(1024)}, u32[]{:S(2)}) copy-start(f32[768]{0:T(1024)} %get-tuple-element.56) | copy-start | bytes 9220
  315.7 19.4 %copy-start.63 = (f32[1024]{0:T(1024)S(1)}, f32[1024]{0:T(1024)}, u32[]{:S(2)}) copy-start(f32[1024]{0:T(1024)} %copy-done.62) | copy-start | bytes 12292
  315.7 19.4 %copy-start.65 = (f32[1536]{0:T(1024)S(1)}, f32[1536]{0:T(1024)}, u32[]{:S(2)}) copy-start(f32[1536]{0:T(1024)} %param.30) | copy-start | bytes 18436
  317.5 8.4 %all-to-all-start.5 = ((bf16[4,2,128]{2,1,0:T(2,128)(2,1)}), bf16[4,2,128]{2,1,0:T(2,128)(2,1)S(1)}, u32[]{:S(2)}, u32[]{:S(2)}) async-start(bf16[4,2,128]{2,1,0:T(2,128)(2,1)} %reshape.763), calls=%async_computation.5 | async-start | bytes 4096 | tf_op jit(solution)/shard_map/all_to_all | solution.py:17
  326.5 8.5 %all-to-all-start.4 = ((bf16[4,4,256]{2,1,0:T(4,128)(2,1)}), bf16[4,4,256]{2,1,0:T(4,128)(2,1)S(1)}, u32[]{:S(2)}, u32[]{:S(2)}) async-start(bf16[4,4,256]{2,1,0:T(4,128)(2,1)} %broadcast_in_dim.155), calls=%async_computation.4 | async-start | bytes 16384 | tf_op jit(solution)/shard_map/all_to_all | solution.py:17
  (87 other events, 406.6 us)
Sparse Core Ops, SparseCore 0:
  230.4 91.5 all-reduce.36
  323.7 32.3 all-gather.1
  360.0 341.6 all-reduce.38
where the time goes:
time: 726 us; the launch traced here: 721 us
  waiting for transfers between devices  220 us (30%)
  blocking collectives  169 us (23%)
  matrix products  153 us (21%)
  other arithmetic  86.6 us (12%)
  local copies, waits for them, and re-layouts  54.2 us (7%)
  starting transfers between devices  19.2 us (3%)
  between operations  18.9 us (3%)
    psum x1, waiting for transfers between devices, local(): lax.psum(grad_gate_proj.astype(jnp.bfloat16), 'dp').astype(jnp.float32)  187 us
    psum x1, blocking collectives, local(): lax.psum(grad_step_proj.astype(jnp.bfloat16), 'dp').astype(jnp.float32)  160 us
    dot_general x3, matrix products, state_space(): jnp.einsum('khts,kshp->kthp', weights, blocked, precision=HIGH_ACCURACY)  48.4 us
    all_to_all x4, waiting for transfers between devices, sent_to_all(): return lax.all_to_all(copies, axis, split_axis=0, concat_axis=0, tiled=True)  32.7 us
    dot_general x3, matrix products, state_space(): jnp.einsum('ktn,khpn,kht->kthp', out_blocks, before, growth, precision=HI...  15.9 us
  transfers between devices with their start and end apart: 8, of which 4 were waited for; matrix products, arithmetic and copies ran while one was open for 27% of the time, Pallas kernels for 0%

commit v1 on v0

--- a/solution.py
+++ b/solution.py
@@ -1,6 +1,10 @@
+import functools
+
 import jax
 import jax.numpy as jnp
 from jax import lax
+from jax.experimental import pallas as pl
+from jax.experimental.pallas import tpu as pltpu
 from jax.sharding import PartitionSpec as P
 
 H = 48
@@ -10,6 +14,201 @@
 
 EPS = 1e-05
 HIGH_ACCURACY = lax.Precision.HIGHEST
+
+
+MESH_ID = pl.DeviceIdType.MESH
+
+
+def place():
+    dp = lax.axis_index("dp")
+    tensor = lax.axis_index("tensor")
+    return {"x": dp // 8, "y": (dp // 4) % 2, "z": dp % 4, "t": tensor}
+
+
+def device_at(at, **moved):
+    spot = dict(at, **moved)
+    return (spot["x"] * 8 + spot["y"] * 4 + spot["z"], spot["t"])
+
+
+def greet(peers):
+    barrier = pltpu.get_barrier_semaphore()
+    for peer in peers:
+        pl.semaphore_signal(barrier, inc=1, device_id=peer, device_id_type=MESH_ID)
+    pl.semaphore_wait(barrier, len(peers))
+
+
+def dp_peers(at):
+    return [
+        device_at(at, x=(at["x"] + 1) % 4),
+        device_at(at, x=(at["x"] + 3) % 4),
+        device_at(at, z=(at["z"] + 1) % 4),
+        device_at(at, z=(at["z"] + 3) % 4),
+        device_at(at, y=1 - at["y"]),
+    ]
+
+
+def tensor_peers(at):
+    return [device_at(at, t=(at["t"] + step) % 4) for step in (1, 2, 3)]
+
+
+def added(*refs):
+    total = refs[0][...].astype(jnp.float32)
+    for ref in refs[1:]:
+        total = total + ref[...].astype(jnp.float32)
+    return total.astype(jnp.bfloat16)
+
+
+class SumOverDp:
+    def __init__(self, at, buf, res, tmps, send, recv, first, order, tensor_rows=None, tensor_tmp=None):
+        self.at, self.buf, self.res, self.tmps = at, buf, res, tmps
+        self.send, self.recv, self.next = send, recv, first
+        self.a_axis, self.b_axis = order
+        self.tensor_rows, self.tensor_tmp = tensor_rows, tensor_tmp
+        self.stage = 0
+        self.flying = []
+
+    def copy(self, src, dst, peer):
+        cp = pltpu.make_async_remote_copy(
+            src_ref=src,
+            dst_ref=dst,
+            send_sem=self.send.at[self.next],
+            recv_sem=self.recv.at[self.next],
+            device_id=peer,
+            device_id_type=MESH_ID,
+        )
+        self.next += 1
+        cp.start()
+        self.flying.append(cp)
+
+    def start(self):
+        at, buf, res = self.at, self.buf, self.res
+        a, b, y = at[self.a_axis], at[self.b_axis], at["y"]
+        a_up, a_down, a_far = (a + 1) % 4, (a + 3) % 4, (a + 2) % 4
+        b_up, b_down, b_far = (b + 1) % 4, (b + 3) % 4, (b + 2) % 4
+        a_right, a_left = device_at(at, **{self.a_axis: a_up}), device_at(at, **{self.a_axis: a_down})
+        b_right, b_left = device_at(at, **{self.b_axis: b_up}), device_at(at, **{self.b_axis: b_down})
+        other = device_at(at, y=1 - y)
+        ta1, ta2, tb1, tb2, ty = self.tmps
+        low, high = pl.ds(0, 2), pl.ds(2, 2)
+        if self.stage == 0:
+            self.copy(buf.at[a_far, low], ta1.at[0], a_right)
+            self.copy(buf.at[a_far, high], ta1.at[1], a_left)
+        elif self.stage == 1:
+            self.copy(buf.at[a_up], ta2.at[0], a_right)
+            self.copy(buf.at[a_down], ta2.at[1], a_left)
+        elif self.stage == 2:
+            self.copy(buf.at[a, b_far, 0], tb1.at[0], b_right)
+            self.copy(buf.at[a, b_far, 1], tb1.at[1], b_left)
+        elif self.stage == 3:
+            self.copy(buf.at[a, b_up], tb2.at[0], b_right)
+            self.copy(buf.at[a, b_down], tb2.at[1], b_left)
+        elif self.stage == 4:
+            self.copy(buf.at[a, b, 1 - y], ty, other)
+        elif self.stage == 5:
+            if self.tensor_rows is not None:
+                for peer in tensor_peers(at):
+                    self.copy(res.at[a, b, y, self.tensor_rows], self.tensor_tmp.at[at["t"]], peer)
+        elif self.stage == 6:
+            self.copy(res.at[a, b, y], res.at[a, b, y], other)
+        elif self.stage == 7:
+            self.copy(res.at[a, b], res.at[a, b], b_right)
+            self.copy(res.at[a, b], res.at[a, b], b_left)
+        elif self.stage == 8:
+            self.copy(res.at[a, b_down, 0], res.at[a, b_down, 0], b_right)
+            self.copy(res.at[a, b_up, 1], res.at[a, b_up, 1], b_left)
+        elif self.stage == 9:
+            self.copy(res.at[a], res.at[a], a_right)
+            self.copy(res.at[a], res.at[a], a_left)
+        elif self.stage == 10:
+            self.copy(res.at[a_down, low], res.at[a_down, low], a_right)
+            self.copy(res.at[a_up, high], res.at[a_up, high], a_left)
+
+    def finish(self):
+        for cp in self.flying:
+            cp.wait()
+        self.flying = []
+        at, buf, res = self.at, self.buf, self.res
+        a, b, y = at[self.a_axis], at[self.b_axis], at["y"]
+        a_up, a_down = (a + 1) % 4, (a + 3) % 4
+        b_up, b_down = (b + 1) % 4, (b + 3) % 4
+        ta1, ta2, tb1, tb2, ty = self.tmps
+        if self.stage == 0:
+            for j in range(2):
+                for k in range(2):
+                    buf[a_up, j, k] = added(buf.at[a_up, j, k], ta1.at[0, j, k])
+                    buf[a_down, 2 + j, k] = added(buf.at[a_down, 2 + j, k], ta1.at[1, j, k])
+        elif self.stage == 1:
+            for j in range(4):
+                for k in range(2):
+                    buf[a, j, k] = added(buf.at[a, j, k], ta2.at[0, j, k], ta2.at[1, j, k])
+        elif self.stage == 2:
+            buf[a, b_up, 0] = added(buf.at[a, b_up, 0], tb1.at[0])
+            buf[a, b_down, 1] = added(buf.at[a, b_down, 1], tb1.at[1])
+        elif self.stage == 3:
+            for k in range(2):
+                buf[a, b, k] = added(buf.at[a, b, k], tb2.at[0, k], tb2.at[1, k])
+        elif self.stage == 4:
+            res[a, b, y] = added(buf.at[a, b, y], ty)
+        elif self.stage == 5 and self.tensor_rows is not None:
+            self.tensor_tmp[at["t"]] = res[a, b, y, self.tensor_rows]
+            res[a, b, y, self.tensor_rows] = added(*(self.tensor_tmp.at[k] for k in range(4)))
+        self.stage += 1
+
+
+STAGES = 11
+
+
+def dp_tmps(rows, width):
+    block = (rows, width)
+    return [
+        pltpu.VMEM((2, 2, 2) + block, jnp.bfloat16),
+        pltpu.VMEM((2, 4, 2) + block, jnp.bfloat16),
+        pltpu.VMEM((2,) + block, jnp.bfloat16),
+        pltpu.VMEM((2, 2) + block, jnp.bfloat16),
+        pltpu.VMEM(block, jnp.bfloat16),
+    ]
+
+
+def sum_kernel(rows, kept, width, tensor_rows, big_in, small_in, big_out, small_out, buf, small, res, small_res, sa1, sa2, sb1, sb2, sy, ta1, ta2, tb1, tb2, ty, ua1, ua2, ub1, ub2, uy, tt0, tt1, tts, send, recv, local):
+    at = place()
+    greet(dp_peers(at) + tensor_peers(at))
+    loads = [pltpu.make_async_copy(big_in, buf, local.at[0]), pltpu.make_async_copy(small_in, small, local.at[1])]
+    for cp in loads:
+        cp.start()
+    for cp in loads:
+        cp.wait()
+    engines = [
+        SumOverDp(at, buf.at[0], res.at[0], (ta1, ta2, tb1, tb2, ty), send, recv, 0, ("x", "z"), pl.ds(kept, rows - kept), tt0),
+        SumOverDp(at, buf.at[1], res.at[1], (ua1, ua2, ub1, ub2, uy), send, recv, 32, ("z", "x"), pl.ds(kept, rows - kept), tt1),
+        SumOverDp(at, small, small_res, (sa1, sa2, sb1, sb2, sy), send, recv, 64, ("x", "z"), pl.ds(tensor_rows, 16), tts),
+    ]
+    for _ in range(STAGES):
+        for engine in engines:
+            engine.start()
+        for engine in engines:
+            engine.finish()
+    stores = [pltpu.make_async_copy(res, big_out, local.at[0]), pltpu.make_async_copy(small_res, small_out, local.at[1])]
+    for cp in stores:
+        cp.start()
+    for cp in stores:
+        cp.wait()
+
+
+def summed_over_dp(big, small, kept):
+    rows, width = big.shape[4:]
+    return pl.pallas_call(
+        functools.partial(sum_kernel, rows, kept, width, 16),
+        out_shape=(jax.ShapeDtypeStruct(big.shape, big.dtype), jax.ShapeDtypeStruct(small.shape, small.dtype)),
+        in_specs=[pl.BlockSpec(memory_space=pl.ANY)] * 2,
+        out_specs=[pl.BlockSpec(memory_space=pl.ANY)] * 2,
+        scratch_shapes=[pltpu.VMEM(big.shape, big.dtype), pltpu.VMEM(small.shape, small.dtype)] * 2
+        + dp_tmps(32, 128) + dp_tmps(rows, width) + dp_tmps(rows, width)
+        + [pltpu.VMEM((4, rows - kept, width), jnp.bfloat16)] * 2
+        + [pltpu.VMEM((4, 16, 128), jnp.bfloat16)]
+        + [pltpu.SemaphoreType.DMA((96,)), pltpu.SemaphoreType.DMA((96,)), pltpu.SemaphoreType.DMA((2,))],
+        compiler_params=pltpu.CompilerParams(collective_id=0, has_side_effects=True, vmem_limit_bytes=48 * 2**20),
+        name="sum_over_dp",
+    )(big, small)
 
 
 def sent_to_all(shard, axis):
@@ -230,7 +429,10 @@
     mixed_y = mixed_y.reshape(row_count, -1)
     gate_act = jax.nn.silu(gate_raw)
     gated = mixed_y * gate_act
-    squares = over_copies(jnp.sum(gated * gated, -1), "tensor")
+    grad_gate_normed = jnp.dot(cotangent, out_proj.T, preferred_element_type=jnp.float32)
+    scaled = grad_gate_normed * gated_norm_gain
+    sums = over_copies(jnp.stack([jnp.sum(gated * gated, -1), jnp.sum(scaled * gated, -1)]), "tensor")
+    squares, cross = sums[0], sums[1]
     gate_scale = lax.rsqrt(squares[:, None] / inner_width + EPS)
     gate_normed = (gated * gate_scale * gated_norm_gain).astype(jnp.bfloat16)
     branch_part = jnp.dot(gate_normed, out_proj, preferred_element_type=jnp.float32)
@@ -244,10 +446,7 @@
     )
     upstream = cotangent.astype(jnp.float32)
     grad_out_proj = jnp.dot(gate_normed.T, cotangent, preferred_element_type=jnp.float32)
-    grad_gate_normed = jnp.dot(cotangent, out_proj.T, preferred_element_type=jnp.float32)
     grad_mixer_gain = jnp.sum(grad_gate_normed * gated * gate_scale, 0)
-    scaled = grad_gate_normed * gated_norm_gain
-    cross = over_copies(jnp.sum(scaled * gated, -1), "tensor")
     grad_gated = (
         gate_scale * scaled
         - gated * gate_scale * gate_scale * gate_scale * cross[:, None] / inner_width
@@ -259,13 +458,7 @@
     grad_value_raw, grad_state_part, grad_step_raw = (pulled[0], pulled[1], pulled[2])
     grad_value_conv, grad_value_conv_bias = (pulled[3], pulled[4])
     grad_step_bias, grad_log_rate, gradient_bypass_gain = (pulled[7], pulled[8], pulled[9])
-    grad_state_raw, grad_state_conv, grad_state_conv_bias = (
-        taken_together(
-            grad_state_part.reshape(row_count, -1).astype(jnp.bfloat16), "tensor"
-        ).astype(jnp.float32),
-        taken_together(pulled[5].astype(jnp.bfloat16), "tensor").astype(jnp.float32),
-        taken_together(pulled[6].astype(jnp.bfloat16), "tensor").astype(jnp.float32),
-    )
+    grad_state_raw, grad_state_conv, grad_state_conv_bias = grad_state_part.reshape(row_count, -1), pulled[5], pulled[6]
     gate_low = grad_gate_raw.astype(jnp.bfloat16)
     value_low = grad_value_raw.reshape(row_count, -1).astype(jnp.bfloat16)
     state_low = grad_state_raw.astype(jnp.bfloat16)
@@ -277,10 +470,9 @@
     normed_part = jnp.dot(gate_low, gate_proj.T, preferred_element_type=jnp.float32)
     normed_part = normed_part + jnp.dot(value_low, value_proj.T, preferred_element_type=jnp.float32)
     normed_part = normed_part + jnp.dot(step_low, step_proj.T, preferred_element_type=jnp.float32)
-    grad_normed = lax.psum(normed_part.astype(jnp.bfloat16), "tensor").astype(
-        jnp.float32
-    ) + jnp.dot(state_low, state_proj.T, preferred_element_type=jnp.float32)
-    grad_norm_gain = jnp.sum(grad_normed * hidden * inverse, 0)
+    normed_part = normed_part + jnp.dot(state_low, state_proj.T, preferred_element_type=jnp.float32)
+    grad_norm_gain = jnp.sum(normed_part * hidden * inverse, 0)
+    grad_normed = lax.psum(normed_part.astype(jnp.bfloat16), "tensor").astype(jnp.float32)
     scaled_in = grad_normed * norm_gain
     grad_tokens = (
         upstream
@@ -292,40 +484,53 @@
         * jnp.sum(scaled_in * hidden, -1, keepdims=True)
         / model_width
     )
-    summed = (
-        lax.psum(grad_gate_proj.astype(jnp.bfloat16), "dp").astype(jnp.float32),
-        lax.psum(grad_value_proj.astype(jnp.bfloat16), "dp").astype(jnp.float32),
-        lax.psum(grad_state_proj.astype(jnp.bfloat16), "dp").astype(jnp.float32),
-        lax.psum(grad_step_proj.astype(jnp.bfloat16), "dp").astype(jnp.float32),
-        lax.psum(grad_value_conv.astype(jnp.bfloat16), "dp").astype(jnp.float32),
-        lax.psum(grad_value_conv_bias.astype(jnp.bfloat16), "dp").astype(jnp.float32),
-        lax.psum(grad_state_conv.astype(jnp.bfloat16), "dp").astype(jnp.float32),
-        lax.psum(grad_state_conv_bias.astype(jnp.bfloat16), "dp").astype(jnp.float32),
-        lax.psum(grad_step_bias.astype(jnp.bfloat16), "dp").astype(jnp.float32),
-        lax.psum(grad_log_rate.astype(jnp.bfloat16), "dp").astype(jnp.float32),
-        lax.psum(gradient_bypass_gain.astype(jnp.bfloat16), "dp").astype(jnp.float32),
-        lax.psum(grad_norm_gain.astype(jnp.bfloat16), "dp").astype(jnp.float32),
-        lax.psum(grad_mixer_gain.astype(jnp.bfloat16), "dp").astype(jnp.float32),
-        lax.psum(grad_out_proj.astype(jnp.bfloat16), "dp").astype(jnp.float32),
-    )
+    big = jnp.concatenate(
+        [
+            piece.astype(jnp.bfloat16).reshape(32, -1, 2, 384)
+            for piece in (grad_gate_proj, grad_value_proj, grad_out_proj, grad_state_proj)
+        ],
+        axis=1,
+    )
+    big = jnp.transpose(big, (2, 0, 1, 3)).reshape(2, 4, 4, 2, 160, 384)
+    own = (grad_step_proj, grad_value_conv, grad_value_conv_bias, grad_step_bias, grad_log_rate, gradient_bypass_gain, grad_mixer_gain)
+    shared_by_all = (grad_state_conv, grad_state_conv_bias, grad_norm_gain)
+    small = jnp.concatenate([packed(own), packed(shared_by_all)], axis=1).reshape(4, 4, 2, 32, 128)
+    big, small = summed_over_dp(big, small, 144)
+    big = jnp.transpose(big.reshape(2, 32, 160, 384), (1, 2, 0, 3)).astype(jnp.float32)
+    small = small.reshape(32, 32, 128).astype(jnp.float32)
+    sum_own = unpacked(small[:, :16], own)
+    sum_shared = unpacked(small[:, 16:], shared_by_all)
     return (
         mixed_out,
         grad_tokens,
-        summed[0],
-        summed[1],
-        summed[2],
-        summed[3],
-        summed[4],
-        summed[5],
-        summed[6],
-        summed[7],
-        summed[8],
-        summed[9],
-        summed[10],
-        summed[11],
-        summed[12],
-        summed[13],
-    )
+        big[:, :48].reshape(grad_gate_proj.shape),
+        big[:, 48:96].reshape(grad_value_proj.shape),
+        big[:, 144:].reshape(grad_state_proj.shape),
+        sum_own[0],
+        sum_own[1],
+        sum_own[2],
+        sum_shared[0],
+        sum_shared[1],
+        sum_own[3],
+        sum_own[4],
+        sum_own[5],
+        sum_shared[2],
+        sum_own[6],
+        big[:, 96:144].reshape(grad_out_proj.shape),
+    )
+
+
+def packed(pieces):
+    flat = jnp.concatenate([piece.reshape(-1).astype(jnp.bfloat16) for piece in pieces])
+    return jnp.pad(flat, (0, 65536 - flat.shape[0])).reshape(32, 16, 128)
+
+
+def unpacked(rows, like):
+    flat, at, pieces = rows.reshape(-1), 0, []
+    for piece in like:
+        pieces.append(flat[at : at + piece.size].reshape(piece.shape))
+        at += piece.size
+    return pieces
 
 
 def solution(mesh):

time: 726 us -> 589 us (0.81)
  waiting for transfers between devices: 220 us -> 47.4 us
  blocking collectives: 169 us -> 0 us
  Pallas kernels: 0 us -> 125 us
  local copies, waits for them, and re-layouts: 54.2 us -> 136 us
  starting transfers between devices: 19.2 us -> 9.84 us
    psum x1 -> x0, waiting for transfers between devices: 187 us -> none  [local(): lax.psum(grad_gate_proj.astype(jnp.bfloat16), 'dp').astype(jnp.float32)]
    psum x1 -> x0, blocking collectives: 160 us -> none  [local(): lax.psum(grad_step_proj.astype(jnp.bfloat16), 'dp').astype(jnp.float32)]
    pallas_call x0 -> x1, Pallas kernels: none -> 125 us  [summed_over_dp(): pl.pallas_call(functools.partial(sum_kernel, rows, kept, width, 16), out_...]
    psum x1, waiting for transfers between devices: 0.02 us -> 47.3 us  [local(): lax.psum(normed_part.astype(jnp.bfloat16), 'tensor').astype(jnp.float32)]
    slice x0 -> x16, local copies, waits for them, and re-layouts: none -> 33.9 us  [the longest x2 18.8 us: local(): big[:, 96:144].reshape(grad_out_proj.shape)]
    all_to_all x4 -> x1, waiting for transfers between devices: 32.7 us -> 0.09 us  [sent_to_all(): return lax.all_to_all(copies, axis, split_axis=0, concat_axis=0, tiled=True)]
    reshape x0 -> x12, local copies, waits for them, and re-layouts: none -> 32.2 us  [the longest x8 20.2 us: local(): piece.astype(jnp.bfloat16).reshape(32, -1, 2, 384)]
    unnamed x215 -> x219, local copies, waits for them, and re-layouts: 11.9 us -> 24.7 us
  transfers between devices with their start and end apart: 8 -> 4, of which waited for: 4 -> 2; matrix products, arithmetic and copies ran while one was open for 27% -> 31% of each run, Pallas kernels for 0% -> 22%
where the time goes in v1:
time: 589 us; the launch traced here: 579 us
  matrix products  153 us (26%)
  local copies, waits for them, and re-layouts  136 us (23%)
  Pallas kernels  125 us (21%)
  other arithmetic  90.2 us (15%)
  waiting for transfers between devices  47.4 us (8%)
  between operations  18.4 us (3%)
  starting transfers between devices  9.84 us (2%)
    pallas_call x1, Pallas kernels, summed_over_dp(): pl.pallas_call(functools.partial(sum_kernel, rows, kept, width, 16), out_...  125 us
    dot_general x3, matrix products, state_space(): jnp.einsum('khts,kshp->kthp', weights, blocked, precision=HIGH_ACCURACY)  50.5 us
    psum x1, waiting for transfers between devices, local(): lax.psum(normed_part.astype(jnp.bfloat16), 'tensor').astype(jnp.float32)  47.3 us
    unnamed x219, local copies, waits for them, and re-layouts  24.7 us
    reshape x8, local copies, waits for them, and re-layouts, local(): piece.astype(jnp.bfloat16).reshape(32, -1, 2, 384)  20.2 us
    slice x2, local copies, waits for them, and re-layouts, local(): big[:, 96:144].reshape(grad_out_proj.shape)  18.8 us
    reduce_sum x2, other arithmetic, causal_conv(): summed = summed + kernel[lag_count] * shifted * keeper  13.7 us
    dot_general x3, matrix products, state_space(): jnp.einsum('khs,kshp,ksn->khpn', tail_weight, blocked, in_blocks, precisi...  13.1 us
  transfers between devices with their start and end apart: 4, of which 2 were waited for; matrix products, arithmetic and copies ran while one was open for 31% of the time, Pallas kernels for 22%

profile of v1, /device:TPU:0, one launch (start us, length us, event | category | flops | bytes accessed | tf_op | source)
XLA Modules:
  0.0 579.0 jit_solution(2024927774846937944)
XLA Ops:
  50.5 5.3 reshape.767
  58.8 5.5 fusion.66
  67.6 15.3 %bitcast_add_fusion.1 = f32[1,4,256,12,64]{2,4,3,1,0:T(8,128)S(1)} fusion(f32[4,12,64,256]{3,2,1,0:T(8,128)S(1)} %fusion.86, f32[4,12,256]{2,1,0:T(8,128)S(1)} %bitcast.481, f32[4,12,256]{2,1,0:T(8,128)S(1)} %fusion.110, f32[4,256,256]{2,1,0:T(8,128)S(1)} %fusion.179, pred[4,256,256]{2,1,0:T(8,128)(4,1)S(1)} %copy-done.47, ...), kind=kOutput, calls=%fused_computation.51 | convolution fusion | flops 2430074880 | bytes 10895360 | tf_op jit(solution)/shard_map/jvp(vmap(khts,kshp->kthp))/dot_general | solution.py:271
  91.0 10.0 %multiply_reduce_fusion.12 = (f32[1024]{0:T(1024)S(1)}, f32[1024]{0:T(1024)S(1)}, f32[1024,768]{1,0:T(8,128)}, f32[1024,768]{1,0:T(8,128)}) fusion(f32[768]{0:T(1024)} %param.31, f32[1024,768]{1,0:T(8,128)} %fusion.180, f32[1024,768]{1,0:T(8,128)} %copy.155, f32[1,1024,768]{2,1,0:T(8,128)} %get-tuple-element.122, f32[768]{0:T(1024)S(1)} %mul.789, ...), kind=kOutput, calls=%fused_computation.78 | convolution fusion | flops 2428499968 | bytes 21248000 | tf_op jit(solution)/shard_map/dot_general | solution.py:432
  106.2 5.5 convert_element_type.152
  113.9 7.2 %convolution_convert_fusion.1 = bf16[768,1536]{1,0:T(8,128)(2,1)} fusion(bf16[1024,1536]{1,0:T(8,128)(2,1)} %param.33, f32[1024,768]{1,0:T(8,128)} %get-tuple-element.118, f32[1024]{0:T(1024)S(1)} %bitcast.486, f32[768]{0:T(1024)} %param.31), kind=kOutput, calls=%fused_computation.35 | convolution fusion | flops 2419458048 | bytes 8657920 | tf_op jit(solution)/shard_map/dot_general | solution.py:448
  126.9 5.9 %fusion.31 = (f32[768]{0:T(1024)}, f32[1024,768]{1,0:T(8,128)}, bf16[1024,768]{1,0:T(8,128)(2,1)}, bf16[768]{0:T(1024)(128)(2,1)}) fusion(f32[1,1024,768]{2,1,0:T(8,128)S(1)} %copy-done.9, f32[1024,768]{1,0:T(8,128)S(1)} %copy-done.24, f32[1024]{0:T(1024)S(1)} %bitcast.485, f32[1024,768]{1,0:T(8,128)S(1)} %copy-done.25, f32[1024,768]{1,0:T(8,128)S(1)} %copy-done.26, ...), kind=kLoop, calls=%fused_computation.61 | loop fusion | flops 24377856 | bytes 20466176 | tf_op jit(solution)/shard_map/transpose(jvp(vmap()))/reduce_sum | solution.py:327
  136.4 5.3 reshape.779
  145.8 6.0 %fusion.82 = f32[4,256,128]{2,1,0:T(8,128)} fusion(f32[4,256,12,64]{1,0,3,2:T(4,128)S(1)} %copy-done.10, f32[4,256,12]{1,2,0:T(8,128)S(1)} %copy-done.50, f32[1,1,12,64,128]{4,3,2,1,0:T(8,128)S(1)} %copy-done.35, f32[1,1,12,64,128]{4,3,2,1,0:T(8,128)S(1)} %copy-done.37, f32[1,1,12,64,128]{4,3,2,1,0:T(8,128)S(1)} %copy-done.39, ...), kind=kOutput, calls=%fused_computation.121 | convolution fusion | flops 1209925632 | bytes 5292032 | tf_op jit(solution)/shard_map/transpose(jvp(vmap(ktn,khpn,kht->kthp)))/dot_general | solution.py:294
  161.8 22.9 %fusion.7 = (f32[4,12,256]{2,1,0:T(8,128)}, f32[4,12,256]{2,1,0:T(8,128)}, f32[4,12,256]{2,1,0:T(8,128)}, f32[4,256,256]{2,1,0:T(8,128)S(1)}) fusion(f32[4,12,256]{2,1,0:T(8,128)S(1)} %bitcast.482, f32[4,12,256]{2,1,0:T(8,128)S(1)} %fusion.110, f32[4,256,256]{2,1,0:T(8,128)} %copy-done.41, pred[4,256,256]{2,1,0:T(8,128)(4,1)} %compare_and_fusion, ...), kind=kOutput, calls=%fused_computation.11 | convolution fusion | flops 2456514560 | bytes 8896512 | tf_op jit(solution)/shard_map/transpose(jvp(vmap(khts,kshp->kthp)))/dot_general | solution.py:271
  190.0 12.3 %bitcast_add_fusion = f32[1,4,256,12,64]{2,4,3,1,0:T(8,128)} fusion(f32[4,256,12,64]{1,3,2,0:T(8,128)S(1)} %convolution_bitcast_fusion, f32[4,12,256]{2,1,0:T(8,128)S(1)} %bitcast.483, f32[4,12,256]{2,1,0:T(8,128)S(1)} %fusion.110, f32[4,256,256]{2,1,0:T(8,128)S(1)} %copy-done.42, pred[4,256,256]{2,1,0:T(8,128)(4,1)S(1)} %copy-done.48, ...), kind=kOutput, calls=%fused_computation.50 | convolution fusion | flops 2430074880 | bytes 10895360 | tf_op jit(solution)/shard_map/transpose(jvp(vmap(khts,kshp->kthp)))/dot_general | solution.py:271
  236.5 11.4 %multiply_reduce_fusion.10 = (f32[768]{0:T(1024)}, f32[768]{0:T(1024)}, f32[768]{0:T(1024)}, bf16[768]{0:T(1024)(128)(2,1)}, f32[768]{0:T(1024)}, /*index=5*/f32[1,1024,768]{2,1,0:T(8,128)}) fusion(f32[1,1024,768]{2,1,0:T(8,128)} %bitcast.422, f32[1024]{0:T(1024)S(1)} %bitcast.476, f32[1024]{0:T(1024)S(1)} %bitcast.470, f32[1024]{0:T(1024)S(1)} %bitcast.464, ...), kind=kLoop, calls=%fused_computation.73 | loop fusion | flops 18084096 | bytes 18903552 | tf_op jit(solution)/shard_map/transpose(jvp(vmap()))/reduce_sum | solution.py:247
  258.0 7.6 %fusion.57 = f32[1024,1536]{1,0:T(8,128)} fusion(bf16[1536,768]{1,0:T(8,128)(2,1)} %param.20, bf16[1,1024,768]{2,1,0:T(8,128)(2,1)} %fusion.23), kind=kOutput, calls=%fused_computation.103 | convolution fusion | flops 2415919104 | bytes 10223616 | tf_op jit(solution)/shard_map/dot_general | solution.py:471
  266.8 7.9 %fusion.172 = (bf16[1024,1536]{1,0:T(8,128)(2,1)}, f32[1024,1536]{1,0:T(8,128)}) fusion(bf16[1536,256]{1,0:T(8,128)(2,1)S(1)} %copy-done.43, bf16[1,1024,256]{2,1,0:T(8,128)(2,1)S(1)} %fusion.90, f32[1024,1536]{1,0:T(8,128)S(1)} %fusion.144, f32[1024,1536]{1,0:T(8,128)S(1)} %bitcast.444, f32[1024,1536]{1,0:T(8,128)} %fusion.57), kind=kOutput, calls=%fused_computation.268 | convolution fusion | flops 811597824 | bytes 29622272 | tf_op jit(solution)/shard_map/dot_general | solution.py:473
  295.4 6.0 %convolution_convert_fusion.2 = bf16[1536,768]{1,0:T(8,128)(2,1)} fusion(bf16[1024,1536]{1,0:T(8,128)(2,1)} %copy-done.4, bf16[1,1024,768]{2,1,0:T(8,128)(2,1)S(1)} %copy-done.40), kind=kOutput, calls=%fused_computation.36 | convolution fusion | flops 2417098752 | bytes 7077888 | tf_op jit(solution)/shard_map/dot_general | solution.py:467
  308.0 6.7 %pad_maximum_fusion = bf16[32,160,2,384]{3,1,0,2:T(8,128)(2,1)} fusion(bf16[32,16,2,384]{3,1,0,2:T(8,128)(2,1)S(1)} %copy.174, bf16[32,48,2,384]{3,1,0,2:T(8,128)(2,1)} %copy.173, bf16[32,48,2,384]{3,1,0,2:T(8,128)(2,1)} %copy.172, bf16[32,48,2,384]{3,1,0,2:T(8,128)(2,1)} %copy.171), kind=kLoop, calls=%fused_computation.9 | loop fusion | flops 31457280 | bytes 15728640 | tf_op jit(solution)/shard_map/concatenate | solution.py:487
  319.8 47.3 %all-reduce.36.cloned.1.call-done = bf16[1024,1536]{1,0:T(8,128)(2,1)} async-done(((bf16[1024,1536]{1,0:T(8,128)(2,1)}), bf16[1024,1536]{1,0:T(8,128)(2,1)}) %all-reduce.36.cloned.1.call-update) | async-done | bytes 3145744 | tf_op jit(solution)/shard_map/psum | solution.py:475
  367.1 5.8 %multiply_reduce_fusion.2 = (bf16[1536]{0:T(1024)(128)(2,1)S(1)}, f32[1024]{0:T(1024)S(1)}) fusion(f32[1024,1536]{1,0:T(8,128)} %get-tuple-element.169, bf16[1024,1536]{1,0:T(8,128)(2,1)} %param.17, f32[1024]{0:T(1024)S(1)} %copy-done.61, f32[1536]{0:T(1024)S(1)} %copy-done.54, bf16[1024,1536]{1,0:T(8,128)(2,1)} %all-reduce.36.cloned.1.call-done), kind=kLoop, calls=%fused_computation.12 | loop fusion | flops 12580352 | bytes 12600320 | tf_op jit(solution)/shard_map/reduce_sum | solution.py:474
  372.9 124.7 %sum_over_dp.1 = (bf16[2,4,4,2,160,384]{5,4,3,2,1,0:T(8,128)(2,1)}, bf16[4,4,2,32,128]{4,3,2,1,0:T(8,128)(2,1)S(1)}) custom-call(bf16[2,4,4,2,160,384]{5,4,3,2,1,0:T(8,128)(2,1)} %bitcast.423, bf16[4,4,2,32,128]{4,3,2,1,0:T(8,128)(2,1)S(1)} %pad_maximum_fusion.1.small_in), custom_call_target="tpu_custom_call" | custom-call | tf_op jit(solution)/shard_map/sum_over_dp/pallas_call | solution.py:199
  502.0 10.8 %convert_bitcast_fusion = f32[32,160,2,384]{3,1,0,2:T(8,128)} fusion(bf16[2,32,160,384]{3,2,1,0:T(8,128)(2,1)} %bitcast.442), kind=kLoop, calls=%fused_computation | loop fusion | flops 3932160 | bytes 23592960 | tf_op jit(solution)/shard_map/convert_element_type | solution.py:499
  512.8 10.6 %fusion.164 = (f32[32,48,2,384]{3,1,0,2:T(8,128)}, f32[32,48,2,384]{3,1,0,2:T(8,128)}, f32[32,48,2,384]{3,1,0,2:T(8,128)}) fusion(f32[32,160,2,384]{3,1,0,2:T(8,128)} %convert_bitcast_fusion), kind=kLoop, calls=%fused_computation.260 | loop fusion | bytes 28311552 | tf_op jit(solution)/shard_map/slice | solution.py:519
  523.4 8.2 %copy.179 = f32[32,48,2,384]{3,2,1,0:T(2,128)} copy(f32[32,48,2,384]{3,1,0,2:T(8,128)} %get-tuple-element.125) | data formatting | bytes 9437184 | tf_op jit(solution)/shard_map/slice | solution.py:519
  531.6 7.1 %reshape.802 = f32[768,1536]{1,0:T(8,128)} reshape(f32[32,48,2,384]{3,2,1,0:T(2,128)} %copy.179) | data formatting | bytes 9437184 | tf_op jit(solution)/shard_map/reshape | solution.py:519
  544.5 6.0 %copy.177 = f32[32,48,2,384]{3,2,1,0:T(2,128)S(1)} copy(f32[32,48,2,384]{3,1,0,2:T(8,128)} %get-tuple-element.126) | data formatting | bytes 9437184 | tf_op jit(solution)/shard_map/slice | solution.py:507
  (349 shorter events, 199.2 us)
Async XLA Ops:
  7.2 83.8 %copy-start = (bf16[768,1536]{1,0:T(8,128)(2,1)S(1)}, bf16[768,1536]{1,0:T(8,128)(2,1)}, u32[]{:S(2)}) copy-start(bf16[768,1536]{1,0:T(8,128)(2,1)} %param.32) | copy-start | bytes 7077892
  7.2 11.1 %copy-start.74 = (f32[4,768]{1,0:T(4,128)S(1)}, f32[4,768]{1,0:T(4,128)}, u32[]{:S(2)}) copy-start(f32[4,768]{1,0:T(4,128)} %param.23) | copy-start | bytes 36868
  7.2 11.7 %copy-start.53 = (f32[1536]{0:T(1024)S(1)}, f32[1536]{0:T(1024)}, u32[]{:S(2)}) copy-start(f32[1536]{0:T(1024)} %param.30) | copy-start | bytes 18436
  8.1 17.4 %copy-start.90 = (f32[12]{0:T(128)}, f32[12]{0:T(128)S(1)}, u32[]{:S(2)}) copy-start(f32[12]{0:T(128)S(1)} %exponential_negate_fusion) | copy-start | bytes 148
  67.6 15.4 %copy-start.16 = (f32[4,12,64,256]{3,2,1,0:T(8,128)}, f32[4,12,64,256]{3,2,1,0:T(8,128)S(1)}, u32[]{:S(2)}) copy-start(f32[4,12,64,256]{3,2,1,0:T(8,128)S(1)} %fusion.86) | copy-start | bytes 9437188
  101.6 10.1 %all-to-all-start = ((f32[4,2,1024]{2,1,0:T(2,128)}), f32[4,2,1024]{2,1,0:T(2,128)}, u32[]{:S(2)}, u32[]{:S(2)}) async-start(f32[4,2,1024]{2,1,0:T(2,128)} %broadcast_in_dim.65), calls=%async_computation | async-start | bytes 65536 | tf_op jit(solution)/shard_map/all_to_all | solution.py:216
  161.7 23.0 %copy-start.12 = (f32[1,1024,128]{2,1,0:T(8,128)S(1)}, f32[1,1024,128]{2,1,0:T(8,128)}, u32[]{:S(2)}) copy-start(f32[1,1024,128]{2,1,0:T(8,128)} %get-tuple-element.138) | copy-start | bytes 1572868
  161.7 23.0 %copy-start.21 = (f32[1,1,12,64,128]{4,3,2,1,0:T(8,128)S(1)}, f32[1,1,12,64,128]{4,3,2,1,0:T(8,128)}, u32[]{:S(2)}) copy-start(f32[1,1,12,64,128]{4,3,2,1,0:T(8,128)} %get-tuple-element.116) | copy-start | bytes 1179652
  161.7 23.0 %copy-start.22 = (f32[1,1,12,64,128]{4,3,2,1,0:T(8,128)S(1)}, f32[1,1,12,64,128]{4,3,2,1,0:T(8,128)}, u32[]{:S(2)}) copy-start(f32[1,1,12,64,128]{4,3,2,1,0:T(8,128)} %get-tuple-element.117) | copy-start | bytes 1179652
  161.7 22.9 %copy-start.23 = (f32[1,1,12,64,128]{4,3,2,1,0:T(8,128)S(1)}, f32[1,1,12,64,128]{4,3,2,1,0:T(8,128)}, u32[]{:S(2)}) copy-start(f32[1,1,12,64,128]{4,3,2,1,0:T(8,128)} %get-tuple-element.133) | copy-start | bytes 1179652
  190.0 12.4 %copy-start.6 = (bf16[1024,1536]{1,0:T(8,128)(2,1)S(1)}, bf16[1024,1536]{1,0:T(8,128)(2,1)}, u32[]{:S(2)}) copy-start(bf16[1024,1536]{1,0:T(8,128)(2,1)} %copy-done.4) | copy-start | bytes 9437188
  190.0 12.4 %copy-start.31 = (bf16[1024,768]{1,0:T(8,128)(2,1)S(1)}, bf16[1024,768]{1,0:T(8,128)(2,1)}, u32[]{:S(2)}) copy-start(bf16[1024,768]{1,0:T(8,128)(2,1)} %get-tuple-element.128) | copy-start | bytes 4718596
  211.1 103.6 %all-to-all-start.1 = ((bf16[4,256,1536]{2,1,0:T(8,128)(2,1)}), bf16[4,256,1536]{2,1,0:T(8,128)(2,1)}, u32[]{:S(2)}, u32[]{:S(2)}) async-start(bf16[4,256,1536]{2,1,0:T(8,128)(2,1)} %bitcast.447), calls=%async_computation.1 | async-start | bytes 6291456 | tf_op jit(solution)/shard_map/all_to_all | solution.py:232
  215.9 151.1 %all-reduce.36.cloned.1.call-start = ((), (), s32[]{:S(2)}) async-start(), calls=%async_computation.3 | async-start | bytes 6291456 | tf_op jit(solution)/shard_map/psum | solution.py:475
  236.4 11.4 %copy-start.66 = (f32[4,12]{1,0:T(4,128)S(1)}, f32[4,12]{1,0:T(4,128)}, u32[]{:S(2)}) copy-start(f32[4,12]{1,0:T(4,128)} %get-tuple-element.105) | copy-start | bytes 580
  236.4 11.7 %copy-start.55 = (f32[4,12,256]{2,1,0:T(8,128)S(1)}, f32[4,12,256]{2,1,0:T(8,128)}, u32[]{:S(2)}) copy-start(f32[4,12,256]{2,1,0:T(8,128)} %get-tuple-element.84) | copy-start | bytes 147460
  236.4 11.7 %copy-start.56 = (f32[4,12,256]{2,1,0:T(8,128)S(1)}, f32[4,12,256]{2,1,0:T(8,128)}, u32[]{:S(2)}) copy-start(f32[4,12,256]{2,1,0:T(8,128)} %get-tuple-element.85) | copy-start | bytes 147460
  236.4 11.7 %copy-start.57 = (f32[4,12,256]{2,1,0:T(8,128)S(1)}, f32[4,12,256]{2,1,0:T(8,128)}, u32[]{:S(2)}) copy-start(f32[4,12,256]{2,1,0:T(8,128)} %get-tuple-element.86) | copy-start | bytes 147460
  236.4 11.7 %copy-start.63 = (f32[4,256]{1,0:T(4,128)S(1)}, f32[4,256]{1,0:T(4,128)}, u32[]{:S(2)}) copy-start(f32[4,256]{1,0:T(4,128)} %copy-done.62) | copy-start | bytes 12292
  236.5 11.7 %copy-start.91 = (f32[12]{0:T(128)S(1)}, f32[12]{0:T(128)}, u32[]{:S(2)}) copy-start(f32[12]{0:T(128)} %copy-done.90) | copy-start | bytes 148
  236.5 12.7 %copy-start.20 = (f32[1,1024,256]{2,1,0:T(8,128)S(1)}, f32[1,1024,256]{2,1,0:T(8,128)}, u32[]{:S(2)}) copy-start(f32[1,1024,256]{2,1,0:T(8,128)} %get-tuple-element.124) | copy-start | bytes 3145732
  288.2 279.8 %all-gather.2.cloned.1.call-start = ((), (), s32[]{:S(2)}) async-start(), calls=%async_computation.2 | async-start | bytes 3932160 | tf_op jit(solution)/shard_map/all_gather | solution.py:444
  317.2 49.9 %copy-start.54 = (f32[1536]{0:T(1024)S(1)}, f32[1536]{0:T(1024)}, u32[]{:S(2)}) copy-start(f32[1536]{0:T(1024)} %param.30) | copy-start | bytes 18436
  317.2 49.8 %copy-start.61 = (f32[1024]{0:T(1024)S(1)}, f32[1024]{0:T(1024)}, u32[]{:S(2)}) copy-start(f32[1024]{0:T(1024)} %copy-done.60) | copy-start | bytes 12292
  (85 other events, 339.8 us)
Sparse Core Ops, SparseCore 0:
  288.4 78.6 all-reduce.35
  368.7 31.9 all-gather.1

commit v2 on v0

v2 whole, which is shorter than its diff:
```python
import jax
import jax.numpy as jnp
from jax import lax
from jax.experimental import pallas as pl
from jax.experimental.pallas import tpu as pltpu
from jax.sharding import PartitionSpec as P

EPS = 1e-05
MESH_ID = pl.DeviceIdType.MESH


def place():
    dp = lax.axis_index("dp")
    tensor = lax.axis_index("tensor")
    return {"x": dp // 8, "y": (dp // 4) % 2, "z": dp % 4, "t": tensor}


def device_at(at, **moved):
    spot = dict(at, **moved)
    return (spot["x"] * 8 + spot["y"] * 4 + spot["z"], spot["t"])


def dp_peers(at):
    return [
        device_at(at, x=(at["x"] + 1) % 4),
        device_at(at, x=(at["x"] + 3) % 4),
        device_at(at, z=(at["z"] + 1) % 4),
        device_at(at, z=(at["z"] + 3) % 4),
        device_at(at, y=1 - at["y"]),
    ]


def tensor_peers(at):
    return [device_at(at, t=(at["t"] + step) % 4) for step in (1, 2, 3)]


def greet(peers):
    barrier = pltpu.get_barrier_semaphore()
    for peer in peers:
        pl.semaphore_signal(barrier, inc=1, device_id=peer, device_id_type=MESH_ID)
    pl.semaphore_wait(barrier, len(peers))


def added(*refs):
    total = refs[0][...].astype(jnp.float32)
    for ref in refs[1:]:
        total = total + ref[...].astype(jnp.float32)
    return total.astype(jnp.bfloat16)


class Staged:
    def __init__(self, send, recv, first):
        self.send, self.recv, self.first = send, recv, first

    def made(self, stage):
        at = self.first + sum(self.counts[:stage])
        for n, (src, dst, peer) in enumerate(self.copies(stage)):
            if peer is None:
                yield pltpu.make_async_copy(src, dst, self.recv.at[at + n])
            else:
                yield pltpu.make_async_remote_copy(
                    src_ref=src,
                    dst_ref=dst,
                    send_sem=self.send.at[at + n],
                    recv_sem=self.recv.at[at + n],
                    device_id=peer,
                    device_id_type=MESH_ID,
                )

    def start(self, stage):
        for cp in self.made(stage):
            cp.start()

    def finish(self, stage):
        for cp in self.made(stage):
            cp.wait()
        self.settle(stage)


class SumOverDp(Staged):
    counts = (2, 2, 2, 2, 1, 3, 2, 2, 2, 2, 2)

    def __init__(self, at, order, buf, res, scratch, sems, tensor_from=None):
        super().__init__(*sems)
        self.at, self.buf, self.res, self.tensor_from = at, buf, res, tensor_from
        self.ta1, self.ta2, self.tb1, self.tb2, self.ty, self.own, self.tt = scratch
        a_axis, b_axis = order
        self.a, self.b, self.y = at[a_axis], at[b_axis], at["y"]
        self.a_up, self.a_down, self.a_far = [(self.a + n) % 4 for n in (1, 3, 2)]
        self.b_up, self.b_down, self.b_far = [(self.b + n) % 4 for n in (1, 3, 2)]
        self.a_right, self.a_left = [device_at(at, **{a_axis: n}) for n in (self.a_up, self.a_down)]
        self.b_right, self.b_left = [device_at(at, **{b_axis: n}) for n in (self.b_up, self.b_down)]
        self.other = device_at(at, y=1 - self.y)
        self.peers = tensor_peers(at)

    def copies(self, stage):
        buf, res, a, b, y = self.buf, self.res, self.a, self.b, self.y
        near, far = pl.ds(0, 2), pl.ds(2, 2)
        if stage == 0:
            return [(buf.at[self.a_far, near], self.ta1.at[0], self.a_right), (buf.at[self.a_far, far], self.ta1.at[1], self.a_left)]
        if stage == 1:
            return [(buf.at[self.a_up], self.ta2.at[0], self.a_right), (buf.at[self.a_down], self.ta2.at[1], self.a_left)]
        if stage == 2:
            return [(buf.at[a, self.b_far, 0], self.tb1.at[0], self.b_right), (buf.at[a, self.b_far, 1], self.tb1.at[1], self.b_left)]
        if stage == 3:
            return [(buf.at[a, self.b_up], self.tb2.at[0], self.b_right), (buf.at[a, self.b_down], self.tb2.at[1], self.b_left)]
        if stage == 4:
            return [(buf.at[a, b, 1 - y], self.ty, self.other)]
        if stage == 5:
            if self.tensor_from is None:
                return []
            rows = pl.ds(self.tensor_from, self.own.shape[0] - self.tensor_from)
            return [(self.own.at[rows], self.tt.at[self.at["t"]], peer) for peer in self.peers]
        if stage == 6:
            return [(self.own, res.at[a, b, y], self.other), (self.own, res.at[a, b, y], None)]
        if stage == 7:
            return [(res.at[a, b], res.at[a, b], self.b_right), (res.at[a, b], res.at[a, b], self.b_left)]
        if stage == 8:
            return [
                (res.at[a, self.b_down, 0], res.at[a, self.b_down, 0], self.b_right),
                (res.at[a, self.b_up, 1], res.at[a, self.b_up, 1], self.b_left),
            ]
        if stage == 9:
            return [(res.at[a], res.at[a], self.a_right), (res.at[a], res.at[a], self.a_left)]
        return [
            (res.at[self.a_down, near], res.at[self.a_down, near], self.a_right),
            (res.at[self.a_up, far], res.at[self.a_up, far], self.a_left),
        ]

    def settle(self, stage):
        buf, a, b, y = self.buf, self.a, self.b, self.y
        if stage == 0:
            for j in range(2):
                for k in range(2):
                    buf[self.a_up, j, k] = added(buf.at[self.a_up, j, k], self.ta1.at[0, j, k])
                    buf[self.a_down, 2 + j, k] = added(buf.at[self.a_down, 2 + j, k], self.ta1.at[1, j, k])
        elif stage == 1:
            for j in range(4):
                for k in range(2):
                    buf[a, j, k] = added(buf.at[a, j, k], self.ta2.at[0, j, k], self.ta2.at[1, j, k])
        elif stage == 2:
            buf[a, self.b_up, 0] = added(buf.at[a, self.b_up, 0], self.tb1.at[0])
            buf[a, self.b_down, 1] = added(buf.at[a, self.b_down, 1], self.tb1.at[1])
        elif stage == 3:
            for k in range(2):
                buf[a, b, k] = added(buf.at[a, b, k], self.tb2.at[0, k], self.tb2.at[1, k])
        elif stage == 4:
            self.own[...] = added(buf.at[a, b, y], self.ty)
        elif stage == 5 and self.tensor_from is not None:
            rows = pl.ds(self.tensor_from, self.own.shape[0] - self.tensor_from)
            self.tt[self.at["t"]] = self.own[rows]
            self.own[rows] = added(*(self.tt.at[n] for n in range(4)))


DP_STAGES = 11
DP_SEMS = sum(SumOverDp.counts)


def dp_scratch(rows, width, tensor_rows):
    shapes = [(2, 2, 2, rows, width), (2, 4, 2, rows, width), (2, rows, width), (2, 2, rows, width), (rows, width), (rows, width)]
    return [pltpu.VMEM(shape, jnp.bfloat16) for shape in shapes + [(4, max(tensor_rows, 16), width)]]


class SumOverTensor(Staged):
    counts = (1, 1, 2, 1)

    def __init__(self, at, buf, res, scratch, sems):
        super().__init__(*sems)
        self.buf, self.res = buf, res
        self.t0, self.t1, self.own = scratch
        self.c, self.h = at["t"] % 2, at["t"] // 2
        self.sibling = device_at(at, t=self.h * 2 + 1 - self.c)
        self.partner = device_at(at, t=(1 - self.h) * 2 + self.c)

    def copies(self, stage):
        buf, res, c, h = self.buf, self.res, self.c, self.h
        if stage == 0:
            return [(buf.at[1 - c], self.t0, self.sibling)]
        if stage == 1:
            return [(buf.at[c, 1 - h], self.t1, self.partner)]
        if stage == 2:
            return [(self.own, res.at[c, h], self.partner), (self.own, res.at[c, h], None)]
        return [(res.at[c], res.at[c], self.sibling)]

    def settle(self, stage):
        buf, c, h = self.buf, self.c, self.h
        if stage == 0:
            for n in range(2):
                buf[c, n] = added(buf.at[c, n], self.t0.at[n])
        elif stage == 1:
            self.own[...] = added(buf.at[c, h], self.t1)


TENSOR_STAGES = 4
TENSOR_SEMS = sum(SumOverTensor.counts)


def tensor_scratch(rows, width):
    return [pltpu.VMEM(shape, jnp.bfloat16) for shape in ((2, rows, width), (rows, width), (rows, width))]


def wide(tile, count=6):
    return jnp.concatenate([tile] * count, axis=1)


def mul(left, right):
    return jnp.dot(left, right, preferred_element_type=jnp.float32)


def mul_nt(left, right):
    return lax.dot_general(left, right, (((1,), (1,)), ((), ())), preferred_element_type=jnp.float32)


def mul_tn(left, right):
    return lax.dot_general(left, right, (((0,), (0,)), ((), ())), preferred_element_type=jnp.float32)


def low(value):
    return value.astype(jnp.bfloat16)


def iota(shape, dim):
    return lax.broadcasted_iota(jnp.int32, shape, dim)


def in_three(value):
    high = low(value).astype(jnp.float32)
    rest = value - high
    middle = low(rest).astype(jnp.float32)
    lane = iota(value.shape, 1)
    return low(jnp.where(lane < 16, high, jnp.where(lane < 32, middle, rest - middle)))


def exact_sum(ones, value):
    high = low(value)
    rest = value - high.astype(jnp.float32)
    middle = low(rest)
    return mul(ones, high) + mul(ones, middle) + mul(ones, low(rest - middle.astype(jnp.float32)))


def softplus(value):
    return jnp.maximum(value, 0.0) + jnp.log1p(jnp.exp(-jnp.abs(value)))


def sigmoid(value):
    return 1.0 / (1.0 + jnp.exp(-value))


def columns_of_segments(seg_ref, segc):
    segc[0:8, :] = jnp.full((8, 128), -1.0, jnp.float32)
    segc[1032:1040, :] = jnp.full((8, 128), -1.0, jnp.float32)

    def fill(k, carry):
        row = jnp.broadcast_to(seg_ref[pl.ds(k, 1), :].astype(jnp.float32), (128, 128))
        segc[pl.ds(pl.multiple_of(8 + k * 128, 8), 128), :] = row.T
        return carry

    lax.fori_loop(0, 8, fill, 0)


def kept(segc, start):
    around = segc[pl.ds(start, 144), :]
    here = around[8:, :]
    return [(pltpu.roll(around, lag, 0)[8:, :] == here).astype(jnp.float32) for lag in (1, 2, 3)]


def lagged(padded, start, keeps):
    around = padded[pl.ds(start, 136), :]
    count = around.shape[1] // 128
    return [around[8:, :]] + [pltpu.roll(around, lag, 0)[8:, :] * wide(keep[:128], count) for lag, keep in zip((1, 2, 3), keeps)]


def convolved(shifted, taps):
    total = taps[4:5, :] + taps[0:1, :] * shifted[0]
    for lag in (1, 2, 3):
        total = total + taps[lag : lag + 1, :] * shifted[lag]
    return total


def decay(k, start, segc, seg_ref, step_raw, heads):
    step = softplus(step_raw[pl.ds(start, 128), :] + heads[0:1, :])
    tri = (iota((128, 128), 0) >= iota((128, 128), 1)).astype(jnp.bfloat16)
    cum = exact_sum(tri, step * heads[1:2, :])
    seg_column = segc[pl.ds(start + 8, 128), :]
    seg_row = seg_ref[pl.ds(k, 1), :].astype(jnp.float32)
    before = segc[pl.ds(start, 8), :][7:8, :]
    last = seg_column[127:128, :]
    growth = jnp.exp(cum)
    tail = jnp.exp(cum[127:128, :] - cum) * (seg_column == last).astype(jnp.float32)
    return step, cum, seg_column, seg_row, before, last, growth, tail


def forward_kernel(
    tokens, cot, seg_ref, w_gate, w_value, w_state, w_step, w_out, taps, state_taps, heads, expand, norm_gain, gated_gain, bypass,
    normed, gate, vpad, spad, step_raw, y_out, q_out, states, sums, segc, carried,
):
    columns_of_segments(seg_ref, segc)
    vpad[0:8, :] = jnp.zeros((8, 768), jnp.float32)
    spad[0:8, :] = jnp.zeros((8, 256), jnp.float32)
    carried[...] = jnp.zeros((128, 768), jnp.float32)

    def project(k, carry):
        rows = pl.ds(pl.multiple_of(k * 256, 256), 256)
        padded = pl.ds(pl.multiple_of(8 + k * 256, 8), 256)
        hidden = tokens[rows, :].astype(jnp.float32)
        inverse = lax.rsqrt(jnp.sum(hidden * hidden, 1, keepdims=True) / 1536 + EPS)
        normal = low(hidden * inverse * norm_gain[...])
        normed[rows, :] = normal
        gate[rows, :] = mul(normal, w_gate[...])
        vpad[padded, :] = mul(normal, w_value[...])
        spad[padded, :] = mul(normal, w_state[...])
        step_raw[rows, :] = mul(normal, w_step[...])
        q_out[rows, :] = mul_nt(cot[rows, :], w_out[...])
        return carry

    lax.fori_loop(0, 4, project, 0)

    def block(k, carry):
        start = pl.multiple_of(k * 128, 128)
        rows = pl.ds(start, 128)
        keeps = kept(segc, start)
        pre = convolved(lagged(vpad, start, keeps), taps)
        x = pre * sigmoid(pre)
        pre = convolved(lagged(spad, start, keeps), state_taps)
        state = low(pre * sigmoid(pre))
        b_in, c_out = state[:, :128], state[:, 128:]
        step, cum, seg_column, seg_row, before, last, growth, tail = decay(k, start, segc, seg_ref, step_raw, heads)
        spread = mul(jnp.concatenate([in_three(step), in_three(growth), in_three(tail)], 0), expand[...])
        xs = x * spread[:128]
        start_keep = (seg_column == before).astype(jnp.float32)
        entering = carried[...]
        states[k] = low(entering)
        outside = mul(c_out, low(entering)) * (spread[128:256] * wide(start_keep))
        through = spread[255:256] * wide((last == before).astype(jnp.float32))
        carried[...] = through * entering + mul_tn(b_in, low(xs * spread[256:]))
        scores = mul_nt(c_out, b_in)
        bias = jnp.where((seg_column == seg_row) & (iota((128, 128), 0) >= iota((128, 128), 1)), 0.0, -1e30)
        cum_rows = cum.T
        first = iota((128, 128), 1) < 64
        inside = []
        for pair in range(6):
            own = xs[:, pair * 128 : (pair + 1) * 128]
            right = low(jnp.concatenate([jnp.where(first, own, 0.0), jnp.where(first, 0.0, own)], 0))
            left = [
                low(scores * jnp.exp(cum[:, h : h + 1] - cum_rows[h : h + 1, :] + bias)) for h in (2 * pair, 2 * pair + 1)
            ]
            inside.append(mul(jnp.concatenate(left, 1), right))
        y = jnp.concatenate(inside, 1) + outside + bypass[...] * x
        y_out[rows, :] = y
        raw = gate[rows, :]
        gated = y * (raw * sigmoid(raw))
        squares = jnp.sum(gated * gated, 1, keepdims=True)
        cross = jnp.sum(q_out[rows, :] * gated_gain[...] * gated, 1, keepdims=True)
        lane = iota((128, 128), 1)
        sums[k] = jnp.where(lane == 0, squares, jnp.where(lane == 1, cross, 0.0)).T[0:8, :]
        return carry

    lax.fori_loop(0, 8, block, 0)


def forward(*operands):
    f32, bf16 = jnp.float32, jnp.bfloat16
    outs = [
        ((1024, 1536), bf16),
        ((1024, 768), f32),
        ((1032, 768), f32),
        ((1032, 256), f32),
        ((1024, 128), f32),
        ((1024, 768), f32),
        ((1024, 768), f32),
        ((8, 128, 768), bf16),
        ((8, 8, 128), f32),
    ]
    return pl.pallas_call(
        forward_kernel,
        out_shape=[jax.ShapeDtypeStruct(shape, kind) for shape, kind in outs],
        in_specs=[pl.BlockSpec(memory_space=pltpu.VMEM)] * len(operands),
        out_specs=[pl.BlockSpec(memory_space=pltpu.VMEM)] * len(outs),
        scratch_shapes=[pltpu.VMEM((1040, 128), f32), pltpu.VMEM((128, 768), f32)],
        compiler_params=pltpu.CompilerParams(vmem_limit_bytes=58 * 2**20),
        name="forward",
    )(*operands)


def per_head_lanes(values):
    padded = jnp.pad(values, [(0, 0)] * (values.ndim - 1) + [(0, 4)])
    return jnp.pad(jnp.concatenate([padded] * 3, -1), [(0, 0)] * (values.ndim - 1) + [(0, 80)])


def expansion():
    row, column = iota((128, 768), 0), iota((128, 768), 1)
    return ((row < 48) & (row % 16 == column // 64)).astype(jnp.bfloat16)


def head_sums(value, expand):
    high = low(value)
    return mul_nt(high, expand) + mul_nt(low(value - high.astype(jnp.float32)), expand)


def slope(pre, sig):
    return sig * (1.0 + pre * (1.0 - sig))


def middle_block(k, total, slot, gated_gain, dy, gate_low, gate_normed, acc_v):
    rows = pl.ds(pl.multiple_of(k * 128, 128), 128)
    columns = jnp.concatenate([total] * 16, 0).T
    scale = lax.rsqrt(columns[:, 0:1] / 3072 + EPS)
    pull = columns[:, 1:2] * scale * scale * scale / 3072
    raw, y, q = slot[0], slot[1], slot[2]
    sig = sigmoid(raw)
    act = raw * sig
    gated = y * act
    scaled = gated * scale
    gate_normed[rows, :] = low(scaled * gated_gain[...])
    acc_v[5:6, :] += jnp.sum(q * scaled, 0, keepdims=True)
    grad_gated = scale * (q * gated_gain[...]) - gated * pull
    dy[rows, :] = grad_gated * act
    gate_low[rows, :] = low(grad_gated * y * slope(raw, sig))


def put(buf, i, first, count, value):
    pieces = low(value.reshape(4, 2, count, 768))
    for stream in range(2):
        buf[stream, i, :, :, first : first + count, :] = pieces[..., stream * 384 : (stream + 1) * 384]


def backward_block(
    k, vpad, spad, step_raw, seg_ref, segc, taps, state_taps, heads, expand, bypass, states, dy,
    dstate, du, dus, head_rows, value_low, state_low, step_low, acc_v, acc_s, acc_h,
):
    start = pl.multiple_of(k * 128, 128)
    rows = pl.ds(start, 128)
    keeps = kept(segc, start)
    values = lagged(vpad, start, keeps)
    pre = convolved(values, taps)
    sig = sigmoid(pre)
    x = pre * sig
    state_values = lagged(spad, start, keeps)
    state_pre = convolved(state_values, state_taps)
    state_sig = sigmoid(state_pre)
    state = low(state_pre * state_sig)
    b_in, c_out = state[:, :128], state[:, 128:]
    step, cum, seg_column, seg_row, before, last, growth, tail = decay(k, start, segc, seg_ref, step_raw, heads)
    spread = mul(jnp.concatenate([in_three(step), in_three(growth), in_three(tail)], 0), expand[...])
    step_wide, tail_wide = spread[:128], spread[256:]
    growth_wide = spread[128:256] * wide((seg_column == before).astype(jnp.float32))
    through = spread[255:256] * wide((last == before).astype(jnp.float32))
    xs = x * step_wide
    entering = states[k]
    grad_state = dstate[...]
    grad_state_low = low(grad_state)
    dyk = dy[rows, :]
    grown = low(dyk * growth_wide)
    outside = mul(c_out, entering) * growth_wide
    dxs_after = mul(b_in, grad_state_low) * tail_wide
    grad_c = mul_nt(grown, entering)
    grad_b = mul_nt(low(xs * tail_wide), grad_state_low)
    end = jnp.sum(entering.astype(jnp.float32) * grad_state, 0, keepdims=True) * through
    dstate[...] = through * grad_state + mul_tn(c_out, grown)
    scores = mul_nt(b_in, c_out)
    row, column = iota((128, 128), 0), iota((128, 128), 1)
    bias = jnp.where((seg_column == seg_row) & (row <= column), 0.0, -1e30)
    tri = (row >= column).astype(jnp.bfloat16)
    strict = row < column
    cum_rows = cum.T
    first = column < 64
    grad_scores = jnp.zeros((128, 128), jnp.float32)
    inside = []
    for pair in range(6):
        lanes = slice(pair * 128, (pair + 1) * 128)
        own = dyk[:, lanes]
        both = low(jnp.concatenate([jnp.where(first, own, 0.0), jnp.where(first, 0.0, own)], 0))
        grad_weights = mul_nt(low(xs[:, lanes]), both)
        weights, moved = [], []
        for side in range(2):
            h = 2 * pair + side
            faded = jnp.exp(cum_rows[h : h + 1, :] - cum[:, h : h + 1] + bias)
            pulled = grad_weights[:, side * 128 : (side + 1) * 128] * faded
            grad_scores = grad_scores + pulled
            moved.append(low(pulled * scores))
            weights.append(low(scores * faded))
        inside.append(mul(jnp.concatenate(weights, 1), both))
        later = mul(jnp.concatenate(moved, 0), tri)
        for side in range(2):
            h = 2 * pair + side
            part = jnp.where(strict, later[side * 128 : (side + 1) * 128], 0.0)
            head_rows[h : h + 1, :] = jnp.sum(part, 0, keepdims=True)
    grad_scores = low(grad_scores)
    grad_b = grad_b + mul(grad_scores, c_out)
    grad_c = grad_c + mul_tn(grad_scores, b_in)
    dxs = jnp.concatenate(inside, 1) + dxs_after
    dx = dxs * step_wide + bypass[...] * dyk
    summed = head_sums(jnp.concatenate([dxs * x, dyk * outside, xs * dxs_after], 0), expand[...])
    end = head_sums(jnp.broadcast_to(end, (16, 768)), expand[...])
    upper = (row <= column).astype(jnp.bfloat16)
    below = (row > column).astype(jnp.bfloat16)
    grad_decay = exact_sum(upper, summed[128:256]) + exact_sum(below, summed[256:]) + end[0:1, :] + head_rows[...].T
    grad_step = summed[:128] + heads[1:2, :] * grad_decay
    grad_raw = grad_step * sigmoid(step_raw[rows, :] + heads[0:1, :])
    step_low[rows, :] = low(jnp.where(column < 16, grad_raw, 0.0))
    acc_h[0:1, :] += jnp.sum(grad_raw, 0, keepdims=True)
    acc_h[1:2, :] += jnp.sum(step * grad_decay, 0, keepdims=True) * heads[1:2, :]
    for grad, grads, shifted, taps_ref, acc, result in (
        (dx * slope(pre, sig), du, values, taps, acc_v, value_low),
        (jnp.concatenate([grad_b, grad_c], 1) * slope(state_pre, state_sig), dus, state_values, state_taps, acc_s, state_low),
    ):
        grads[128:136, :] = grads[0:8, :]
        grads[0:128, :] = grad
        for lag in range(4):
            acc[lag : lag + 1, :] += jnp.sum(grad * shifted[lag], 0, keepdims=True)
        acc[4:5, :] += jnp.sum(grad, 0, keepdims=True)
        around = grads[...]
        count = around.shape[1] // 128
        total = grad * taps_ref[0:1, :]
        for lag, keep in zip((1, 2, 3), keeps):
            total = total + taps_ref[lag : lag + 1, :] * pltpu.roll(around * wide(keep, count), 136 - lag, 0)[:128, :]
        result[rows, :] = low(total)
    acc_v[6:7, :] += jnp.sum(dyk * x, 0, keepdims=True)


def put_small(small, acc_v, acc_s, acc_h, acc_n, step_grad):
    def block(j):
        return (j // 8, (j // 2) % 4, j % 2)

    small[...] = jnp.zeros_like(small)
    pad = jnp.zeros((8, 128), jnp.float32)
    for j in range(12):
        small[block(j) + (slice(0, 16), slice(None))] = low(step_grad[:, j * 128 : (j + 1) * 128])
    for j in range(6):
        small[block(12 + j) + (slice(0, 16), slice(None))] = low(jnp.concatenate([acc_v[:, j * 128 : (j + 1) * 128], pad], 0))
    small[block(18) + (slice(0, 16), slice(None))] = low(jnp.concatenate([acc_h[...], pad], 0))
    for j in range(2):
        small[block(j) + (slice(16, 32), slice(None))] = low(jnp.concatenate([acc_s[:, j * 128 : (j + 1) * 128], pad], 0))
    gains = [acc_n[0:1, j * 128 : (j + 1) * 128] for j in range(12)] + [jnp.zeros((4, 128), jnp.float32)]
    small[block(2) + (slice(16, 32), slice(None))] = low(jnp.concatenate(gains, 0))


class Loads:
    def __init__(self, sems):
        self.sems, self.used = sems, 0

    def make(self, src, dst):
        self.used += 1
        return pltpu.make_async_copy(src, dst, self.sems.at[self.used - 1])


def stream_copies(k, slot, sources, slots, sems):
    rows = pl.ds(pl.multiple_of(k * 128, 128), 128)
    return [pltpu.make_async_copy(src.at[rows], slots.at[slot, n], sems.at[slot, n]) for n, src in enumerate(sources)]


def backward_kernel(
    tokens, cot_in, normed_in, seg_ref, w_gate_in, w_value_in, w_state_in, w_step_in, w_out_in, taps, state_taps, heads, expand, gated_gain, bypass,
    gate, vpad, spad, step_raw, y_in, q_in, states, sums,
    big, small, branch, dx_part,
    segc, dy, gate_low, gate_normed, value_low, state_low, step_low, du, dus, dstate, head_rows, acc_v, acc_s, acc_h, acc_n,
    normed, cot, w_gate, w_value, w_state, w_step, w_out, slots, token_rows, slot_sems, sems,
):
    loads = Loads(sems)
    early_loads = [loads.make(*pair) for pair in ((normed_in, normed), (cot_in, cot), (w_out_in, w_out))]
    late_loads = [
        loads.make(*pair)
        for pair in ((w_gate_in, w_gate), (w_value_in, w_value), (w_state_in, w_state), (w_step_in, w_step))
    ]
    streamed = (gate, y_in, q_in)
    for cp in stream_copies(0, 0, streamed, slots, slot_sems) + early_loads + late_loads:
        cp.start()
    columns_of_segments(seg_ref, segc)
    for ref in (du, dus, dstate, head_rows, acc_v, acc_s, acc_h, acc_n):
        ref[...] = jnp.zeros_like(ref)

    def middle(k, carry):
        slot = k % 2

        @pl.when(k < 7)
        def _():
            for cp in stream_copies(k + 1, 1 - slot, streamed, slots, slot_sems):
                cp.start()

        for cp in stream_copies(k, slot, streamed, slots, slot_sems):
            cp.wait()
        middle_block(k, sums[k], slots.at[slot], gated_gain, dy, gate_low, gate_normed, acc_v)
        return carry

    lax.fori_loop(0, 8, middle, 0)
    for cp in early_loads:
        cp.wait()

    def early(i, carry):
        wide_columns = pl.ds(pl.multiple_of(i * 384, 128), 384)
        out_rows = pl.ds(pl.multiple_of((i % 2) * 384, 128), 384)
        out_columns = pl.ds(pl.multiple_of((i // 2) * 768, 128), 768)
        put(big, i, 0, 48, mul_tn(normed[:, wide_columns], gate_low[...]))
        put(big, i, 96, 48, mul_tn(gate_normed[:, out_rows], cot[:, out_columns]))
        rows = pl.ds(pl.multiple_of(i * 256, 256), 256)
        branch[rows, :] = low(mul(gate_normed[rows, :], w_out[...]))
        return carry

    lax.fori_loop(0, 4, early, 0)

    def scan(i, carry):
        backward_block(
            7 - i, vpad, spad, step_raw, seg_ref, segc, taps, state_taps, heads, expand, bypass, states, dy,
            dstate, du, dus, head_rows, value_low, state_low, step_low, acc_v, acc_s, acc_h,
        )
        return carry

    lax.fori_loop(0, 8, scan, 0)
    for cp in late_loads:
        cp.wait()

    def late(i, carry):
        rows = pl.ds(pl.multiple_of(i * 256, 256), 256)
        fetch = pltpu.make_async_copy(tokens.at[rows], token_rows, sems.at[7])
        fetch.start()
        wide_columns = pl.ds(pl.multiple_of(i * 384, 128), 384)
        put(big, i, 48, 48, mul_tn(normed[:, wide_columns], value_low[...]))
        thirds = [
            mul_tn(normed[:, pl.ds(pl.multiple_of(q * 512 + i * 128, 128), 128)], state_low[...]) for q in range(3)
        ]
        put(big, i, 144, 16, jnp.concatenate(thirds, 1))
        part = mul_nt(gate_low[rows, :], w_gate[...]) + mul_nt(value_low[rows, :], w_value[...])
        part = part + mul_nt(state_low[rows, :], w_state[...]) + mul_nt(step_low[rows, :], w_step[...])
        dx_part[rows, :] = low(part)
        fetch.wait()
        hidden = token_rows[...].astype(jnp.float32)
        inverse = lax.rsqrt(jnp.sum(hidden * hidden, 1, keepdims=True) / 1536 + EPS)
        acc_n[0:1, :] += jnp.sum(part * (hidden * inverse), 0, keepdims=True)
        return carry

    lax.fori_loop(0, 4, late, 0)
    step_grad = mul_tn(step_low[...], normed[...])[0:16, :]
    put_small(small, acc_v, acc_s, acc_h, acc_n, step_grad)


def backward(*operands):
    f32, bf16 = jnp.float32, jnp.bfloat16
    outs = [((2, 4, 4, 2, 160, 384), bf16), ((4, 4, 2, 32, 128), bf16), ((1024, 1536), bf16), ((1024, 1536), bf16)]
    scratch = [
        ((1040, 128), f32), ((1024, 768), f32), ((1024, 768), bf16), ((1024, 768), bf16), ((1024, 768), bf16),
        ((1024, 256), bf16), ((1024, 128), bf16), ((136, 768), f32), ((136, 256), f32), ((128, 768), f32),
        ((128, 128), f32), ((8, 768), f32), ((8, 256), f32), ((8, 128), f32), ((8, 1536), f32),
        ((1024, 1536), bf16), ((1024, 1536), bf16), ((1536, 768), bf16), ((1536, 768), bf16), ((1536, 256), bf16),
        ((1536, 128), bf16), ((768, 1536), bf16), ((2, 3, 128, 768), f32), ((256, 1536), bf16),
    ]
    vmem, hbm = pl.BlockSpec(memory_space=pltpu.VMEM), pl.BlockSpec(memory_space=pl.ANY)
    in_hbm = (0, 1, 2, 4, 5, 6, 7, 8, 15, 19, 20)
    return pl.pallas_call(
        backward_kernel,
        out_shape=[jax.ShapeDtypeStruct(shape, kind) for shape, kind in outs],
        in_specs=[hbm if n in in_hbm else vmem for n in range(len(operands))],
        out_specs=[vmem] * len(outs),
        scratch_shapes=[pltpu.VMEM(shape, kind) for shape, kind in scratch]
        + [pltpu.SemaphoreType.DMA((2, 3)), pltpu.SemaphoreType.DMA((8,))],
        compiler_params=pltpu.CompilerParams(vmem_limit_bytes=62 * 2**20),
        name="backward",
    )(*operands)


def exchange_kernel(sums, total, landed, send, recv):
    at = place()
    greet(tensor_peers(at))
    copies = [
        pltpu.make_async_remote_copy(
            src_ref=sums,
            dst_ref=landed.at[at["t"]],
            send_sem=send.at[n],
            recv_sem=recv.at[n],
            device_id=peer,
            device_id_type=MESH_ID,
        )
        for n, peer in enumerate(tensor_peers(at))
    ]
    for cp in copies:
        cp.start()
    landed[at["t"]] = sums[...]
    for cp in copies:
        cp.wait()
    total[...] = (landed[0] + landed[1]) + (landed[2] + landed[3])


def summed_over_tensor(sums):
    vmem = pl.BlockSpec(memory_space=pltpu.VMEM)
    return pl.pallas_call(
        exchange_kernel,
        out_shape=jax.ShapeDtypeStruct(sums.shape, sums.dtype),
        in_specs=[vmem],
        out_specs=vmem,
        scratch_shapes=[
            pltpu.VMEM((4,) + sums.shape, sums.dtype),
            pltpu.SemaphoreType.DMA((3,)),
            pltpu.SemaphoreType.DMA((3,)),
        ],
        compiler_params=pltpu.CompilerParams(collective_id=1, has_side_effects=True),
        name="exchange",
    )(sums)


def sum_kernel(big_in, small_in, branch_in, dx_in, big_out, small_out, branch_out, dx_out, big, small, branch, dx, *rest):
    dp0, dp1, dps, tb, td = rest[0:7], rest[7:14], rest[14:21], rest[21:24], rest[24:27]
    send, recv, local = rest[27:]
    at = place()
    loads = [
        pltpu.make_async_copy(src, dst, local.at[n])
        for n, (src, dst) in enumerate(((big_in, big), (small_in, small), (branch_in, branch), (dx_in, dx)))
    ]
    for cp in loads:
        cp.start()
    greet(dp_peers(at) + tensor_peers(at))
    for cp in loads:
        cp.wait()
    kept_rows = big.shape[4] - 16
    dp_sums = [
        SumOverDp(at, ("x", "z"), big.at[0], big_out.at[0], dp0, (send, recv, 0), kept_rows),
        SumOverDp(at, ("z", "x"), big.at[1], big_out.at[1], dp1, (send, recv, DP_SEMS), kept_rows),
        SumOverDp(at, ("x", "z"), small, small_out, dps, (send, recv, 2 * DP_SEMS), 16),
    ]
    tensor_sums = [
        SumOverTensor(at, branch, branch_out, tb, (send, recv, 3 * DP_SEMS)),
        SumOverTensor(at, dx, dx_out, td, (send, recv, 3 * DP_SEMS + TENSOR_SEMS)),
    ]
    pending = [(tensor_sums[0], n) for n in range(TENSOR_STAGES)] + [(tensor_sums[1], n) for n in range(TENSOR_STAGES)]
    for stage in range(DP_STAGES):
        for engine in dp_sums:
            engine.start(stage)
        if stage < len(pending):
            pending[stage][0].start(pending[stage][1])
        for engine in dp_sums:
            engine.finish(stage)
        if stage < len(pending):
            pending[stage][0].finish(pending[stage][1])


def summed(big, small, branch, dx):
    operands = (big, small, branch, dx)
    rows = big.shape[4]
    hbm = pl.BlockSpec(memory_space=pl.ANY)
    count = 3 * DP_SEMS + 2 * TENSOR_SEMS
    return pl.pallas_call(
        sum_kernel,
        out_shape=[jax.ShapeDtypeStruct(operand.shape, operand.dtype) for operand in operands],
        in_specs=[hbm] * 4,
        out_specs=[hbm] * 4,
        scratch_shapes=[pltpu.VMEM(operand.shape, operand.dtype) for operand in operands]
        + dp_scratch(rows, 384, 16)
        + dp_scratch(rows, 384, 16)
        + dp_scratch(32, 128, 16)
        + tensor_scratch(256, 1536)
        + tensor_scratch(256, 1536)
        + [pltpu.SemaphoreType.DMA((count,)), pltpu.SemaphoreType.DMA((count,)), pltpu.SemaphoreType.DMA((4,))],
        compiler_params=pltpu.CompilerParams(collective_id=0, has_side_effects=True, vmem_limit_bytes=56 * 2**20),
        name="sums",
    )(*operands)


def finish_kernel(tokens, cot, norm_gain, big, branch, dx, mixed, grad_tokens, gate, value, out, state):
    hidden = tokens[...].astype(jnp.float32)
    inverse = lax.rsqrt(jnp.sum(hidden * hidden, 1, keepdims=True) / 1536 + EPS)
    mixed[...] = low(hidden + branch[...].astype(jnp.float32))
    scaled = dx[...].astype(jnp.float32) * norm_gain[...]
    along = jnp.sum(scaled * hidden, 1, keepdims=True) * (inverse * inverse * inverse / 1536)
    grad_tokens[...] = cot[...].astype(jnp.float32) + inverse * scaled - hidden * along
    for stream in range(2):
        columns = slice(stream * 384, (stream + 1) * 384)
        for j in range(2):
            for y in range(2):
                part = big[stream, 0, j, y].astype(jnp.float32)
                rows = slice((j * 2 + y) * 48, (j * 2 + y + 1) * 48)
                gate[rows, columns] = part[0:48]
                value[rows, columns] = part[48:96]
                out[rows, columns] = part[96:144]
    for j in range(2):
        for y in range(2):
            rows = slice((j * 2 + y) * 16, (j * 2 + y + 1) * 16)
            left = big[0, 0, j, y, 144:160].astype(jnp.float32)
            right = big[1, 0, j, y, 144:160].astype(jnp.float32)
            state[0, rows, :] = left[:, 0:256]
            state[1, rows, 0:128] = left[:, 256:384]
            state[1, rows, 128:256] = right[:, 0:128]
            state[2, rows, :] = right[:, 128:384]


def finished(tokens, cot, norm_gain, big, branch, dx):
    f32 = jnp.float32
    by_rows = pl.BlockSpec((128, 1536), lambda g: (g, 0))
    weight = pl.BlockSpec((192, 768), lambda g: (g, 0))
    return pl.pallas_call(
        finish_kernel,
        grid=(8,),
        out_shape=[
            jax.ShapeDtypeStruct((1024, 1536), jnp.bfloat16),
            jax.ShapeDtypeStruct((1024, 1536), f32),
            jax.ShapeDtypeStruct((1536, 768), f32),
            jax.ShapeDtypeStruct((1536, 768), f32),
            jax.ShapeDtypeStruct((768, 1536), f32),
            jax.ShapeDtypeStruct((3, 512, 256), f32),
        ],
        in_specs=[
            by_rows,
            by_rows,
            pl.BlockSpec((1, 1536), lambda g: (0, 0)),
            pl.BlockSpec((2, 1, 2, 2, 160, 384), lambda g: (0, g // 2, g % 2, 0, 0, 0)),
            by_rows,
            by_rows,
        ],
        out_specs=[
            by_rows,
            by_rows,
            weight,
            weight,
            pl.BlockSpec((192, 768), lambda g: ((g // 2) % 2 * 2 + g % 2, g // 4)),
            pl.BlockSpec((3, 64, 256), lambda g: (0, g, 0)),
        ],
        compiler_params=pltpu.CompilerParams(vmem_limit_bytes=40 * 2**20),
        name="finish",
    )(tokens, cot, norm_gain, big, branch, dx)


def local(
    tokens,
    segment,
    gate_proj,
    value_proj,
    state_proj,
    step_proj,
    value_conv,
    value_conv_bias,
    state_conv,
    state_conv_bias,
    step_bias,
    log_rate,
    bypass_gain,
    norm_gain,
    gated_norm_gain,
    out_proj,
    cotangent,
):
    taps = jnp.concatenate([value_conv, value_conv_bias[None], jnp.zeros((3, 768), jnp.float32)], 0)
    state_taps = jnp.concatenate([state_conv, state_conv_bias[None], jnp.zeros((3, 256), jnp.float32)], 0)
    heads = jnp.pad(per_head_lanes(jnp.stack([step_bias, -jnp.exp(log_rate)])), ((0, 6), (0, 0)))
    segments = segment.reshape(8, 128)
    step_wide = per_head_lanes(step_proj)
    expand = expansion()
    gated_gain = gated_norm_gain[None]
    bypass = jnp.repeat(bypass_gain, 64)[None]
    normed, gate, vpad, spad, step_raw, y, q, states, sums = forward(
        tokens, cotangent, segments, gate_proj, value_proj, state_proj, step_wide, out_proj,
        taps, state_taps, heads, expand, norm_gain[None], gated_gain, bypass,
    )
    sums = summed_over_tensor(sums)
    big, small, branch, dx = backward(
        tokens, cotangent, normed, segments, gate_proj, value_proj, state_proj, step_wide, out_proj,
        taps, state_taps, heads, expand, gated_gain, bypass, gate, vpad, spad, step_raw, y, q, states, sums,
    )
    quarters = (2, 2, 256, 1536)
    big, small, branch, dx = summed(big, small, branch.reshape(quarters), dx.reshape(quarters))
    mixed_out, grad_tokens, grad_gate, grad_value, grad_out, grad_state = finished(
        tokens, cotangent, norm_gain[None], big, branch.reshape(1024, 1536), dx.reshape(1024, 1536)
    )
    small = small.reshape(32, 32, 128).astype(jnp.float32)
    grad_step = jnp.concatenate([small[j, 0:12] for j in range(12)], 1).T
    channels = jnp.concatenate([small[12 + j, 0:8] for j in range(6)], 1)
    states_small = jnp.concatenate([small[j, 16:24] for j in range(2)], 1)
    return (
        mixed_out,
        grad_tokens,
        grad_gate,
        grad_value,
        grad_state.reshape(1536, 256),
        grad_step,
        channels[0:4],
        channels[4],
        states_small[0:4],
        states_small[4],
        small[18, 0, 0:12],
        small[18, 1, 0:12],
        channels[6].reshape(12, 64).sum(1),
        small[2, 16:28].reshape(1536),
        channels[5],
        grad_out,
    )


def solution(mesh):
    placed = (
        P("dp", None),
        P("dp", None),
        P(None, "tensor"),
        P(None, "tensor"),
        P(),
        P(None, "tensor"),
        P(None, "tensor"),
        P("tensor"),
        P(),
        P(),
        P("tensor"),
        P("tensor"),
        P("tensor"),
        P(),
        P("tensor"),
        P("tensor", None),
        P("dp", None),
    )
    return jax.shard_map(
        local,
        mesh=mesh,
        in_specs=placed,
        out_specs=(
            P("dp", None),
            P("dp", None),
            P(None, "tensor"),
            P(None, "tensor"),
            P(),
            P(None, "tensor"),
            P(None, "tensor"),
            P("tensor"),
            P(),
            P(),
            P("tensor"),
            P("tensor"),
            P("tensor"),
            P(),
            P("tensor"),
            P("tensor", None),
        ),
        check_vma=False,
    )
```

time: 726 us -> 320 us (0.44)
  Pallas kernels: 0 us -> 287 us
  waiting for transfers between devices: 220 us -> 0 us
  blocking collectives: 169 us -> 0 us
  matrix products: 153 us -> 0 us
  other arithmetic: 86.6 us -> 7.8 us
  local copies, waits for them, and re-layouts: 54.2 us -> 23.7 us
  starting transfers between devices: 19.2 us -> 0 us
  between operations: 18.9 us -> 0.92 us
    pallas_call x0 -> x5, Pallas kernels: none -> 287 us  [the longest x1 168 us: summed(): pl.pallas_call(sum_kernel, out_shape=[jax.ShapeDtypeStruct(operand.shape,...]
    psum x2 -> x0, waiting for transfers between devices: 187 us -> none  [the longest x1 187 us: local(): lax.psum(grad_gate_proj.astype(jnp.bfloat16), 'dp').astype(jnp.float32)]
    psum x1 -> x0, blocking collectives: 160 us -> none  [local(): lax.psum(grad_step_proj.astype(jnp.bfloat16), 'dp').astype(jnp.float32)]
    dot_general x29 -> x0, matrix products: 153 us -> none  [the longest x3 48.4 us: state_space(): jnp.einsum('khts,kshp->kthp', weights, blocked, precision=HIGH_ACCURACY)]
    reduce_sum x14 -> x1, other arithmetic: 34 us -> 0.63 us  [local(): channels[6].reshape(12, 64).sum(1)]
    all_to_all x5 -> x0, waiting for transfers between devices: 32.7 us -> none  [the longest x4 32.7 us: sent_to_all(): return lax.all_to_all(copies, axis, split_axis=0, concat_axis=0, tiled=True)]
    convert_element_type x23 -> x2, other arithmetic: 27.1 us -> 1.83 us  [the longest x1 1 us: local(): small = small.reshape(32, 32, 128).astype(jnp.float32)]
    all_to_all x5 -> x0, starting transfers between devices: 19.1 us -> none  [the longest x4 14.4 us: sent_to_all(): return lax.all_to_all(copies, axis, split_axis=0, concat_axis=0, tiled=True)]
  transfers between devices with their start and end apart: 8 -> 0, of which waited for: 4 -> 0; matrix products, arithmetic and copies ran while one was open for 27% -> 0% of each run, Pallas kernels for 0% -> 0%
where the time goes in v2:
time: 320 us; the launch traced here: 319 us
  Pallas kernels  287 us (90%)
  local copies, waits for them, and re-layouts  23.7 us (7%)
  other arithmetic  7.8 us (2%)
    pallas_call x1, Pallas kernels, summed(): pl.pallas_call(sum_kernel, out_shape=[jax.ShapeDtypeStruct(operand.shape,...  168 us
    pallas_call x1, Pallas kernels, backward(): pl.pallas_call(backward_kernel, out_shape=[jax.ShapeDtypeStruct(shape, ki...  66.6 us
    pallas_call x1, Pallas kernels, forward(): pl.pallas_call(forward_kernel, out_shape=[jax.ShapeDtypeStruct(shape, kin...  32.2 us
    unnamed x30, local copies, waits for them, and re-layouts  13.4 us
    pallas_call x1, Pallas kernels, finished(): pl.pallas_call(finish_kernel, grid=(8,), out_shape=[jax.ShapeDtypeStruct(...  12.8 us
    pallas_call x1, Pallas kernels, summed_over_tensor(): pl.pallas_call(exchange_kernel, out_shape=jax.ShapeDtypeStruct(sums.shape...  7.19 us

profile of v2, /device:TPU:0, one launch (start us, length us, event | category | flops | bytes accessed | tf_op | source)
XLA Modules:
  0.0 319.0 jit_solution(3429427889031581595)
XLA Ops:
  2.8 1.3 broadcast_in_dim.27.gated_gain
  4.7 1.3 broadcast_in_dim.22.norm_gain
  6.0 1.4 maximum_maximum_fusion.1.state_taps
  7.4 0.7 broadcast_in_dim.28
  8.8 1.4 maximum_maximum_fusion.taps
  10.1 0.8 pad.20
  11.0 0.8 fusion.1.expand
  12.0 0.8 pad.21.w_step.w_step_in
  12.8 32.2 %forward.1 = (bf16[1024,1536]{1,0:T(8,128)(2,1)}, f32[1024,768]{1,0:T(8,128)}, f32[1032,768]{1,0:T(8,128)}, f32[1032,256]{1,0:T(8,128)}, f32[1024,128]{1,0:T(8,1...) custom-call(bf16[1024,1536]{1,0:T(8,128)(2,1)} %tokens.5, ...), custom_call_target="tpu_custom_call" | custom-call | tf_op jit(solution)/shard_map/forward/pallas_call | solution.py:374
  45.1 7.2 %exchange.1.sums = f32[8,8,128]{2,1,0:T(8,128)} custom-call(f32[8,8,128]{2,1,0:T(8,128)} %get-tuple-element.47.sums), custom_call_target="tpu_custom_call" | custom-call | tf_op jit(solution)/shard_map/exchange/pallas_call | solution.py:684
  52.3 66.6 %backward.1 = (bf16[2,4,4,2,160,384]{5,4,3,2,1,0:T(8,128)(2,1)}, bf16[4,4,2,32,128]{4,3,2,1,0:T(8,128)(2,1)}, bf16[1024,1536]{1,0:T(8,128)(2,1)}, bf16[1024,1536]{1,0:T(8,128)(2,1)}) custom-call(bf16[1024,1536]{1,0:T(8,128)(2,1)} %tokens.5, bf16[1024,1536]{1,0:T(8,128)(2,1)} %cot.3, bf16[1024,1536]{1,0:T(8,128)(2,1)} %get-tuple-element.39.normed_in, ...), custom_call_target="tpu_custom_call" | custom-call | tf_op jit(solution)/shard_map/backward/pallas_call | solution.py:648
  118.9 167.8 %sums.1 = (bf16[2,4,4,2,160,384]{5,4,3,2,1,0:T(8,128)(2,1)}, bf16[4,4,2,32,128]{4,3,2,1,0:T(8,128)(2,1)}, bf16[2,2,256,1536]{3,2,1,0:T(8,128)(2,1)}, bf16[2,2,256,1536]{3,2,1,0:T(8,128)(2,1)}) custom-call(bf16[2,4,4,2,160,384]{5,4,3,2,1,0:T(8,128)(2,1)} %get-tuple-element.48.big_in, bf16[4,4,2,32,128]{4,3,2,1,0:T(8,128)(2,1)} %get-tuple-element.49.small_in, ...), custom_call_target="tpu_custom_call" | custom-call | tf_op jit(solution)/shard_map/sums/pallas_call | solution.py:739
  286.7 1.0 bitcast_convert_fusion
  292.0 0.7 constant_dynamic-update-slice_fusion.11
  292.7 0.7 constant_dynamic-update-slice_fusion.10
  293.4 0.7 constant_dynamic-update-slice_fusion.9
  294.1 0.7 constant_dynamic-update-slice_fusion.8
  295.5 0.7 constant_dynamic-update-slice_fusion.6
  296.2 0.7 constant_dynamic-update-slice_fusion.5
  298.3 0.7 constant_dynamic-update-slice_fusion.2
  300.4 1.9 copy-done.1
  302.3 1.9 copy-done.2
  304.2 1.9 copy-done.3
  306.1 12.8 %finish.1 = (bf16[1024,1536]{1,0:T(8,128)(2,1)}, f32[1024,1536]{1,0:T(8,128)}, f32[1536,768]{1,0:T(8,128)}, f32[1536,768]{1,0:T(8,128)}, f32[768,1536]{1,0:T(8,128)}, /*index=5*/f32[3,512,256]{2,1,0:T(8,128)}) custom-call(bf16[1024,1536]{1,0:T(8,128)(2,1)S(1)} %copy-done, bf16[1024,1536]{1,0:T(8,128)(2,1)S(1)} %copy-done.1, f32[1,1536]{1,0:T(1,128)S(1)} %copy-done.4, ...), custom_call_target="tpu_custom_call" | custom-call | tf_op jit(solution)/shard_map/finish/pallas_call | solution.py:787
  (45 shorter events, 11.5 us)
Async XLA Ops:
  118.8 181.6 %copy-start = (bf16[1024,1536]{1,0:T(8,128)(2,1)S(1)}, bf16[1024,1536]{1,0:T(8,128)(2,1)}, u32[]{:S(2)}) copy-start(bf16[1024,1536]{1,0:T(8,128)(2,1)} %tokens.5) | copy-start | bytes 9437188
  118.9 181.5 %copy-start.4 = (f32[1,1536]{1,0:T(1,128)S(1)}, f32[1,1536]{1,0:T(1,128)}, u32[]{:S(2)}) copy-start(f32[1,1536]{1,0:T(1,128)} %broadcast_in_dim.22.norm_gain) | copy-start | bytes 18436
  287.7 2.4 copy-start.5
  300.4 18.5 %copy-start.6 = (f32[12,1536]{1,0:T(8,128)}, f32[12,1536]{1,0:T(8,128)S(1)}, u32[]{:S(2)}) copy-start(f32[12,1536]{1,0:T(8,128)S(1)} %constant_dynamic-update-slice_fusion) | copy-start | bytes 221188
  300.4 1.9 copy-start.1
  302.3 1.9 copy-start.2
  304.2 1.9 copy-start.3

commit v3 on v2

v3 whole, which is shorter than its diff:
```python
import functools

import jax
import jax.numpy as jnp
from jax import lax
from jax.experimental import pallas as pl
from jax.experimental.pallas import tpu as pltpu
from jax.sharding import PartitionSpec as P

EPS = 1e-05
MESH_ID = pl.DeviceIdType.MESH


def place():
    dp = lax.axis_index("dp")
    tensor = lax.axis_index("tensor")
    return {"x": dp // 8, "y": (dp // 4) % 2, "z": dp % 4, "t": tensor}


def device_at(at, **moved):
    spot = dict(at, **moved)
    return (spot["x"] * 8 + spot["y"] * 4 + spot["z"], spot["t"])


def dp_peers(at):
    return [
        device_at(at, x=(at["x"] + 1) % 4),
        device_at(at, x=(at["x"] + 3) % 4),
        device_at(at, z=(at["z"] + 1) % 4),
        device_at(at, z=(at["z"] + 3) % 4),
        device_at(at, y=1 - at["y"]),
    ]


def tensor_peers(at):
    return [device_at(at, t=(at["t"] + step) % 4) for step in (1, 2, 3)]


def greet(peers):
    barrier = pltpu.get_barrier_semaphore()
    for peer in peers:
        pl.semaphore_signal(barrier, inc=1, device_id=peer, device_id_type=MESH_ID)
    pl.semaphore_wait(barrier, len(peers))


def added(*refs):
    total = refs[0][...].astype(jnp.float32)
    for ref in refs[1:]:
        total = total + ref[...].astype(jnp.float32)
    return total.astype(jnp.bfloat16)


class Staged:
    def __init__(self, send, recv, first):
        self.send, self.recv, self.first = send, recv, first

    def made(self, stage):
        at = self.first + sum(self.counts[:stage])
        for n, (src, dst, peer) in enumerate(self.copies(stage)):
            if peer is None:
                yield pltpu.make_async_copy(src, dst, self.recv.at[at + n])
            else:
                yield pltpu.make_async_remote_copy(
                    src_ref=src,
                    dst_ref=dst,
                    send_sem=self.send.at[at + n],
                    recv_sem=self.recv.at[at + n],
                    device_id=peer,
                    device_id_type=MESH_ID,
                )

    def start(self, stage):
        for cp in self.made(stage):
            cp.start()

    def finish(self, stage):
        for cp in self.made(stage):
            cp.wait()
        self.settle(stage)


class SumOverDp(Staged):
    counts = (2, 2, 3, 1, 3, 4, 2, 2)

    def __init__(self, at, order, buf, res, scratch, sems, across=None):
        super().__init__(*sems)
        self.at, self.buf, self.res, self.across = at, buf, res, across
        self.ta1, self.ta2, self.tb, self.ty, self.own, self.tt = scratch
        a_axis, b_axis = order
        self.a, self.b = at[a_axis], at[b_axis]
        self.a_up, self.a_down, self.a_far = [(self.a + n) % 4 for n in (1, 3, 2)]
        self.a_right, self.a_left = [device_at(at, **{a_axis: n}) for n in (self.a_up, self.a_down)]
        self.b_others = [(self.b + n) % 4 for n in (1, 2, 3)]
        self.b_peers = [device_at(at, **{b_axis: n}) for n in self.b_others]
        self.other = device_at(at, y=1 - at["y"])

    def copies(self, stage):
        buf, res, a, b, own = self.buf, self.res, self.a, self.b, self.own
        near, far = pl.ds(0, 2), pl.ds(2, 2)
        if stage == 0:
            return [(buf.at[self.a_far, near], self.ta1.at[0], self.a_right), (buf.at[self.a_far, far], self.ta1.at[1], self.a_left)]
        if stage == 1:
            return [(buf.at[self.a_up], self.ta2.at[0], self.a_right), (buf.at[self.a_down], self.ta2.at[1], self.a_left)]
        if stage == 2:
            return [(buf.at[a, j], self.tb.at[n], peer) for n, (j, peer) in enumerate(zip(self.b_others, self.b_peers))]
        if stage == 3:
            return [(buf.at[a, b], self.ty, self.other)]
        if stage == 4:
            return [(own.at[self.across], self.tt.at[self.at["t"]], peer) for peer in tensor_peers(self.at)]
        if stage == 5:
            return [(own, res.at[a, b], peer) for peer in self.b_peers] + [(own, res.at[a, b], None)]
        if stage == 6:
            return [(res.at[a], res.at[a], self.a_right), (res.at[a], res.at[a], self.a_left)]
        return [
            (res.at[self.a_down, near], res.at[self.a_down, near], self.a_right),
            (res.at[self.a_up, far], res.at[self.a_up, far], self.a_left),
        ]

    def settle(self, stage):
        buf, a, b, own = self.buf, self.a, self.b, self.own
        if stage == 0:
            for j in range(2):
                buf[self.a_up, j] = added(buf.at[self.a_up, j], self.ta1.at[0, j])
                buf[self.a_down, 2 + j] = added(buf.at[self.a_down, 2 + j], self.ta1.at[1, j])
        elif stage == 1:
            for j in range(4):
                buf[a, j] = added(buf.at[a, j], self.ta2.at[0, j], self.ta2.at[1, j])
        elif stage == 2:
            buf[a, b] = added(buf.at[a, b], *(self.tb.at[n] for n in range(3)))
        elif stage == 3:
            own[...] = added(buf.at[a, b], self.ty)
        elif stage == 4:
            self.tt[self.at["t"]] = own[self.across]
            own[self.across] = added(*(self.tt.at[n] for n in range(4)))


DP_SEMS = sum(SumOverDp.counts)


def dp_scratch(rows, width, across=16):
    shapes = [(2, 2, rows, width), (2, 4, rows, width), (3, rows, width), (rows, width), (rows, width), (4, across, width)]
    return [pltpu.VMEM(shape, jnp.bfloat16) for shape in shapes]


class SumOverTensor(Staged):
    counts = (1, 1, 2, 1)

    def __init__(self, at, columns, buf, res, scratch, sems):
        super().__init__(*sems)
        self.buf, self.res, self.columns = buf, res, columns
        self.t0, self.t1 = scratch
        self.c, self.h = at["t"] % 2, at["t"] // 2
        self.sibling = device_at(at, t=self.h * 2 + 1 - self.c)
        self.partner = device_at(at, t=(1 - self.h) * 2 + self.c)

    def copies(self, stage):
        buf, res, c, h, columns = self.buf, self.res, self.c, self.h, self.columns
        if stage == 0:
            return [(buf.at[1 - c, :, :, columns], self.t0.at[:, :, columns], self.sibling)]
        if stage == 1:
            return [(buf.at[c, 1 - h, :, columns], self.t1.at[:, columns], self.partner)]
        if stage == 2:
            mine, theirs = buf.at[c, h, :, columns], res.at[c, h, :, columns]
            return [(mine, theirs, self.partner), (mine, theirs, None)]
        return [(res.at[c, :, :, columns], res.at[c, :, :, columns], self.sibling)]

    def settle(self, stage):
        buf, c, h, columns = self.buf, self.c, self.h, self.columns
        if stage == 0:
            for n in range(2):
                buf[c, n, :, columns] = added(buf.at[c, n, :, columns], self.t0.at[n, :, columns])
        elif stage == 1:
            buf[c, h, :, columns] = added(buf.at[c, h, :, columns], self.t1.at[:, columns])


TENSOR_SEMS = sum(SumOverTensor.counts)


def wide(tile, count=6):
    return jnp.concatenate([tile] * count, axis=1)


def mul(left, right):
    return jnp.dot(left, right, preferred_element_type=jnp.float32)


def mul_nt(left, right):
    return lax.dot_general(left, right, (((1,), (1,)), ((), ())), preferred_element_type=jnp.float32)


def mul_tn(left, right):
    return lax.dot_general(left, right, (((0,), (0,)), ((), ())), preferred_element_type=jnp.float32)


def low(value):
    return value.astype(jnp.bfloat16)


def iota(shape, dim):
    return lax.broadcasted_iota(jnp.int32, shape, dim)


def in_three(value):
    high = low(value).astype(jnp.float32)
    rest = value - high
    middle = low(rest).astype(jnp.float32)
    lane = iota(value.shape, 1)
    return low(jnp.where(lane < 16, high, jnp.where(lane < 32, middle, rest - middle)))


def exact_sum(ones, value):
    high = low(value)
    rest = value - high.astype(jnp.float32)
    middle = low(rest)
    return mul(ones, high) + mul(ones, middle) + mul(ones, low(rest - middle.astype(jnp.float32)))


def softplus(value):
    return jnp.maximum(value, 0.0) + jnp.log1p(jnp.exp(-jnp.abs(value)))


def sigmoid(value):
    return 1.0 / (1.0 + jnp.exp(-value))


def columns_of_segments(seg_ref, segc):
    segc[0:8, :] = jnp.full((8, 128), -1.0, jnp.float32)
    segc[1032:1040, :] = jnp.full((8, 128), -1.0, jnp.float32)

    def fill(k, carry):
        row = jnp.broadcast_to(seg_ref[:, pl.ds(pl.multiple_of(k * 128, 128), 128)].astype(jnp.float32), (128, 128))
        segc[pl.ds(pl.multiple_of(8 + k * 128, 8), 128), :] = row.T
        return carry

    lax.fori_loop(0, 8, fill, 0)


def kept(segc, start):
    around = segc[pl.ds(start, 144), :]
    here = around[8:, :]
    return [(pltpu.roll(around, lag, 0)[8:, :] == here).astype(jnp.float32) for lag in (1, 2, 3)]


def lagged(padded, start, keeps):
    around = padded[pl.ds(start, 136), :]
    count = around.shape[1] // 128
    return [around[8:, :]] + [pltpu.roll(around, lag, 0)[8:, :] * wide(keep[:128], count) for lag, keep in zip((1, 2, 3), keeps)]


def convolved(shifted, taps):
    total = taps[4:5, :] + taps[0:1, :] * shifted[0]
    for lag in (1, 2, 3):
        total = total + taps[lag : lag + 1, :] * shifted[lag]
    return total


def decay(k, start, segc, seg_ref, step_raw, heads):
    rows = pl.ds(start, 128)
    step = softplus(step_raw[rows, :] + heads[0:1, :])
    tri = (iota((128, 128), 0) >= iota((128, 128), 1)).astype(jnp.bfloat16)
    cum = exact_sum(tri, step * heads[1:2, :])
    seg_column = segc[pl.ds(start + 8, 128), :]
    seg_row = seg_ref[:, rows].astype(jnp.float32)
    before = segc[pl.ds(start, 8), :][7:8, :]
    last = seg_column[127:128, :]
    growth = jnp.exp(cum)
    tail = jnp.exp(cum[127:128, :] - cum) * (seg_column == last).astype(jnp.float32)
    return step, cum, seg_column, seg_row, before, last, growth, tail


def expansion():
    row, column = iota((128, 768), 0), iota((128, 768), 1)
    return ((row < 48) & (row % 16 == column // 64)).astype(jnp.bfloat16)


def head_sums(value, expand):
    high = low(value)
    return mul_nt(high, expand) + mul_nt(low(value - high.astype(jnp.float32)), expand)


def slope(pre, sig):
    return sig * (1.0 + pre * (1.0 - sig))


def middle_block(k, total, gated_gain, gate, y_ref, q_ref, acc_v):
    rows = pl.ds(pl.multiple_of(k * 128, 128), 128)
    columns = jnp.concatenate([total] * 16, 0).T
    scale = lax.rsqrt(columns[:, 0:1] / 3072 + EPS)
    pull = columns[:, 1:2] * scale * scale * scale / 3072
    raw, y, q = [ref[rows, :].astype(jnp.float32) for ref in (gate, y_ref, q_ref)]
    sig = sigmoid(raw)
    act = raw * sig
    gated = y * act
    scaled = gated * scale
    y_ref[rows, :] = low(scaled * gated_gain)
    acc_v[5:6, :] += jnp.sum(q * scaled, 0, keepdims=True)
    grad_gated = scale * (q * gated_gain) - gated * pull
    q_ref[rows, :] = low(grad_gated * act)
    gate[rows, :] = low(grad_gated * y * slope(raw, sig))


def put(buf, i, value):
    pieces = low(value.reshape(4, buf.shape[3], 768))
    for stream in range(2):
        buf[stream, i] = pieces[..., stream * 384 : (stream + 1) * 384]


def backward_block(
    k, vpad, spad, step_raw, seg_ref, segc, taps, state_taps, heads, expand, bypass, states, dy,
    dstate, du, dus, head_rows, value_low, state_low, step_low, acc_v, acc_s, acc_h, between,
):
    start = pl.multiple_of(k * 128, 128)
    rows = pl.ds(start, 128)
    keeps = kept(segc, start)
    values = lagged(vpad, start, keeps)
    pre = convolved(values, taps)
    sig = sigmoid(pre)
    x = pre * sig
    state_values = lagged(spad, start, keeps)
    state_pre = convolved(state_values, state_taps)
    state_sig = sigmoid(state_pre)
    state = low(state_pre * state_sig)
    b_in, c_out = state[:, :128], state[:, 128:]
    step, cum, seg_column, seg_row, before, last, growth, tail = decay(k, start, segc, seg_ref, step_raw, heads)
    spread = mul(jnp.concatenate([in_three(step), in_three(growth), in_three(tail)], 0), expand[...])
    step_wide, tail_wide = spread[:128], spread[256:]
    growth_wide = spread[128:256] * wide((seg_column == before).astype(jnp.float32))
    through = spread[255:256] * wide((last == before).astype(jnp.float32))
    xs = x * step_wide
    entering = states[k]
    grad_state = dstate[...]
    grad_state_low = low(grad_state)
    dyk = dy[rows, :].astype(jnp.float32)
    grown = low(dyk * growth_wide)
    outside = mul(c_out, entering) * growth_wide
    dxs_after = mul(b_in, grad_state_low) * tail_wide
    grad_c = mul_nt(grown, entering)
    grad_b = mul_nt(low(xs * tail_wide), grad_state_low)
    end = jnp.sum(entering.astype(jnp.float32) * grad_state, 0, keepdims=True) * through
    dstate[...] = through * grad_state + mul_tn(c_out, grown)
    scores = mul_nt(b_in, c_out)
    row, column = iota((128, 128), 0), iota((128, 128), 1)
    bias = jnp.where((seg_column == seg_row) & (row <= column), 0.0, -1e30)
    tri = (row >= column).astype(jnp.bfloat16)
    strict = row < column
    cum_rows = cum.T
    first = column < 64
    grad_scores = jnp.zeros((128, 128), jnp.float32)
    inside = []
    for pair in range(6):
        if pair == 3:
            between()
        lanes = slice(pair * 128, (pair + 1) * 128)
        own = dyk[:, lanes]
        both = low(jnp.concatenate([jnp.where(first, own, 0.0), jnp.where(first, 0.0, own)], 0))
        grad_weights = mul_nt(low(xs[:, lanes]), both)
        weights, moved = [], []
        for side in range(2):
            h = 2 * pair + side
            faded = jnp.exp(cum_rows[h : h + 1, :] - cum[:, h : h + 1] + bias)
            pulled = grad_weights[:, side * 128 : (side + 1) * 128] * faded
            grad_scores = grad_scores + pulled
            moved.append(low(pulled * scores))
            weights.append(low(scores * faded))
        inside.append(mul(jnp.concatenate(weights, 1), both))
        later = mul(jnp.concatenate(moved, 0), tri)
        for side in range(2):
            h = 2 * pair + side
            part = jnp.where(strict, later[side * 128 : (side + 1) * 128], 0.0)
            head_rows[h : h + 1, :] = jnp.sum(part, 0, keepdims=True)
    grad_scores = low(grad_scores)
    grad_b = grad_b + mul(grad_scores, c_out)
    grad_c = grad_c + mul_tn(grad_scores, b_in)
    dxs = jnp.concatenate(inside, 1) + dxs_after
    dx = dxs * step_wide + bypass * dyk
    summed = head_sums(jnp.concatenate([dxs * x, dyk * outside, xs * dxs_after], 0), expand[...])
    end = head_sums(jnp.broadcast_to(end, (16, 768)), expand[...])
    upper = (row <= column).astype(jnp.bfloat16)
    below = (row > column).astype(jnp.bfloat16)
    grad_decay = exact_sum(upper, summed[128:256]) + exact_sum(below, summed[256:]) + end[0:1, :] + head_rows[...].T
    grad_step = summed[:128] + heads[1:2, :] * grad_decay
    grad_raw = grad_step * sigmoid(step_raw[rows, :] + heads[0:1, :])
    step_low[rows, :] = low(jnp.where(column < 16, grad_raw, 0.0))
    acc_h[0:1, :] += jnp.sum(grad_raw, 0, keepdims=True)
    acc_h[1:2, :] += jnp.sum(step * grad_decay, 0, keepdims=True) * heads[1:2, :]
    for grad, grads, shifted, taps_ref, acc, result in (
        (dx * slope(pre, sig), du, values, taps, acc_v, value_low),
        (jnp.concatenate([grad_b, grad_c], 1) * slope(state_pre, state_sig), dus, state_values, state_taps, acc_s, state_low),
    ):
        grads[128:136, :] = grads[0:8, :]
        grads[0:128, :] = grad
        for lag in range(4):
            acc[lag : lag + 1, :] += jnp.sum(grad * shifted[lag], 0, keepdims=True)
        acc[4:5, :] += jnp.sum(grad, 0, keepdims=True)
        around = grads[...]
        count = around.shape[1] // 128
        total = grad * taps_ref[0:1, :]
        for lag, keep in zip((1, 2, 3), keeps):
            total = total + taps_ref[lag : lag + 1, :] * pltpu.roll(around * wide(keep, count), 136 - lag, 0)[:128, :]
        result[rows, :] = low(total)
    acc_v[6:7, :] += jnp.sum(dyk * x, 0, keepdims=True)


def small_block(j, across):
    first = 32 * across + 16 * (j % 2)
    return (j // 8, (j // 2) % 4, slice(first, first + 16))


def put_small(small, acc_v, acc_s, acc_h, acc_n, step_grad):
    small[...] = jnp.zeros_like(small)
    pad = jnp.zeros((8, 128), jnp.float32)
    for j in range(12):
        small[small_block(j, 0)] = low(step_grad[:, j * 128 : (j + 1) * 128])
    for j in range(6):
        small[small_block(12 + j, 0)] = low(jnp.concatenate([acc_v[:, j * 128 : (j + 1) * 128], pad], 0))
    small[small_block(18, 0)] = low(jnp.concatenate([acc_h[...], pad], 0))
    for j in range(2):
        small[small_block(j, 1)] = low(jnp.concatenate([acc_s[:, j * 128 : (j + 1) * 128], pad], 0))
    gains = [acc_n[:, j * 128 : (j + 1) * 128] for j in range(12)] + [jnp.zeros((4, 128), jnp.float32)]
    small[small_block(2, 1)] = low(jnp.concatenate(gains, 0))


SCAN_PLANS = (
    {0: ("g0>",), 1: ("o0>",), 2: ("b0>",)},
    {3: ("g1>",), 4: ("o1>",), 5: ("g2>",), 6: ("o2>",), 7: ("g3>",)},
)
AFTER_SCAN = ()
VALUE_PLANS = {0: ("o3>",), 1: ("b1>",)}
AFTER_STATE = ("g4>",)
DX_PLANS = ({2: ("o4>",)}, {2: ("v0>",), 3: ("d0>",)})
TAIL = (
    "e0>", "g5>", "s0>", "b2>", "o5>", "b3.", "d1>", "e1>", "v1>", "g6.", "s1>", "o6.",
    "s2>", "v2>", "s3>", "v3>", "s4>", "d2>", "e2>", "d3.", "s5>", "v4>", "e3.", "s6>",
    "v5>", "s7.", "v6.",
)
STEPS = dict.fromkeys("gov", (0, 1, 2, 3, 5, 6, 7)) | {"s": range(8)} | dict.fromkeys("bde", range(4))


def head_row(values, lane, group):
    row = jnp.zeros(lane.shape, jnp.float32)
    for h in range(12):
        row = jnp.where(group(lane, h), values[h], row)
    return row


def layer_kernel(
    remote,
    tokens, cot_in, w_gate_in, w_value_in, w_state_in, w_out_in,
    seg, w_step_in, value_conv, value_bias, state_conv, state_bias, norm_gain, gated_gain, step_bias, log_rate, bypass_gain,
    res_gate, res_out, res_value, res_state, res_small, res_branch, res_dx,
    normed, gate, y_ref, q_ref, vpad, spad, state_low, step_low, step_raw, segc, states, carried, du, dus, head_rows,
    acc_v, acc_s, acc_h, acc_n, taps, state_taps, heads, expand, gains,
    w_gate, w_value, w_state, w_step, w_out, cot, sums, landed,
    sum_gate, sum_out, sum_value, sum_state, small, branch,
    *rest,
):
    scratch = [rest[n * 6 : (n + 1) * 6] for n in range(7)]
    value_scratch = [
        (shared[0], own_ta2, shared[2], own_ty, *shared[4:])
        for shared, own_ta2, own_ty in zip(scratch[0:2], rest[42:44], rest[44:46])
    ]
    branch_scratch = rest[46:48]
    send, recv, local = rest[48:]
    at = place()
    dx = cot
    slots = branch.at[0]

    def fetch(k):
        return pltpu.make_async_copy(tokens.at[pl.ds(pl.multiple_of(k * 256, 256), 256)], slots.at[k % 2], local.at[k % 2])

    loads = [
        pltpu.make_async_copy(src, dst, local.at[2 + n])
        for n, (src, dst) in enumerate(
            ((w_gate_in, w_gate), (w_value_in, w_value), (w_state_in, w_state), (cot_in, cot), (w_out_in, w_out))
        )
    ]
    fetch(0).start()
    for cp in loads:
        cp.start()
    if remote:
        greet(dp_peers(at) + tensor_peers(at))

    orders = (("x", "z"), ("z", "x"))

    def pair(first, buf, res, scratch, across=None):
        return [
            SumOverDp(at, order, buf.at[n], res.at[n], scratch[n], (send, recv, (first + n) * DP_SEMS), across)
            for n, order in enumerate(orders)
        ]

    last = 9 * DP_SEMS
    dx_scratch = (w_out.at[pl.ds(0, 2)], w_out.at[2])
    left, right, both_sides = pl.ds(0, 768), pl.ds(768, 768), pl.ds(0, 1536)
    engines = {
        "g": pair(0, sum_gate, res_gate, scratch[0:2]),
        "o": pair(2, sum_out, res_out, scratch[2:4]),
        "v": pair(4, sum_value, res_value, value_scratch),
        "s": pair(6, sum_state, res_state, scratch[4:6], pl.ds(0, 32))
        + [SumOverDp(at, orders[0], small, res_small, scratch[6], (send, recv, 8 * DP_SEMS), pl.ds(32, 32))],
        "b": [SumOverTensor(at, both_sides, branch, res_branch, branch_scratch, (send, recv, last))],
        "d": [SumOverTensor(at, left, dx, res_dx, dx_scratch, (send, recv, last + TENSOR_SEMS))],
        "e": [SumOverTensor(at, right, dx, res_dx, dx_scratch, (send, recv, last + 2 * TENSOR_SEMS))],
    }

    def act(*plan):
        if not remote:
            return
        for word in plan:
            steps, step = STEPS[word[0]], int(word[1])
            if word[2:]:
                for engine in engines[word[0]]:
                    engine.finish(steps[step])
                step += 1
            if word[2:] != ".":
                for engine in engines[word[0]]:
                    engine.start(steps[step])

    def act_at(i, plans):
        for n, plan in plans.items():

            @pl.when(i == n)
            def _():
                act(*plan)

    for ref in (du, dus, head_rows, carried, acc_v, acc_s, acc_h, acc_n, taps, state_taps, gains):
        ref[...] = jnp.zeros_like(ref)
    vpad[0:8, :] = jnp.zeros((8, 768), jnp.float32)
    spad[0:8, :] = jnp.zeros((8, 256), jnp.float32)
    columns_of_segments(seg, segc)
    taps[0:4, :] = value_conv[...]
    taps[4:5, :] = value_bias[...].reshape(1, 768)
    state_taps[0:4, :] = state_conv[...]
    state_taps[4:5, :] = state_bias[...].reshape(1, 256)
    lane = iota((8, 128), 1)
    heads[...] = head_row(step_bias, lane, lambda l, h: (l % 16 == h) & (l < 48))
    rate = head_row(log_rate, lane, lambda l, h: (l % 16 == h) & (l < 48))
    heads[1:2, :] = jnp.where((lane % 16 < 12) & (lane < 48), -jnp.exp(rate), 0.0)[0:1]
    gains[0:1, :] = norm_gain[...].reshape(1, 1536)
    gains[1:2, 0:768] = gated_gain[...].reshape(1, 768)
    gains[2:3, 0:768] = head_row(bypass_gain, iota((1, 768), 1), lambda l, h: l // 64 == h)
    expand[...] = expansion()
    chosen = ((iota((12, 128), 1) % 16 == iota((12, 128), 0)) & (iota((12, 128), 1) < 48)).astype(jnp.bfloat16)
    w_step[...] = low(mul_tn(chosen, w_step_in[...]))
    for cp in loads[:3]:
        cp.wait()

    def project(k, carry):
        rows = pl.ds(pl.multiple_of(k * 256, 256), 256)
        padded = pl.ds(pl.multiple_of(8 + k * 256, 8), 256)

        @pl.when(k < 3)
        def _():
            fetch(k + 1).start()

        fetch(k).wait()
        hidden = slots[k % 2].astype(jnp.float32)
        inverse = lax.rsqrt(jnp.sum(hidden * hidden, 1, keepdims=True) / 1536 + EPS)
        normal = low(hidden * inverse * gains[0:1, :])
        normed[rows, :] = normal
        gate[rows, :] = low(mul(normal, w_gate[...]))
        vpad[padded, :] = mul(normal, w_value[...])
        spad[padded, :] = mul(normal, w_state[...])
        step_raw[rows, :] = mul_nt(normal, w_step[...])
        return carry

    lax.fori_loop(0, 4, project, 0)
    for cp in loads[3:]:
        cp.wait()

    def project_back(k, carry):
        rows = pl.ds(pl.multiple_of(k * 256, 256), 256)
        q_ref[rows, :] = low(mul_nt(cot[k // 2, k % 2], w_out[...].reshape(768, 1536)))
        return carry

    lax.fori_loop(0, 4, project_back, 0)

    def forward_block(k, carry):
        start = pl.multiple_of(k * 128, 128)
        rows = pl.ds(start, 128)
        keeps = kept(segc, start)
        pre = convolved(lagged(vpad, start, keeps), taps)
        x = pre * sigmoid(pre)
        pre = convolved(lagged(spad, start, keeps), state_taps)
        state = low(pre * sigmoid(pre))
        b_in, c_out = state[:, :128], state[:, 128:]
        step, cum, seg_column, seg_row, before, last, growth, tail = decay(k, start, segc, seg, step_raw, heads)
        spread = mul(jnp.concatenate([in_three(step), in_three(growth), in_three(tail)], 0), expand[...])
        xs = x * spread[:128]
        start_keep = (seg_column == before).astype(jnp.float32)
        entering = carried[...]
        states[k] = low(entering)
        outside = mul(c_out, low(entering)) * (spread[128:256] * wide(start_keep))
        through = spread[255:256] * wide((last == before).astype(jnp.float32))
        carried[...] = through * entering + mul_tn(b_in, low(xs * spread[256:]))
        scores = mul_nt(c_out, b_in)
        bias = jnp.where((seg_column == seg_row) & (iota((128, 128), 0) >= iota((128, 128), 1)), 0.0, -1e30)
        cum_rows = cum.T
        first = iota((128, 128), 1) < 64
        inside = []
        for pair in range(6):
            own = xs[:, pair * 128 : (pair + 1) * 128]
            right = low(jnp.concatenate([jnp.where(first, own, 0.0), jnp.where(first, 0.0, own)], 0))
            left = [
                low(scores * jnp.exp(cum[:, h : h + 1] - cum_rows[h : h + 1, :] + bias)) for h in (2 * pair, 2 * pair + 1)
            ]
            inside.append(mul(jnp.concatenate(left, 1), right))
        y = jnp.concatenate(inside, 1) + outside + gains[2:3, 0:768] * x
        y_ref[rows, :] = low(y)
        raw = gate[rows, :].astype(jnp.float32)
        gated = y * (raw * sigmoid(raw))
        squares = jnp.sum(gated * gated, 1, keepdims=True)
        cross = jnp.sum(q_ref[rows, :].astype(jnp.float32) * gains[1:2, 0:768] * gated, 1, keepdims=True)
        lanes = iota((128, 128), 1)
        sums[k] = jnp.where(lanes == 0, squares, jnp.where(lanes == 1, cross, 0.0)).T[0:8, :]
        return carry

    lax.fori_loop(0, 8, forward_block, 0)

    if remote:
        peers = tensor_peers(at)
        exchange = [
            pltpu.make_async_remote_copy(
                src_ref=sums,
                dst_ref=landed.at[at["t"]],
                send_sem=send.at[last + 3 * TENSOR_SEMS + n],
                recv_sem=recv.at[last + 3 * TENSOR_SEMS + n],
                device_id=peer,
                device_id_type=MESH_ID,
            )
            for n, peer in enumerate(peers)
        ]
        for cp in exchange:
            cp.start()
        landed[at["t"]] = sums[...]
        for cp in exchange:
            cp.wait()
    else:
        for n in range(4):
            landed[n] = sums[...] * 0.75

    def middle(k, carry):
        total = (landed[0, k] + landed[1, k]) + (landed[2, k] + landed[3, k])
        middle_block(k, total, gains[1:2, 0:768], gate, y_ref, q_ref, acc_v)
        return carry

    lax.fori_loop(0, 8, middle, 0)
    gate_low, gate_normed, dy = gate, y_ref, q_ref
    value_low = y_ref

    def gate_weights(i, carry):
        put(sum_gate, i, mul_tn(normed[:, pl.ds(pl.multiple_of(i * 384, 128), 384)], gate_low[...]))
        return carry

    def out_weights(i, carry):
        out_rows = pl.ds(pl.multiple_of((i % 2) * 384, 128), 384)
        out_columns = pl.ds(pl.multiple_of((i // 2) * 768, 128), 768)
        put(sum_out, i, mul_tn(gate_normed[:, out_rows], cot[:, :, :, out_columns].reshape(1024, 768)))
        return carry

    def branch_rows(i, carry):
        rows = pl.ds(pl.multiple_of(i * 256, 256), 256)
        branch[i // 2, i % 2] = low(mul(gate_normed[rows, :], w_out[...].reshape(768, 1536)))
        return carry

    lax.fori_loop(0, 4, gate_weights, 0)
    act("g0")
    lax.fori_loop(0, 4, out_weights, 0)
    act("o0")
    lax.fori_loop(0, 4, branch_rows, 0)
    act("b0")
    carried[...] = jnp.zeros((128, 768), jnp.float32)

    def scan(i, carry):
        act_at(i, SCAN_PLANS[0])
        backward_block(
            7 - i, vpad, spad, step_raw, seg, segc, taps, state_taps, heads, expand, gains[2:3, 0:768], states, dy,
            carried, du, dus, head_rows, value_low, state_low, step_low, acc_v, acc_s, acc_h,
            lambda: act_at(i, SCAN_PLANS[1]),
        )
        return carry

    lax.fori_loop(0, 8, scan, 0)
    act(*AFTER_SCAN)

    def value_weights(i, carry):
        put(sum_value, i, mul_tn(normed[:, pl.ds(pl.multiple_of(i * 384, 128), 384)], value_low[...]))
        act_at(i, VALUE_PLANS)
        return carry

    def state_weights(i, carry):
        thirds = [
            mul_tn(normed[:, pl.ds(pl.multiple_of(q * 512 + i * 128, 128), 128)], state_low[...]) for q in range(3)
        ]
        put(sum_state, i, jnp.concatenate(thirds, 1))
        return carry

    lax.fori_loop(0, 4, value_weights, 0)
    act("v0")
    lax.fori_loop(0, 4, state_weights, 0)
    act(*AFTER_STATE)

    def dx_rows(half, i):
        rows = pl.ds(pl.multiple_of(i * 256, 256), 256)
        columns = slice(half * 768, half * 768 + 768)
        part = mul_nt(gate_low[rows, :], w_gate[columns, :]) + mul_nt(value_low[rows, :], w_value[columns, :])
        part = part + mul_nt(state_low[rows, :], w_state[columns, :]) + mul(step_low[rows, :], w_step[:, columns])
        dx[i // 2, i % 2, :, columns] = low(part)
        acc_n[0:1, columns] += jnp.sum(part * normed[rows, columns].astype(jnp.float32), 0, keepdims=True)
        act_at(i, DX_PLANS[half])

    for half in range(2):

        def dx_half(i, carry):
            dx_rows(half, i)
            return carry

        lax.fori_loop(0, 4, dx_half, 0)
        act("de"[half] + "0")
    step_grad = mul_tn(step_low[...], normed[...])[0:16, :]
    put_small(small, acc_v, acc_s, acc_h, acc_n[0:1, :] / gains[0:1, :], step_grad)
    act("s0", *TAIL)
    if not remote:
        results = (res_gate, res_out, res_value, res_state, res_small, res_branch, res_dx)
        copies = [
            pltpu.make_async_copy(src, dst, local.at[n])
            for n, (src, dst) in enumerate(zip((sum_gate, sum_out, sum_value, sum_state, small, branch, dx), results))
        ]
        for cp in copies:
            cp.start()
        for cp in copies:
            cp.wait()


def layer(*operands, remote=True):
    f32, bf16 = jnp.float32, jnp.bfloat16
    weight, rows = (2, 4, 4, 96, 384), (2, 2, 256, 1536)
    outs = [weight, weight, weight, (2, 4, 4, 32, 384), (4, 4, 64, 128), rows, rows]
    scratch = [
        ((1024, 1536), bf16), ((1024, 768), bf16), ((1024, 768), bf16), ((1024, 768), bf16), ((1032, 768), f32),
        ((1032, 256), f32), ((1024, 256), bf16), ((1024, 128), bf16), ((1024, 128), f32),
        ((1040, 128), f32), ((8, 128, 768), bf16), ((128, 768), f32), ((136, 768), f32), ((136, 256), f32), ((128, 128), f32),
        ((8, 768), f32), ((8, 256), f32), ((8, 128), f32), ((8, 1536), f32), ((8, 768), f32), ((8, 256), f32),
        ((8, 128), f32), ((128, 768), bf16), ((8, 1536), f32),
        ((1536, 768), bf16), ((1536, 768), bf16), ((1536, 256), bf16), ((128, 1536), bf16), ((3, 256, 1536), bf16),
        (rows, bf16), ((8, 8, 128), f32), ((4, 8, 8, 128), f32),
    ] + [(shape, bf16) for shape in outs[:6]]
    vmem, hbm, smem = [pl.BlockSpec(memory_space=space) for space in (pltpu.VMEM, pl.ANY, pltpu.SMEM)]
    count = 9 * DP_SEMS + 3 * TENSOR_SEMS + 3
    return pl.pallas_call(
        functools.partial(layer_kernel, remote),
        out_shape=[jax.ShapeDtypeStruct(shape, bf16) for shape in outs],
        in_specs=[hbm] * 6 + [vmem] * 8 + [smem] * 3,
        out_specs=[hbm] * 7,
        scratch_shapes=[pltpu.VMEM(shape, kind) for shape, kind in scratch]
        + dp_scratch(96, 384) * 4
        + dp_scratch(32, 384, 32) * 2
        + dp_scratch(64, 128, 32)
        + [pltpu.VMEM((2, 4, 96, 384), bf16)] * 2
        + [pltpu.VMEM((96, 384), bf16)] * 2
        + [pltpu.VMEM((2, 256, 1536), bf16), pltpu.VMEM((256, 1536), bf16)]
        + [pltpu.SemaphoreType.DMA((count,)), pltpu.SemaphoreType.DMA((count,)), pltpu.SemaphoreType.DMA((7,))],
        compiler_params=pltpu.CompilerParams(
            collective_id=0 if remote else None, has_side_effects=True, vmem_limit_bytes=63 * 2**20
        ),
        name="layer",
    )(*operands)


def finish_kernel(
    tokens, cot, norm_gain, sum_gate, sum_out, sum_value, sum_state, small, branch, dx,
    mixed, grad_tokens, gate, value, out, state, step, value_taps, value_bias, state_taps, state_bias, step_bias, log_rate,
    bypass, gain, mixer_gain,
):
    hidden = tokens[...].astype(jnp.float32)
    inverse = lax.rsqrt(jnp.sum(hidden * hidden, 1, keepdims=True) / 1536 + EPS)
    mixed[...] = low(hidden + branch[...].astype(jnp.float32))
    scaled = dx[...].astype(jnp.float32) * norm_gain[...].reshape(1, 1536)
    along = jnp.sum(scaled * hidden, 1, keepdims=True) * (inverse * inverse * inverse / 1536)
    grad_tokens[...] = cot[...].astype(jnp.float32) + inverse * scaled - hidden * along
    for stream in range(2):
        columns = slice(stream * 384, (stream + 1) * 384)
        for j in range(2):
            rows = slice(j * 96, (j + 1) * 96)
            for result, summed in ((gate, sum_gate), (out, sum_out), (value, sum_value)):
                result[rows, columns] = summed[stream, 0, j].astype(jnp.float32)
    for j in range(2):
        rows = slice(j * 32, (j + 1) * 32)
        first, second = [sum_state[stream, 0, j].astype(jnp.float32) for stream in range(2)]
        state[0, rows, :] = first[:, 0:256]
        state[1, rows, 0:128] = first[:, 256:384]
        state[1, rows, 128:256] = second[:, 0:128]
        state[2, rows, :] = second[:, 128:384]

    @pl.when(pl.program_id(0) == 0)
    def _():
        def block(j, across):
            return small[small_block(j, across)].astype(jnp.float32)

        step[...] = jnp.concatenate([block(j, 0) for j in range(12)], 1)[0:12, :]
        channels = jnp.concatenate([block(12 + j, 0) for j in range(6)], 1)
        value_taps[...] = channels[0:4]
        value_bias[...] = channels[4:5].reshape(768)
        mixer_gain[...] = channels[5:6].reshape(768)
        bypass[...] = mul_nt(low(channels), expansion())[6:7, 0:12].reshape(12)
        per_head = block(18, 0)
        step_bias[...] = per_head[0:1, 0:12].reshape(12)
        log_rate[...] = per_head[1:2, 0:12].reshape(12)
        states_small = jnp.concatenate([block(j, 1) for j in range(2)], 1)
        state_taps[...] = states_small[0:4]
        state_bias[...] = states_small[4:5].reshape(256)
        gains = block(2, 1)
        gain[...] = jnp.concatenate([gains[j : j + 1, :] for j in range(12)], 1).reshape(1536)


def finished(tokens, cot, norm_gain, *sums):
    f32 = jnp.float32
    by_rows = pl.BlockSpec((128, 1536), lambda g: (g, 0))
    weight = pl.BlockSpec((192, 768), lambda g: (g, 0))

    def whole(*shape):
        return pl.BlockSpec(shape, lambda g: (0,) * len(shape))

    rest = [(12, 1536), (4, 768), (768,), (4, 256), (256,), (12,), (12,), (12,), (1536,), (768,)]
    return pl.pallas_call(
        finish_kernel,
        grid=(8,),
        out_shape=[
            jax.ShapeDtypeStruct((1024, 1536), jnp.bfloat16),
            jax.ShapeDtypeStruct((1024, 1536), f32),
            jax.ShapeDtypeStruct((1536, 768), f32),
            jax.ShapeDtypeStruct((1536, 768), f32),
            jax.ShapeDtypeStruct((768, 1536), f32),
            jax.ShapeDtypeStruct((3, 512, 256), f32),
        ]
        + [jax.ShapeDtypeStruct(shape, f32) for shape in rest],
        in_specs=[
            by_rows,
            by_rows,
            whole(1536),
            *[pl.BlockSpec((2, 1, 2, 96, 384), lambda g: (0, g // 2, g % 2, 0, 0))] * 3,
            pl.BlockSpec((2, 1, 2, 32, 384), lambda g: (0, g // 2, g % 2, 0, 0)),
            whole(4, 4, 64, 128),
            by_rows,
            by_rows,
        ],
        out_specs=[
            by_rows,
            by_rows,
            weight,
            weight,
            pl.BlockSpec((192, 768), lambda g: ((g // 2) % 2 * 2 + g % 2, g // 4)),
            pl.BlockSpec((3, 64, 256), lambda g: (0, g, 0)),
        ]
        + [whole(*shape) for shape in rest],
        compiler_params=pltpu.CompilerParams(vmem_limit_bytes=60 * 2**20),
        name="finish",
    )(tokens, cot, norm_gain, *sums)


def local(
    tokens,
    segment,
    gate_proj,
    value_proj,
    state_proj,
    step_proj,
    value_conv,
    value_conv_bias,
    state_conv,
    state_conv_bias,
    step_bias,
    log_rate,
    bypass_gain,
    norm_gain,
    gated_norm_gain,
    out_proj,
    cotangent,
):
    *sums, branch, dx = layer(
        tokens, cotangent.reshape(2, 2, 256, 1536), gate_proj, value_proj, state_proj, out_proj.reshape(3, 256, 1536), segment, step_proj.T,
        value_conv, value_conv_bias, state_conv, state_conv_bias, norm_gain, gated_norm_gain, step_bias, log_rate, bypass_gain,
    )
    rows = tokens.shape
    (
        mixed_out, grad_tokens, grad_gate, grad_value, grad_out, grad_state, grad_step, grad_value_conv, grad_value_bias,
        grad_state_conv, grad_state_bias, grad_step_bias, grad_log_rate, grad_bypass, grad_gain, grad_mixer_gain,
    ) = finished(tokens, cotangent, norm_gain, *sums, branch.reshape(rows), dx.reshape(rows))
    return (
        mixed_out,
        grad_tokens,
        grad_gate,
        grad_value,
        grad_state.reshape(state_proj.shape),
        grad_step.T,
        grad_value_conv,
        grad_value_bias,
        grad_state_conv,
        grad_state_bias,
        grad_step_bias,
        grad_log_rate,
        grad_bypass,
        grad_gain,
        grad_mixer_gain,
        grad_out,
    )


def solution(mesh):
    placed = (
        P("dp", None),
        P("dp", None),
        P(None, "tensor"),
        P(None, "tensor"),
        P(),
        P(None, "tensor"),
        P(None, "tensor"),
        P("tensor"),
        P(),
        P(),
        P("tensor"),
        P("tensor"),
        P("tensor"),
        P(),
        P("tensor"),
        P("tensor", None),
        P("dp", None),
    )
    return jax.shard_map(
        local,
        mesh=mesh,
        in_specs=placed,
        out_specs=(
            P("dp", None),
            P("dp", None),
            P(None, "tensor"),
            P(None, "tensor"),
            P(),
            P(None, "tensor"),
            P(None, "tensor"),
            P("tensor"),
            P(),
            P(),
            P("tensor"),
            P("tensor"),
            P("tensor"),
            P(),
            P("tensor"),
            P("tensor", None),
        ),
        check_vma=False,
    )
```

time: 320 us -> 188 us (0.59)
  Pallas kernels: 287 us -> 187 us
  local copies, waits for them, and re-layouts: 23.7 us -> 0 us
  other arithmetic: 7.8 us -> 0 us
    pallas_call x4 -> x1, Pallas kernels: 274 us -> 168 us  [layer(): pl.pallas_call(functools.partial(layer_kernel, remote), out_shape=[jax.Sh...]
    unnamed x30 -> x0, local copies, waits for them, and re-layouts: 13.4 us -> none
    pallas_call x1, Pallas kernels: 12.8 us -> 18.6 us  [finished(): pl.pallas_call(finish_kernel, grid=(8,), out_shape=[jax.ShapeDtypeStruct(...]
    concatenate x6 -> x0, other arithmetic: 3.99 us -> none  [the longest x1 1.37 us: local(): jnp.concatenate([value_conv, value_conv_bias[None], jnp.zeros((3, 768), j...]
    broadcast_in_dim x5 -> x0, local copies, waits for them, and re-layouts: 3.97 us -> none  [the longest x1 1.29 us: local(): norm_gain[None]]
where the time goes in v3:
time: 188 us
  Pallas kernels  187 us (99%)
    pallas_call x1, Pallas kernels, layer(): pl.pallas_call(functools.partial(layer_kernel, remote), out_shape=[jax.Sh...  168 us
    pallas_call x1, Pallas kernels, finished(): pl.pallas_call(finish_kernel, grid=(8,), out_shape=[jax.ShapeDtypeStruct(...  18.6 us

profile of v3, /device:TPU:0, one launch (start us, length us, event | category | flops | bytes accessed | tf_op | source)
XLA Modules:
  0.0 187.6 jit_solution(3404433885990554480)
XLA Ops:
  0.7 168.2 %layer.1 = (bf16[2,4,4,96,384]{4,3,2,1,0:T(8,128)(2,1)}, bf16[2,4,4,96,384]{4,3,2,1,0:T(8,128)(2,1)}, bf16[2,4,4,96,384]{4,3,2,1,0:T(8,128)(2,1)}, bf16[2,4,4,32...) custom-call(bf16[1024,1536]{1,0:T(8,128)(2,1)} %tokens.3, ...), custom_call_target="tpu_custom_call" | custom-call | tf_op jit(solution)/shard_map/layer/pallas_call | solution.py:749
  168.8 18.6 %finish.1 = (bf16[1024,1536]{1,0:T(8,128)(2,1)}, f32[1024,1536]{1,0:T(8,128)}, f32[1536,768]{1,0:T(8,128)}, f32[1536,768]{1,0:T(8,128)}, f32[768,1536]{1,0:T(8,1...) custom-call(bf16[1024,1536]{1,0:T(8,128)(2,1)} %tokens.3, ...), custom_call_target="tpu_custom_call" | custom-call | tf_op jit(solution)/shard_map/finish/pallas_call | solution.py:824

commit v4 on v3

--- a/solution.py
+++ b/solution.py
@@ -40,7 +40,6 @@
     barrier = pltpu.get_barrier_semaphore()
     for peer in peers:
         pl.semaphore_signal(barrier, inc=1, device_id=peer, device_id_type=MESH_ID)
-    pl.semaphore_wait(barrier, len(peers))
 
 
 def added(*refs):
@@ -80,16 +79,18 @@
 
 
 class SumOverDp(Staged):
-    counts = (2, 2, 3, 1, 3, 4, 2, 2)
-
-    def __init__(self, at, order, buf, res, scratch, sems, across=None):
+    counts = (3, 2, 3, 1, 3, 4, 3, 2)
+
+    def __init__(self, at, order, buf, res, scratch, sems, across=None, direct=False):
         super().__init__(*sems)
-        self.at, self.buf, self.res, self.across = at, buf, res, across
+        self.at, self.buf, self.res, self.across, self.direct = at, buf, res, across, direct
         self.ta1, self.ta2, self.tb, self.ty, self.own, self.tt = scratch
         a_axis, b_axis = order
         self.a, self.b = at[a_axis], at[b_axis]
         self.a_up, self.a_down, self.a_far = [(self.a + n) % 4 for n in (1, 3, 2)]
         self.a_right, self.a_left = [device_at(at, **{a_axis: n}) for n in (self.a_up, self.a_down)]
+        self.a_others = [(self.a + n) % 4 for n in (1, 2, 3)]
+        self.a_peers = [device_at(at, **{a_axis: n}) for n in self.a_others]
         self.b_others = [(self.b + n) % 4 for n in (1, 2, 3)]
         self.b_peers = [device_at(at, **{b_axis: n}) for n in self.b_others]
         self.other = device_at(at, y=1 - at["y"])
@@ -97,6 +98,10 @@
     def copies(self, stage):
         buf, res, a, b, own = self.buf, self.res, self.a, self.b, self.own
         near, far = pl.ds(0, 2), pl.ds(2, 2)
+        if stage == 0 and self.direct:
+            return [(buf.at[i], self.ta1.at[n], peer) for n, (i, peer) in enumerate(zip(self.a_others, self.a_peers))]
+        if stage == 6 and self.direct:
+            return [(res.at[a], res.at[a], peer) for peer in self.a_peers]
         if stage == 0:
             return [(buf.at[self.a_far, near], self.ta1.at[0], self.a_right), (buf.at[self.a_far, far], self.ta1.at[1], self.a_left)]
         if stage == 1:
@@ -108,7 +113,8 @@
         if stage == 4:
             return [(own.at[self.across], self.tt.at[self.at["t"]], peer) for peer in tensor_peers(self.at)]
         if stage == 5:
-            return [(own, res.at[a, b], peer) for peer in self.b_peers] + [(own, res.at[a, b], None)]
+            home = res.at[a, b]
+            return [(own, home, peer) for peer in self.b_peers] + [(own, home, None)]
         if stage == 6:
             return [(res.at[a], res.at[a], self.a_right), (res.at[a], res.at[a], self.a_left)]
         return [
@@ -118,7 +124,10 @@
 
     def settle(self, stage):
         buf, a, b, own = self.buf, self.a, self.b, self.own
-        if stage == 0:
+        if stage == 0 and self.direct:
+            for j in range(4):
+                buf[a, j] = added(buf.at[a, j], *(self.ta1.at[n, j] for n in range(3)))
+        elif stage == 0:
             for j in range(2):
                 buf[self.a_up, j] = added(buf.at[self.a_up, j], self.ta1.at[0, j])
                 buf[self.a_down, 2 + j] = added(buf.at[self.a_down, 2 + j], self.ta1.at[1, j])
@@ -137,8 +146,9 @@
 DP_SEMS = sum(SumOverDp.counts)
 
 
-def dp_scratch(rows, width, across=16):
-    shapes = [(2, 2, rows, width), (2, 4, rows, width), (3, rows, width), (rows, width), (rows, width), (4, across, width)]
+def dp_scratch(rows, width, across=16, direct=False):
+    first = [(3, 4, rows, width), (1, 16, width)] if direct else [(2, 2, rows, width), (2, 4, rows, width)]
+    shapes = first + [(3, rows, width), (rows, width), (rows, width), (4, across, width)]
     return [pltpu.VMEM(shape, jnp.bfloat16) for shape in shapes]
 
 
@@ -174,6 +184,66 @@
 
 
 TENSOR_SEMS = sum(SumOverTensor.counts)
+
+
+class SumState(Staged):
+    counts = (1, 3, 3, 1, 1, 4, 3, 1)
+
+    def __init__(self, at, buf, res, scratch, sems):
+        super().__init__(*sems)
+        self.buf, self.res = buf, res
+        self.t0, self.ta, self.tb, self.ty, self.tt, self.own = scratch
+        x, y, z, t = at["x"], at["y"], at["z"], at["t"]
+        c = t % 2
+        self.c, self.a, self.b = c, x * (1 - c) + z * c, z * (1 - c) + x * c
+        self.sibling = device_at(at, t=t // 2 * 2 + 1 - c)
+        self.partner = device_at(at, t=(1 - t // 2) * 2 + c)
+        self.other = device_at(at, y=1 - y)
+        self.a_peers = [device_at(at, x=(x + n * (1 - c)) % 4, z=(z + n * c) % 4) for n in (1, 2, 3)]
+        self.b_peers = [device_at(at, x=(x + n * c) % 4, z=(z + n * (1 - c)) % 4) for n in (1, 2, 3)]
+
+    def copies(self, stage):
+        buf, res, a, b, c, own = self.buf, self.res, self.a, self.b, self.c, self.own
+        if stage == 0:
+            return [(buf.at[1 - c], self.t0, self.sibling)]
+        if stage == 1:
+            return [(buf.at[c, (a + n + 1) % 4], self.ta.at[n], peer) for n, peer in enumerate(self.a_peers)]
+        if stage == 2:
+            return [(buf.at[c, a, (b + n + 1) % 4], self.tb.at[n], peer) for n, peer in enumerate(self.b_peers)]
+        if stage == 3:
+            return [(buf.at[c, a, b], self.ty, self.other)]
+        if stage == 4:
+            return [(own, self.tt, self.partner)]
+        if stage == 5:
+            return [(own, res.at[c, a, b], peer) for peer in self.b_peers] + [(own, res.at[c, a, b], None)]
+        if stage == 6:
+            return [(res.at[c, a], res.at[c, a], peer) for peer in self.a_peers]
+        return [(res.at[c], res.at[c], self.sibling)]
+
+    def settle(self, stage):
+        buf, a, b, c = self.buf, self.a, self.b, self.c
+        if stage == 0:
+            for i in range(4):
+                for j in range(4):
+                    buf[c, i, j] = added(buf.at[c, i, j], self.t0.at[i, j])
+        elif stage == 1:
+            for j in range(4):
+                buf[c, a, j] = added(buf.at[c, a, j], *(self.ta.at[n, j] for n in range(3)))
+        elif stage == 2:
+            buf[c, a, b] = added(buf.at[c, a, b], *(self.tb.at[n] for n in range(3)))
+        elif stage == 3:
+            self.own[...] = added(buf.at[c, a, b], self.ty)
+        elif stage == 4:
+            self.own[...] = added(self.own, self.tt)
+
+
+STATE_SEMS = sum(SumState.counts)
+
+
+def state_scratch(rows, width):
+    block = (rows, width)
+    shapes = [(4, 4) + block, (3, 4) + block, (3,) + block, block, block, block]
+    return [pltpu.VMEM(shape, jnp.bfloat16) for shape in shapes]
 
 
 def wide(tile, count=6):
@@ -300,7 +370,7 @@
 
 
 def put(buf, i, value):
-    pieces = low(value.reshape(4, buf.shape[3], 768))
+    pieces = low(value.reshape(4, value.shape[0] // 4, 768))
     for stream in range(2):
         buf[stream, i] = pieces[..., stream * 384 : (stream + 1) * 384]
 
@@ -401,39 +471,45 @@
     acc_v[6:7, :] += jnp.sum(dyk * x, 0, keepdims=True)
 
 
-def small_block(j, across):
-    first = 32 * across + 16 * (j % 2)
-    return (j // 8, (j // 2) % 4, slice(first, first + 16))
-
-
-def put_small(small, acc_v, acc_s, acc_h, acc_n, step_grad):
+def put_small(small, acc_v, acc_h, step_grad):
     small[...] = jnp.zeros_like(small)
-    pad = jnp.zeros((8, 128), jnp.float32)
+    rows = [acc_v[n : n + 1, j * 128 : (j + 1) * 128] for n in range(7) for j in range(6)] + [acc_h[0:1, :], acc_h[1:2, :]]
+    place_in = iota((16, 128), 0)
     for j in range(12):
-        small[small_block(j, 0)] = low(step_grad[:, j * 128 : (j + 1) * 128])
-    for j in range(6):
-        small[small_block(12 + j, 0)] = low(jnp.concatenate([acc_v[:, j * 128 : (j + 1) * 128], pad], 0))
-    small[small_block(18, 0)] = low(jnp.concatenate([acc_h[...], pad], 0))
-    for j in range(2):
-        small[small_block(j, 1)] = low(jnp.concatenate([acc_s[:, j * 128 : (j + 1) * 128], pad], 0))
-    gains = [acc_n[:, j * 128 : (j + 1) * 128] for j in range(12)] + [jnp.zeros((4, 128), jnp.float32)]
-    small[small_block(2, 1)] = low(jnp.concatenate(gains, 0))
+        block = jnp.where(place_in < 12, step_grad[:, j * 128 : (j + 1) * 128], 0.0)
+        for n, row in enumerate(rows[4 * j : 4 * j + 4]):
+            block = jnp.where(place_in == 12 + n, row, block)
+        small[j // 4, j % 4] = low(block)
+
+
+def put_shared(shared, acc_s, acc_n):
+    shared[...] = jnp.zeros_like(shared)
+    place_in = iota((16, 128), 0)
+    for j, rows in enumerate(
+        (
+            [acc_n[:, n * 128 : (n + 1) * 128] for n in range(12)],
+            [acc_s[n : n + 1, j * 128 : (j + 1) * 128] for n in range(5) for j in range(2)],
+        )
+    ):
+        block = jnp.zeros((16, 128), jnp.float32)
+        for n, row in enumerate(rows):
+            block = jnp.where(place_in == n, row, block)
+        shared[0, j] = low(block)
 
 
 SCAN_PLANS = (
-    {0: ("g0>",), 1: ("o0>",), 2: ("b0>",)},
-    {3: ("g1>",), 4: ("o1>",), 5: ("g2>",), 6: ("o2>",), 7: ("g3>",)},
+    {4: ("g2>",), 6: ("o0>", "b1>"), 7: ("g4>",)},
+    {0: ("b0>",), 2: ("g1>",), 4: ("o0",), 5: ("g3>",)},
 )
 AFTER_SCAN = ()
-VALUE_PLANS = {0: ("o3>",), 1: ("b1>",)}
-AFTER_STATE = ("g4>",)
-DX_PLANS = ({2: ("o4>",)}, {2: ("v0>",), 3: ("d0>",)})
+VALUE_PLANS = {}
+AFTER_STATE = ("o1>",)
+DX_PLANS = ({3: ("g5>", "b2>")}, {0: ("v0>",), 1: ("o2>",), 3: ("d0>", "g6.", "o3>", "b3.")})
 TAIL = (
-    "e0>", "g5>", "s0>", "b2>", "o5>", "b3.", "d1>", "e1>", "v1>", "g6.", "s1>", "o6.",
-    "s2>", "v2>", "s3>", "v3>", "s4>", "d2>", "e2>", "d3.", "s5>", "v4>", "e3.", "s6>",
-    "v5>", "s7.", "v6.",
+    "v1>", "e0>", "s0>", "o4>", "d1>", "v2>", "s1>", "s2>", "o5>", "v3>", "s3>", "e1>",
+    "s4>", "o6.", "v4>", "d2>", "s5>", "d3.", "e2>", "s6>", "e3.", "v5>", "s7.", "v6.",
 )
-STEPS = dict.fromkeys("gov", (0, 1, 2, 3, 5, 6, 7)) | {"s": range(8)} | dict.fromkeys("bde", range(4))
+RING = (0, 1, 2, 3, 5, 6, 7)
 
 
 def head_row(values, lane, group):
@@ -447,17 +523,17 @@
     remote,
     tokens, cot_in, w_gate_in, w_value_in, w_state_in, w_out_in,
     seg, w_step_in, value_conv, value_bias, state_conv, state_bias, norm_gain, gated_gain, step_bias, log_rate, bypass_gain,
-    res_gate, res_out, res_value, res_state, res_small, res_branch, res_dx,
+    res_gate, res_out, res_value, res_state, res_small, res_shared, res_branch, res_dx,
     normed, gate, y_ref, q_ref, vpad, spad, state_low, step_low, step_raw, segc, states, carried, du, dus, head_rows,
     acc_v, acc_s, acc_h, acc_n, taps, state_taps, heads, expand, gains,
     w_gate, w_value, w_state, w_step, w_out, cot, sums, landed,
-    sum_gate, sum_out, sum_value, sum_state, small, branch,
+    sum_gate, sum_out, sum_value, sum_state, small, shared, branch,
     *rest,
 ):
     scratch = [rest[n * 6 : (n + 1) * 6] for n in range(7)]
     value_scratch = [
-        (shared[0], own_ta2, shared[2], own_ty, *shared[4:])
-        for shared, own_ta2, own_ty in zip(scratch[0:2], rest[42:44], rest[44:46])
+        (early[0], own_ta2, early[2], own_ty, *early[4:])
+        for early, own_ta2, own_ty in zip(scratch[0:2], rest[42:44], rest[44:46])
     ]
     branch_scratch = rest[46:48]
     send, recv, local = rest[48:]
@@ -475,45 +551,54 @@
         )
     ]
     fetch(0).start()
-    for cp in loads:
+    for cp in loads[:3]:
         cp.start()
+    friends = dp_peers(at) + tensor_peers(at)
     if remote:
-        greet(dp_peers(at) + tensor_peers(at))
+        greet(friends)
 
     orders = (("x", "z"), ("z", "x"))
 
-    def pair(first, buf, res, scratch, across=None):
+    def pair(first, buf, res, scratch):
         return [
-            SumOverDp(at, order, buf.at[n], res.at[n], scratch[n], (send, recv, (first + n) * DP_SEMS), across)
+            (SumOverDp(at, order, buf.at[n], res.at[n], scratch[n], (send, recv, (first + n) * DP_SEMS)), RING)
             for n, order in enumerate(orders)
         ]
 
-    last = 9 * DP_SEMS
+    last = 8 * DP_SEMS + STATE_SEMS
     dx_scratch = (w_out.at[pl.ds(0, 2)], w_out.at[2])
     left, right, both_sides = pl.ds(0, 768), pl.ds(768, 768), pl.ds(0, 1536)
     engines = {
         "g": pair(0, sum_gate, res_gate, scratch[0:2]),
         "o": pair(2, sum_out, res_out, scratch[2:4]),
-        "v": pair(4, sum_value, res_value, value_scratch),
-        "s": pair(6, sum_state, res_state, scratch[4:6], pl.ds(0, 32))
-        + [SumOverDp(at, orders[0], small, res_small, scratch[6], (send, recv, 8 * DP_SEMS), pl.ds(32, 32))],
-        "b": [SumOverTensor(at, both_sides, branch, res_branch, branch_scratch, (send, recv, last))],
-        "d": [SumOverTensor(at, left, dx, res_dx, dx_scratch, (send, recv, last + TENSOR_SEMS))],
-        "e": [SumOverTensor(at, right, dx, res_dx, dx_scratch, (send, recv, last + 2 * TENSOR_SEMS))],
+        "v": pair(4, sum_value, res_value, value_scratch)
+        + [(SumOverDp(at, orders[0], small, res_small, scratch[4], (send, recv, 6 * DP_SEMS)), RING)],
+        "s": [
+            (SumState(at, sum_state, res_state, scratch[6], (send, recv, 8 * DP_SEMS)), range(8)),
+            (
+                SumOverDp(at, orders[0], shared, res_shared, scratch[5], (send, recv, 7 * DP_SEMS), pl.ds(0, 16), True),
+                (None, 0, 2, 3, 4, 5, 6, None),
+            ),
+        ],
+        "b": [(SumOverTensor(at, both_sides, branch, res_branch, branch_scratch, (send, recv, last)), range(4))],
+        "d": [(SumOverTensor(at, left, dx, res_dx, dx_scratch, (send, recv, last + TENSOR_SEMS)), range(4))],
+        "e": [(SumOverTensor(at, right, dx, res_dx, dx_scratch, (send, recv, last + 2 * TENSOR_SEMS)), range(4))],
     }
 
     def act(*plan):
         if not remote:
             return
         for word in plan:
-            steps, step = STEPS[word[0]], int(word[1])
+            step = int(word[1])
             if word[2:]:
-                for engine in engines[word[0]]:
-                    engine.finish(steps[step])
+                for engine, stages in engines[word[0]]:
+                    if stages[step] is not None:
+                        engine.finish(stages[step])
                 step += 1
             if word[2:] != ".":
-                for engine in engines[word[0]]:
-                    engine.start(steps[step])
+                for engine, stages in engines[word[0]]:
+                    if stages[step] is not None:
+                        engine.start(stages[step])
 
     def act_at(i, plans):
         for n, plan in plans.items():
@@ -543,6 +628,8 @@
     w_step[...] = low(mul_tn(chosen, w_step_in[...]))
     for cp in loads[:3]:
         cp.wait()
+    for cp in loads[3:]:
+        cp.start()
 
     def project(k, carry):
         rows = pl.ds(pl.multiple_of(k * 256, 256), 256)
@@ -617,6 +704,7 @@
     lax.fori_loop(0, 8, forward_block, 0)
 
     if remote:
+        pl.semaphore_wait(pltpu.get_barrier_semaphore(), len(friends))
         peers = tensor_peers(at)
         exchange = [
             pltpu.make_async_remote_copy(
@@ -664,10 +752,10 @@
 
     lax.fori_loop(0, 4, gate_weights, 0)
     act("g0")
-    lax.fori_loop(0, 4, out_weights, 0)
-    act("o0")
     lax.fori_loop(0, 4, branch_rows, 0)
     act("b0")
+    lax.fori_loop(0, 4, out_weights, 0)
+    act("g0>")
     carried[...] = jnp.zeros((128, 768), jnp.float32)
 
     def scan(i, carry):
@@ -695,6 +783,7 @@
         return carry
 
     lax.fori_loop(0, 4, value_weights, 0)
+    put_small(small, acc_v, acc_h, mul_tn(step_low[...], normed[...])[0:16, :])
     act("v0")
     lax.fori_loop(0, 4, state_weights, 0)
     act(*AFTER_STATE)
@@ -716,14 +805,13 @@
 
         lax.fori_loop(0, 4, dx_half, 0)
         act("de"[half] + "0")
-    step_grad = mul_tn(step_low[...], normed[...])[0:16, :]
-    put_small(small, acc_v, acc_s, acc_h, acc_n[0:1, :] / gains[0:1, :], step_grad)
+    put_shared(shared, acc_s, acc_n[0:1, :] / gains[0:1, :])
     act("s0", *TAIL)
     if not remote:
-        results = (res_gate, res_out, res_value, res_state, res_small, res_branch, res_dx)
+        results = (res_gate, res_out, res_value, res_state, res_small, res_shared, res_branch, res_dx)
         copies = [
             pltpu.make_async_copy(src, dst, local.at[n])
-            for n, (src, dst) in enumerate(zip((sum_gate, sum_out, sum_value, sum_state, small, branch, dx), results))
+            for n, (src, dst) in enumerate(zip((sum_gate, sum_out, sum_value, sum_state, small, shared, branch, dx), results))
         ]
         for cp in copies:
             cp.start()
@@ -734,7 +822,7 @@
 def layer(*operands, remote=True):
     f32, bf16 = jnp.float32, jnp.bfloat16
     weight, rows = (2, 4, 4, 96, 384), (2, 2, 256, 1536)
-    outs = [weight, weight, weight, (2, 4, 4, 32, 384), (4, 4, 64, 128), rows, rows]
+    outs = [weight, weight, weight, (2, 4, 4, 32, 384), (4, 4, 16, 128), (4, 4, 16, 128), rows, rows]
     scratch = [
         ((1024, 1536), bf16), ((1024, 768), bf16), ((1024, 768), bf16), ((1024, 768), bf16), ((1032, 768), f32),
         ((1032, 256), f32), ((1024, 256), bf16), ((1024, 128), bf16), ((1024, 128), f32),
@@ -743,22 +831,23 @@
         ((8, 128), f32), ((128, 768), bf16), ((8, 1536), f32),
         ((1536, 768), bf16), ((1536, 768), bf16), ((1536, 256), bf16), ((128, 1536), bf16), ((3, 256, 1536), bf16),
         (rows, bf16), ((8, 8, 128), f32), ((4, 8, 8, 128), f32),
-    ] + [(shape, bf16) for shape in outs[:6]]
+    ] + [(shape, bf16) for shape in outs[:7]]
     vmem, hbm, smem = [pl.BlockSpec(memory_space=space) for space in (pltpu.VMEM, pl.ANY, pltpu.SMEM)]
-    count = 9 * DP_SEMS + 3 * TENSOR_SEMS + 3
+    count = 8 * DP_SEMS + STATE_SEMS + 3 * TENSOR_SEMS + 3
     return pl.pallas_call(
         functools.partial(layer_kernel, remote),
         out_shape=[jax.ShapeDtypeStruct(shape, bf16) for shape in outs],
         in_specs=[hbm] * 6 + [vmem] * 8 + [smem] * 3,
-        out_specs=[hbm] * 7,
+        out_specs=[hbm] * 8,
         scratch_shapes=[pltpu.VMEM(shape, kind) for shape, kind in scratch]
         + dp_scratch(96, 384) * 4
-        + dp_scratch(32, 384, 32) * 2
-        + dp_scratch(64, 128, 32)
+        + dp_scratch(16, 128)
+        + dp_scratch(16, 128, 16, True)
+        + state_scratch(32, 384)
         + [pltpu.VMEM((2, 4, 96, 384), bf16)] * 2
         + [pltpu.VMEM((96, 384), bf16)] * 2
         + [pltpu.VMEM((2, 256, 1536), bf16), pltpu.VMEM((256, 1536), bf16)]
-        + [pltpu.SemaphoreType.DMA((count,)), pltpu.SemaphoreType.DMA((count,)), pltpu.SemaphoreType.DMA((7,))],
+        + [pltpu.SemaphoreType.DMA((count,)), pltpu.SemaphoreType.DMA((count,)), pltpu.SemaphoreType.DMA((8,))],
         compiler_params=pltpu.CompilerParams(
             collective_id=0 if remote else None, has_side_effects=True, vmem_limit_bytes=63 * 2**20
         ),
@@ -767,91 +856,99 @@
 
 
 def finish_kernel(
-    tokens, cot, norm_gain, sum_gate, sum_out, sum_value, sum_state, small, branch, dx,
-    mixed, grad_tokens, gate, value, out, state, step, value_taps, value_bias, state_taps, state_bias, step_bias, log_rate,
-    bypass, gain, mixer_gain,
+    tokens_in, cot_in, norm_gain, gate_in, out_in, value_in, state_in, small, shared, branch_in, dx_in,
+    mixed_out, tokens_out, gate_out, value_out, out_out, state_out, step, value_taps, value_bias, state_taps, state_bias, step_bias,
+    log_rate, bypass, gain, mixer_gain,
+    tokens, cot, branch, dx, sum_gate, sum_out, sum_value, sum_state, mixed, grad_tokens, gate, value, out, state, arrive, leave,
 ):
-    hidden = tokens[...].astype(jnp.float32)
-    inverse = lax.rsqrt(jnp.sum(hidden * hidden, 1, keepdims=True) / 1536 + EPS)
-    mixed[...] = low(hidden + branch[...].astype(jnp.float32))
-    scaled = dx[...].astype(jnp.float32) * norm_gain[...].reshape(1, 1536)
-    along = jnp.sum(scaled * hidden, 1, keepdims=True) * (inverse * inverse * inverse / 1536)
-    grad_tokens[...] = cot[...].astype(jnp.float32) + inverse * scaled - hidden * along
-    for stream in range(2):
-        columns = slice(stream * 384, (stream + 1) * 384)
-        for j in range(2):
-            rows = slice(j * 96, (j + 1) * 96)
-            for result, summed in ((gate, sum_gate), (out, sum_out), (value, sum_value)):
-                result[rows, columns] = summed[stream, 0, j].astype(jnp.float32)
-    for j in range(2):
-        rows = slice(j * 32, (j + 1) * 32)
-        first, second = [sum_state[stream, 0, j].astype(jnp.float32) for stream in range(2)]
+    quarters = [pl.ds(n * 256, 256) for n in range(4)]
+    loads = []
+    for n, (src, dst) in enumerate(((gate_in, sum_gate), (value_in, sum_value), (out_in, sum_out), (state_in, sum_state))):
+        loads.append([pltpu.make_async_copy(src, dst, arrive.at[n])])
+    for n, rows in enumerate(quarters):
+        loads.append(
+            [
+                pltpu.make_async_copy(src.at[rows], dst.at[rows], arrive.at[4 + 4 * n + m])
+                for m, (src, dst) in enumerate(((tokens_in, tokens), (dx_in, dx), (cot_in, cot), (branch_in, branch)))
+            ]
+        )
+    for group in loads:
+        for cp in group:
+            cp.start()
+    stores = []
+
+    def store(src, dst):
+        stores.append(pltpu.make_async_copy(src, dst, leave.at[len(stores)]))
+        stores[-1].start()
+
+    for n, (summed, result, home) in enumerate(
+        ((sum_gate, gate, gate_out), (sum_value, value, value_out), (sum_out, out, out_out))
+    ):
+        loads[n][0].wait()
+        for i in range(4):
+            for stream in range(2):
+                if n < 2:
+                    rows, columns = pl.ds(i * 384, 384), pl.ds(stream * 384, 384)
+                else:
+                    rows, columns = pl.ds(i % 2 * 384, 384), pl.ds(i // 2 * 768 + stream * 384, 384)
+                result[rows, columns] = summed[stream, i].astype(jnp.float32).reshape(384, 384)
+            if n < 2:
+                store(result.at[rows], home.at[rows])
+            elif i > 1:
+                store(result.at[rows], home.at[rows])
+    blocks = [small[j // 4, j % 4].astype(jnp.float32) for j in range(12)]
+    step[...] = jnp.concatenate([block[0:12] for block in blocks], 1)
+    rows = [block[n : n + 1] for block in blocks for n in range(12, 16)]
+    channels = [jnp.concatenate(rows[6 * n : 6 * n + 6], 1) for n in range(7)]
+    value_taps[...] = jnp.concatenate(channels[0:4], 0)
+    value_bias[...] = channels[4].reshape(768)
+    mixer_gain[...] = channels[5].reshape(768)
+    bypass[...] = mul_nt(low(jnp.broadcast_to(channels[6], (16, 768))), expansion())[0:1, 0:12].reshape(12)
+    step_bias[...] = rows[42][:, 0:12].reshape(12)
+    log_rate[...] = rows[43][:, 0:12].reshape(12)
+    gains, convs = [shared[0, j].astype(jnp.float32) for j in range(2)]
+    gain[...] = jnp.concatenate([gains[n : n + 1] for n in range(12)], 1).reshape(1536)
+    taps = [jnp.concatenate([convs[2 * n : 2 * n + 1], convs[2 * n + 1 : 2 * n + 2]], 1) for n in range(5)]
+    state_taps[...] = jnp.concatenate(taps[0:4], 0)
+    state_bias[...] = taps[4].reshape(256)
+    loads[3][0].wait()
+    for i in range(4):
+        rows = pl.ds(i * 128, 128)
+        first, second = [sum_state[stream, i].astype(jnp.float32).reshape(128, 384) for stream in range(2)]
         state[0, rows, :] = first[:, 0:256]
         state[1, rows, 0:128] = first[:, 256:384]
         state[1, rows, 128:256] = second[:, 0:128]
         state[2, rows, :] = second[:, 128:384]
-
-    @pl.when(pl.program_id(0) == 0)
-    def _():
-        def block(j, across):
-            return small[small_block(j, across)].astype(jnp.float32)
-
-        step[...] = jnp.concatenate([block(j, 0) for j in range(12)], 1)[0:12, :]
-        channels = jnp.concatenate([block(12 + j, 0) for j in range(6)], 1)
-        value_taps[...] = channels[0:4]
-        value_bias[...] = channels[4:5].reshape(768)
-        mixer_gain[...] = channels[5:6].reshape(768)
-        bypass[...] = mul_nt(low(channels), expansion())[6:7, 0:12].reshape(12)
-        per_head = block(18, 0)
-        step_bias[...] = per_head[0:1, 0:12].reshape(12)
-        log_rate[...] = per_head[1:2, 0:12].reshape(12)
-        states_small = jnp.concatenate([block(j, 1) for j in range(2)], 1)
-        state_taps[...] = states_small[0:4]
-        state_bias[...] = states_small[4:5].reshape(256)
-        gains = block(2, 1)
-        gain[...] = jnp.concatenate([gains[j : j + 1, :] for j in range(12)], 1).reshape(1536)
+    store(state, state_out)
+    for n, rows in enumerate(quarters):
+        for cp in loads[4 + n]:
+            cp.wait()
+        hidden = tokens[rows, :].astype(jnp.float32)
+        inverse = lax.rsqrt(jnp.sum(hidden * hidden, 1, keepdims=True) / 1536 + EPS)
+        mixed[rows, :] = low(hidden + branch[rows, :].astype(jnp.float32))
+        store(mixed.at[rows], mixed_out.at[rows])
+        scaled = dx[rows, :].astype(jnp.float32) * norm_gain[...].reshape(1, 1536)
+        along = jnp.sum(scaled * hidden, 1, keepdims=True) * (inverse * inverse * inverse / 1536)
+        grad_tokens[rows, :] = cot[rows, :].astype(jnp.float32) + inverse * scaled - hidden * along
+        store(grad_tokens.at[rows], tokens_out.at[rows])
+    for cp in stores:
+        cp.wait()
 
 
 def finished(tokens, cot, norm_gain, *sums):
-    f32 = jnp.float32
-    by_rows = pl.BlockSpec((128, 1536), lambda g: (g, 0))
-    weight = pl.BlockSpec((192, 768), lambda g: (g, 0))
-
-    def whole(*shape):
-        return pl.BlockSpec(shape, lambda g: (0,) * len(shape))
-
-    rest = [(12, 1536), (4, 768), (768,), (4, 256), (256,), (12,), (12,), (12,), (1536,), (768,)]
+    f32, bf16 = jnp.float32, jnp.bfloat16
+    large = [((1024, 1536), bf16), ((1024, 1536), f32), ((1536, 768), f32), ((1536, 768), f32), ((768, 1536), f32), ((3, 512, 256), f32)]
+    rest = [((12, 1536), f32), ((4, 768), f32), ((768,), f32), ((4, 256), f32), ((256,), f32)] + [((12,), f32)] * 3
+    rest += [((1536,), f32), ((768,), f32)]
+    scratch = [((1024, 1536), bf16)] * 4 + [((2, 4, 4, 96, 384), bf16)] * 3 + [((2, 4, 4, 32, 384), bf16)] + large
+    vmem, hbm = pl.BlockSpec(memory_space=pltpu.VMEM), pl.BlockSpec(memory_space=pl.ANY)
     return pl.pallas_call(
         finish_kernel,
-        grid=(8,),
-        out_shape=[
-            jax.ShapeDtypeStruct((1024, 1536), jnp.bfloat16),
-            jax.ShapeDtypeStruct((1024, 1536), f32),
-            jax.ShapeDtypeStruct((1536, 768), f32),
-            jax.ShapeDtypeStruct((1536, 768), f32),
-            jax.ShapeDtypeStruct((768, 1536), f32),
-            jax.ShapeDtypeStruct((3, 512, 256), f32),
-        ]
-        + [jax.ShapeDtypeStruct(shape, f32) for shape in rest],
-        in_specs=[
-            by_rows,
-            by_rows,
-            whole(1536),
-            *[pl.BlockSpec((2, 1, 2, 96, 384), lambda g: (0, g // 2, g % 2, 0, 0))] * 3,
-            pl.BlockSpec((2, 1, 2, 32, 384), lambda g: (0, g // 2, g % 2, 0, 0)),
-            whole(4, 4, 64, 128),
-            by_rows,
-            by_rows,
-        ],
-        out_specs=[
-            by_rows,
-            by_rows,
-            weight,
-            weight,
-            pl.BlockSpec((192, 768), lambda g: ((g // 2) % 2 * 2 + g % 2, g // 4)),
-            pl.BlockSpec((3, 64, 256), lambda g: (0, g, 0)),
-        ]
-        + [whole(*shape) for shape in rest],
+        out_shape=[jax.ShapeDtypeStruct(shape, kind) for shape, kind in large + rest],
+        in_specs=[hbm, hbm, vmem, hbm, hbm, hbm, hbm, vmem, vmem, hbm, hbm],
+        out_specs=[hbm] * len(large) + [vmem] * len(rest),
+        scratch_shapes=[pltpu.VMEM(shape, kind) for shape, kind in scratch]
+        + [pltpu.SemaphoreType.DMA((20,)), pltpu.SemaphoreType.DMA((19,))],
         compiler_params=pltpu.CompilerParams(vmem_limit_bytes=60 * 2**20),
         name="finish",
     )(tokens, cot, norm_gain, *sums)

time: 188 us -> 176 us (0.936)
  Pallas kernels: 187 us -> 175 us
    pallas_call x1, Pallas kernels: 168 us -> 157 us  [layer(): pl.pallas_call(functools.partial(layer_kernel, remote), out_shape=[jax.Sh...]
where the time goes in v4:
time: 176 us; the launch traced here: 175 us
  Pallas kernels  175 us (99%)
    pallas_call x1, Pallas kernels, layer(): pl.pallas_call(functools.partial(layer_kernel, remote), out_shape=[jax.Sh...  157 us
    pallas_call x1, Pallas kernels, finished(): pl.pallas_call(finish_kernel, out_shape=[jax.ShapeDtypeStruct(shape, kind...  17.9 us

profile of v4, /device:TPU:0, one launch (start us, length us, event | category | flops | bytes accessed | tf_op | source)
XLA Modules:
  0.0 175.3 jit_solution(11475727489335141012)
XLA Ops:
  0.7 156.6 %layer.1 = (bf16[2,4,4,96,384]{4,3,2,1,0:T(8,128)(2,1)}, bf16[2,4,4,96,384]{4,3,2,1,0:T(8,128)(2,1)}, bf16[2,4,4,96,384]{4,3,2,1,0:T(8,128)(2,1)}, bf16[2,4,4,32...) custom-call(bf16[1024,1536]{1,0:T(8,128)(2,1)} %tokens_in.1, ...), custom_call_target="tpu_custom_call" | custom-call | tf_op jit(solution)/shard_map/layer/pallas_call | solution.py:837
  157.2 17.9 %finish.1 = (bf16[1024,1536]{1,0:T(8,128)(2,1)}, f32[1024,1536]{1,0:T(8,128)}, f32[1536,768]{1,0:T(8,128)}, f32[1536,768]{1,0:T(8,128)}, f32[768,1536]{1,0:T(8,1...) custom-call(bf16[1024,1536]{1,0:T(8,128)(2,1)} %tokens_in.1, ...), custom_call_target="tpu_custom_call" | custom-call | tf_op jit(solution)/shard_map/finish/pallas_call | solution.py:945

commit v5 on v4

--- a/solution.py
+++ b/solution.py
@@ -155,32 +155,33 @@
 class SumOverTensor(Staged):
     counts = (1, 1, 2, 1)
 
-    def __init__(self, at, columns, buf, res, scratch, sems):
+    def __init__(self, at, rows, buf, res, scratch, sems, ending):
         super().__init__(*sems)
-        self.buf, self.res, self.columns = buf, res, columns
+        self.buf, self.res, self.rows, self.ending = buf, res, rows, ending
         self.t0, self.t1 = scratch
         self.c, self.h = at["t"] % 2, at["t"] // 2
         self.sibling = device_at(at, t=self.h * 2 + 1 - self.c)
         self.partner = device_at(at, t=(1 - self.h) * 2 + self.c)
 
     def copies(self, stage):
-        buf, res, c, h, columns = self.buf, self.res, self.c, self.h, self.columns
+        buf, res, c, h, rows = self.buf, self.res, self.c, self.h, self.rows
         if stage == 0:
-            return [(buf.at[1 - c, :, :, columns], self.t0.at[:, :, columns], self.sibling)]
+            return [(buf.at[1 - c, :, rows], self.t0.at[:, rows], self.sibling)]
         if stage == 1:
-            return [(buf.at[c, 1 - h, :, columns], self.t1.at[:, columns], self.partner)]
+            return [(buf.at[c, 1 - h, rows], self.t1.at[rows], self.partner)]
         if stage == 2:
-            mine, theirs = buf.at[c, h, :, columns], res.at[c, h, :, columns]
+            mine, theirs = buf.at[c, h, rows], res.at[c, h, rows]
             return [(mine, theirs, self.partner), (mine, theirs, None)]
-        return [(res.at[c, :, :, columns], res.at[c, :, :, columns], self.sibling)]
+        return [(res.at[c, :, rows], res.at[c, :, rows], self.sibling)]
 
     def settle(self, stage):
-        buf, c, h, columns = self.buf, self.c, self.h, self.columns
+        buf, c, h, rows = self.buf, self.c, self.h, self.rows
         if stage == 0:
             for n in range(2):
-                buf[c, n, :, columns] = added(buf.at[c, n, :, columns], self.t0.at[n, :, columns])
+                buf[c, n, rows] = added(buf.at[c, n, rows], self.t0.at[n, rows])
         elif stage == 1:
-            buf[c, h, :, columns] = added(buf.at[c, h, :, columns], self.t1.at[:, columns])
+            total = buf[c, h, rows].astype(jnp.float32) + self.t1[rows].astype(jnp.float32)
+            buf[c, h, rows] = self.ending(total, rows)
 
 
 TENSOR_SEMS = sum(SumOverTensor.counts)
@@ -344,29 +345,27 @@
 
 
 def head_sums(value, expand):
-    high = low(value)
-    return mul_nt(high, expand) + mul_nt(low(value - high.astype(jnp.float32)), expand)
+    return mul_nt(low(value), expand)
 
 
 def slope(pre, sig):
     return sig * (1.0 + pre * (1.0 - sig))
 
 
-def middle_block(k, total, gated_gain, gate, y_ref, q_ref, acc_v):
+def middle_block(k, total, kept_act, bent, gated_ref, pulled, acc_v):
     rows = pl.ds(pl.multiple_of(k * 128, 128), 128)
     columns = jnp.concatenate([total] * 16, 0).T
     scale = lax.rsqrt(columns[:, 0:1] / 3072 + EPS)
     pull = columns[:, 1:2] * scale * scale * scale / 3072
-    raw, y, q = [ref[rows, :].astype(jnp.float32) for ref in (gate, y_ref, q_ref)]
-    sig = sigmoid(raw)
-    act = raw * sig
-    gated = y * act
+    gated, q, act, bend = [
+        value.astype(jnp.float32) for value in (gated_ref[rows, :], pulled[rows, :], kept_act[...], bent[rows, :])
+    ]
     scaled = gated * scale
-    y_ref[rows, :] = low(scaled * gated_gain)
     acc_v[5:6, :] += jnp.sum(q * scaled, 0, keepdims=True)
-    grad_gated = scale * (q * gated_gain) - gated * pull
-    q_ref[rows, :] = low(grad_gated * act)
-    gate[rows, :] = low(grad_gated * y * slope(raw, sig))
+    grad_gated = scale * q - gated * pull
+    pulled[rows, :] = low(grad_gated * act)
+    bent[rows, :] = low(grad_gated * bend)
+    return rows, scaled
 
 
 def put(buf, i, value):
@@ -416,43 +415,47 @@
     cum_rows = cum.T
     first = column < 64
     grad_scores = jnp.zeros((128, 128), jnp.float32)
+    own_steps = jnp.zeros((128, 128), jnp.float32)
     inside = []
+    between(1)
     for pair in range(6):
-        if pair == 3:
-            between()
         lanes = slice(pair * 128, (pair + 1) * 128)
         own = dyk[:, lanes]
         both = low(jnp.concatenate([jnp.where(first, own, 0.0), jnp.where(first, 0.0, own)], 0))
-        grad_weights = mul_nt(low(xs[:, lanes]), both)
-        weights, moved = [], []
+        grad_weights = mul_nt(low(x[:, lanes]), both)
+        weights, moved, steps = [], [], []
         for side in range(2):
             h = 2 * pair + side
             faded = jnp.exp(cum_rows[h : h + 1, :] - cum[:, h : h + 1] + bias)
             pulled = grad_weights[:, side * 128 : (side + 1) * 128] * faded
-            grad_scores = grad_scores + pulled
+            steps.append(step[:, h : h + 1])
+            grad_scores = grad_scores + pulled * steps[side]
             moved.append(low(pulled * scores))
             weights.append(low(scores * faded))
         inside.append(mul(jnp.concatenate(weights, 1), both))
         later = mul(jnp.concatenate(moved, 0), tri)
         for side in range(2):
             h = 2 * pair + side
-            part = jnp.where(strict, later[side * 128 : (side + 1) * 128], 0.0)
-            head_rows[h : h + 1, :] = jnp.sum(part, 0, keepdims=True)
+            part = later[side * 128 : (side + 1) * 128]
+            own_steps = jnp.where(column == h, part[:, 0:1], own_steps)
+            head_rows[h : h + 1, :] = jnp.sum(jnp.where(strict, part * steps[side], 0.0), 0, keepdims=True)
+    between(2)
     grad_scores = low(grad_scores)
     grad_b = grad_b + mul(grad_scores, c_out)
     grad_c = grad_c + mul_tn(grad_scores, b_in)
     dxs = jnp.concatenate(inside, 1) + dxs_after
     dx = dxs * step_wide + bypass * dyk
-    summed = head_sums(jnp.concatenate([dxs * x, dyk * outside, xs * dxs_after], 0), expand[...])
+    summed = head_sums(jnp.concatenate([dyk * outside, x * dxs_after], 0), expand[...])
     end = head_sums(jnp.broadcast_to(end, (16, 768)), expand[...])
     upper = (row <= column).astype(jnp.bfloat16)
     below = (row > column).astype(jnp.bfloat16)
-    grad_decay = exact_sum(upper, summed[128:256]) + exact_sum(below, summed[256:]) + end[0:1, :] + head_rows[...].T
-    grad_step = summed[:128] + heads[1:2, :] * grad_decay
+    grad_decay = exact_sum(upper, summed[:128]) + exact_sum(below, step * summed[128:]) + end[0:1, :] + head_rows[...].T
+    grad_step = own_steps + summed[128:] + heads[1:2, :] * grad_decay
     grad_raw = grad_step * sigmoid(step_raw[rows, :] + heads[0:1, :])
     step_low[rows, :] = low(jnp.where(column < 16, grad_raw, 0.0))
     acc_h[0:1, :] += jnp.sum(grad_raw, 0, keepdims=True)
     acc_h[1:2, :] += jnp.sum(step * grad_decay, 0, keepdims=True) * heads[1:2, :]
+    between(3)
     for grad, grads, shifted, taps_ref, acc, result in (
         (dx * slope(pre, sig), du, values, taps, acc_v, value_low),
         (jnp.concatenate([grad_b, grad_c], 1) * slope(state_pre, state_sig), dus, state_values, state_taps, acc_s, state_low),
@@ -497,13 +500,16 @@
         shared[0, j] = low(block)
 
 
+BRANCH_PLANS = {}
+OUT_PLANS = {3: ("g0>",)}
+VALUE_PLANS = {}
+STATE_PLANS = {3: ("o1>",)}
 SCAN_PLANS = (
     {4: ("g2>",), 6: ("o0>", "b1>"), 7: ("g4>",)},
+    {},
     {0: ("b0>",), 2: ("g1>",), 4: ("o0",), 5: ("g3>",)},
+    {},
 )
-AFTER_SCAN = ()
-VALUE_PLANS = {}
-AFTER_STATE = ("o1>",)
 DX_PLANS = ({3: ("g5>", "b2>")}, {0: ("v0>",), 1: ("o2>",), 3: ("d0>", "g6.", "o3>", "b3.")})
 TAIL = (
     "v1>", "e0>", "s0>", "o4>", "d1>", "v2>", "s1>", "s2>", "o5>", "v3>", "s3>", "e1>",
@@ -536,7 +542,7 @@
         for early, own_ta2, own_ty in zip(scratch[0:2], rest[42:44], rest[44:46])
     ]
     branch_scratch = rest[46:48]
-    send, recv, local = rest[48:]
+    own_tokens, own_cot, send, recv, local = rest[48:]
     at = place()
     dx = cot
     slots = branch.at[0]
@@ -547,7 +553,15 @@
     loads = [
         pltpu.make_async_copy(src, dst, local.at[2 + n])
         for n, (src, dst) in enumerate(
-            ((w_gate_in, w_gate), (w_value_in, w_value), (w_state_in, w_state), (cot_in, cot), (w_out_in, w_out))
+            (
+                (w_gate_in, w_gate),
+                (w_value_in, w_value),
+                (w_state_in, w_state),
+                (cot_in, cot),
+                (w_out_in, w_out),
+                (tokens.at[pl.ds(pl.multiple_of((at["t"] % 2 * 2 + at["t"] // 2) * 256, 256), 256)], own_tokens),
+                (cot_in.at[at["t"] % 2, at["t"] // 2], own_cot),
+            )
         )
     ]
     fetch(0).start()
@@ -567,7 +581,21 @@
 
     last = 8 * DP_SEMS + STATE_SEMS
     dx_scratch = (w_out.at[pl.ds(0, 2)], w_out.at[2])
-    left, right, both_sides = pl.ds(0, 768), pl.ds(768, 768), pl.ds(0, 1536)
+    upper, lower, all_rows = pl.ds(0, 128), pl.ds(128, 128), pl.ds(0, 256)
+
+    def mixed_rows(total, rows):
+        return low(own_tokens[rows].astype(jnp.float32) + total)
+
+    def token_gradient(total, rows):
+        hidden = own_tokens[rows].astype(jnp.float32)
+        inverse = lax.rsqrt(jnp.sum(hidden * hidden, 1, keepdims=True) / 1536 + EPS)
+        scaled = total * gains[0:1, :]
+        along = jnp.sum(scaled * hidden, 1, keepdims=True) * (inverse * inverse * inverse / 1536)
+        return low(own_cot[rows].astype(jnp.float32) + inverse * scaled - hidden * along)
+
+    def over_tensor(n, rows, buf, res, scratch, ending):
+        return [(SumOverTensor(at, rows, buf, res, scratch, (send, recv, last + n * TENSOR_SEMS), ending), range(4))]
+
     engines = {
         "g": pair(0, sum_gate, res_gate, scratch[0:2]),
         "o": pair(2, sum_out, res_out, scratch[2:4]),
@@ -580,9 +608,9 @@
                 (None, 0, 2, 3, 4, 5, 6, None),
             ),
         ],
-        "b": [(SumOverTensor(at, both_sides, branch, res_branch, branch_scratch, (send, recv, last)), range(4))],
-        "d": [(SumOverTensor(at, left, dx, res_dx, dx_scratch, (send, recv, last + TENSOR_SEMS)), range(4))],
-        "e": [(SumOverTensor(at, right, dx, res_dx, dx_scratch, (send, recv, last + 2 * TENSOR_SEMS)), range(4))],
+        "b": over_tensor(0, all_rows, branch, res_branch, branch_scratch, mixed_rows),
+        "d": over_tensor(1, upper, dx, res_dx, dx_scratch, token_gradient),
+        "e": over_tensor(2, lower, dx, res_dx, dx_scratch, token_gradient),
     }
 
     def act(*plan):
@@ -656,10 +684,14 @@
 
     def project_back(k, carry):
         rows = pl.ds(pl.multiple_of(k * 256, 256), 256)
-        q_ref[rows, :] = low(mul_nt(cot[k // 2, k % 2], w_out[...].reshape(768, 1536)))
+        q_ref[rows, :] = low(mul_nt(cot[k // 2, k % 2], w_out[...].reshape(768, 1536)) * gains[1:2, 0:768])
         return carry
 
     lax.fori_loop(0, 4, project_back, 0)
+
+    def act_of(k):
+        rows, columns = pl.ds(k // 2 % 2 * 128, 128), pl.ds(pl.multiple_of(k % 2 * 768, 128), 768)
+        return branch.at[1, k // 4, rows, columns]
 
     def forward_block(k, carry):
         start = pl.multiple_of(k * 128, 128)
@@ -692,46 +724,60 @@
             ]
             inside.append(mul(jnp.concatenate(left, 1), right))
         y = jnp.concatenate(inside, 1) + outside + gains[2:3, 0:768] * x
-        y_ref[rows, :] = low(y)
         raw = gate[rows, :].astype(jnp.float32)
-        gated = y * (raw * sigmoid(raw))
+        sig = sigmoid(raw)
+        act = raw * sig
+        gated = y * act
+        y_ref[rows, :] = low(gated)
+        gate[rows, :] = low(y * slope(raw, sig))
+        act_of(k)[...] = low(act)
         squares = jnp.sum(gated * gated, 1, keepdims=True)
-        cross = jnp.sum(q_ref[rows, :].astype(jnp.float32) * gains[1:2, 0:768] * gated, 1, keepdims=True)
+        cross = jnp.sum(q_ref[rows, :].astype(jnp.float32) * gated, 1, keepdims=True)
         lanes = iota((128, 128), 1)
         sums[k] = jnp.where(lanes == 0, squares, jnp.where(lanes == 1, cross, 0.0)).T[0:8, :]
         return carry
 
-    lax.fori_loop(0, 8, forward_block, 0)
-
-    if remote:
-        pl.semaphore_wait(pltpu.get_barrier_semaphore(), len(friends))
-        peers = tensor_peers(at)
-        exchange = [
+    def exchange(half):
+        blocks, first = pl.ds(4 * half, 4), last + 3 * TENSOR_SEMS + 3 * half
+        copies = [
             pltpu.make_async_remote_copy(
-                src_ref=sums,
-                dst_ref=landed.at[at["t"]],
-                send_sem=send.at[last + 3 * TENSOR_SEMS + n],
-                recv_sem=recv.at[last + 3 * TENSOR_SEMS + n],
+                src_ref=sums.at[blocks],
+                dst_ref=landed.at[at["t"], blocks],
+                send_sem=send.at[first + n],
+                recv_sem=recv.at[first + n],
                 device_id=peer,
                 device_id_type=MESH_ID,
             )
-            for n, peer in enumerate(peers)
+            for n, peer in enumerate(tensor_peers(at))
         ]
-        for cp in exchange:
+        if not remote:
+            for n in range(4):
+                landed[n, blocks] = sums[blocks] * 0.75
+            return []
+        for cp in copies:
             cp.start()
-        landed[at["t"]] = sums[...]
-        for cp in exchange:
-            cp.wait()
-    else:
-        for n in range(4):
-            landed[n] = sums[...] * 0.75
+        landed[at["t"], blocks] = sums[blocks]
+        return copies
 
     def middle(k, carry):
         total = (landed[0, k] + landed[1, k]) + (landed[2, k] + landed[3, k])
-        middle_block(k, total, gains[1:2, 0:768], gate, y_ref, q_ref, acc_v)
+        rows, scaled = middle_block(k, total, act_of(k), gate, y_ref, q_ref, acc_v)
+        y_ref[rows, :] = low(scaled * gains[1:2, 0:768])
         return carry
 
-    lax.fori_loop(0, 8, middle, 0)
+    lax.fori_loop(0, 4, forward_block, 0)
+    if remote:
+        pl.semaphore_wait(pltpu.get_barrier_semaphore(), len(friends))
+    first_sums = exchange(0)
+    lax.fori_loop(4, 8, forward_block, 0)
+    second_sums = exchange(1)
+    for cp in first_sums:
+        cp.wait()
+    lax.fori_loop(0, 4, middle, 0)
+    for cp in second_sums:
+        cp.wait()
+    lax.fori_loop(4, 8, middle, 0)
+    acc_v[5:6, :] = acc_v[5:6, :] / gains[1:2, 0:768]
     gate_low, gate_normed, dy = gate, y_ref, q_ref
     value_low = y_ref
 
@@ -743,11 +789,13 @@
         out_rows = pl.ds(pl.multiple_of((i % 2) * 384, 128), 384)
         out_columns = pl.ds(pl.multiple_of((i // 2) * 768, 128), 768)
         put(sum_out, i, mul_tn(gate_normed[:, out_rows], cot[:, :, :, out_columns].reshape(1024, 768)))
+        act_at(i, OUT_PLANS)
         return carry
 
     def branch_rows(i, carry):
         rows = pl.ds(pl.multiple_of(i * 256, 256), 256)
         branch[i // 2, i % 2] = low(mul(gate_normed[rows, :], w_out[...].reshape(768, 1536)))
+        act_at(i, BRANCH_PLANS)
         return carry
 
     lax.fori_loop(0, 4, gate_weights, 0)
@@ -755,7 +803,6 @@
     lax.fori_loop(0, 4, branch_rows, 0)
     act("b0")
     lax.fori_loop(0, 4, out_weights, 0)
-    act("g0>")
     carried[...] = jnp.zeros((128, 768), jnp.float32)
 
     def scan(i, carry):
@@ -763,12 +810,11 @@
         backward_block(
             7 - i, vpad, spad, step_raw, seg, segc, taps, state_taps, heads, expand, gains[2:3, 0:768], states, dy,
             carried, du, dus, head_rows, value_low, state_low, step_low, acc_v, acc_s, acc_h,
-            lambda: act_at(i, SCAN_PLANS[1]),
+            lambda point: act_at(i, SCAN_PLANS[point]),
         )
         return carry
 
     lax.fori_loop(0, 8, scan, 0)
-    act(*AFTER_SCAN)
 
     def value_weights(i, carry):
         put(sum_value, i, mul_tn(normed[:, pl.ds(pl.multiple_of(i * 384, 128), 384)], value_low[...]))
@@ -780,21 +826,26 @@
             mul_tn(normed[:, pl.ds(pl.multiple_of(q * 512 + i * 128, 128), 128)], state_low[...]) for q in range(3)
         ]
         put(sum_state, i, jnp.concatenate(thirds, 1))
+        act_at(i, STATE_PLANS)
         return carry
 
     lax.fori_loop(0, 4, value_weights, 0)
     put_small(small, acc_v, acc_h, mul_tn(step_low[...], normed[...])[0:16, :])
     act("v0")
     lax.fori_loop(0, 4, state_weights, 0)
-    act(*AFTER_STATE)
 
     def dx_rows(half, i):
-        rows = pl.ds(pl.multiple_of(i * 256, 256), 256)
-        columns = slice(half * 768, half * 768 + 768)
-        part = mul_nt(gate_low[rows, :], w_gate[columns, :]) + mul_nt(value_low[rows, :], w_value[columns, :])
-        part = part + mul_nt(state_low[rows, :], w_state[columns, :]) + mul(step_low[rows, :], w_step[:, columns])
-        dx[i // 2, i % 2, :, columns] = low(part)
-        acc_n[0:1, columns] += jnp.sum(part * normed[rows, columns].astype(jnp.float32), 0, keepdims=True)
+        firsts = [pl.ds(pl.multiple_of((i // 2 * 2 + n) * 256 + half * 128, 128), 128) for n in range(2)]
+        columns = pl.ds(pl.multiple_of(i % 2 * 768, 128), 768)
+
+        def both(ref, *lanes):
+            return jnp.concatenate([ref[(rows, *lanes)] for rows in firsts], 0)
+
+        part = mul_nt(both(gate_low), w_gate[columns, :]) + mul_nt(both(value_low), w_value[columns, :])
+        part = part + mul_nt(both(state_low), w_state[columns, :]) + mul(both(step_low), w_step[:, columns])
+        for n in range(2):
+            dx[i // 2, n, half * 128 : half * 128 + 128, columns] = low(part[n * 128 : n * 128 + 128])
+        acc_n[0:1, columns] += jnp.sum(part * both(normed, columns).astype(jnp.float32), 0, keepdims=True)
         act_at(i, DX_PLANS[half])
 
     for half in range(2):
@@ -833,7 +884,7 @@
         (rows, bf16), ((8, 8, 128), f32), ((4, 8, 8, 128), f32),
     ] + [(shape, bf16) for shape in outs[:7]]
     vmem, hbm, smem = [pl.BlockSpec(memory_space=space) for space in (pltpu.VMEM, pl.ANY, pltpu.SMEM)]
-    count = 8 * DP_SEMS + STATE_SEMS + 3 * TENSOR_SEMS + 3
+    count = 8 * DP_SEMS + STATE_SEMS + 3 * TENSOR_SEMS + 6
     return pl.pallas_call(
         functools.partial(layer_kernel, remote),
         out_shape=[jax.ShapeDtypeStruct(shape, bf16) for shape in outs],
@@ -846,8 +897,8 @@
         + state_scratch(32, 384)
         + [pltpu.VMEM((2, 4, 96, 384), bf16)] * 2
         + [pltpu.VMEM((96, 384), bf16)] * 2
-        + [pltpu.VMEM((2, 256, 1536), bf16), pltpu.VMEM((256, 1536), bf16)]
-        + [pltpu.SemaphoreType.DMA((count,)), pltpu.SemaphoreType.DMA((count,)), pltpu.SemaphoreType.DMA((8,))],
+        + [pltpu.VMEM((2, 256, 1536), bf16)] + [pltpu.VMEM((256, 1536), bf16)] * 3
+        + [pltpu.SemaphoreType.DMA((count,)), pltpu.SemaphoreType.DMA((count,)), pltpu.SemaphoreType.DMA((9,))],
         compiler_params=pltpu.CompilerParams(
             collective_id=0 if remote else None, has_side_effects=True, vmem_limit_bytes=63 * 2**20
         ),
@@ -856,22 +907,16 @@
 
 
 def finish_kernel(
-    tokens_in, cot_in, norm_gain, gate_in, out_in, value_in, state_in, small, shared, branch_in, dx_in,
+    gate_in, out_in, value_in, state_in, small, shared, branch_in, dx_in,
     mixed_out, tokens_out, gate_out, value_out, out_out, state_out, step, value_taps, value_bias, state_taps, state_bias, step_bias,
     log_rate, bypass, gain, mixer_gain,
-    tokens, cot, branch, dx, sum_gate, sum_out, sum_value, sum_state, mixed, grad_tokens, gate, value, out, state, arrive, leave,
+    dx, sum_gate, sum_out, sum_value, sum_state, mixed, grad_tokens, gate, value, out, state, arrive, leave,
 ):
-    quarters = [pl.ds(n * 256, 256) for n in range(4)]
     loads = []
     for n, (src, dst) in enumerate(((gate_in, sum_gate), (value_in, sum_value), (out_in, sum_out), (state_in, sum_state))):
         loads.append([pltpu.make_async_copy(src, dst, arrive.at[n])])
-    for n, rows in enumerate(quarters):
-        loads.append(
-            [
-                pltpu.make_async_copy(src.at[rows], dst.at[rows], arrive.at[4 + 4 * n + m])
-                for m, (src, dst) in enumerate(((tokens_in, tokens), (dx_in, dx), (cot_in, cot), (branch_in, branch)))
-            ]
-        )
+    for n in range(4):
+        loads.append([pltpu.make_async_copy(dx_in.at[n], dx.at[n], arrive.at[4 + n])])
     for group in loads:
         for cp in group:
             cp.start()
@@ -881,6 +926,8 @@
         stores.append(pltpu.make_async_copy(src, dst, leave.at[len(stores)]))
         stores[-1].start()
 
+    mixed_load = pltpu.make_async_copy(branch_in, mixed, arrive.at[8])
+    mixed_load.start()
     for n, (summed, result, home) in enumerate(
         ((sum_gate, gate, gate_out), (sum_value, value, value_out), (sum_out, out, out_out))
     ):
@@ -920,38 +967,34 @@
         state[1, rows, 128:256] = second[:, 0:128]
         state[2, rows, :] = second[:, 128:384]
     store(state, state_out)
-    for n, rows in enumerate(quarters):
-        for cp in loads[4 + n]:
-            cp.wait()
-        hidden = tokens[rows, :].astype(jnp.float32)
-        inverse = lax.rsqrt(jnp.sum(hidden * hidden, 1, keepdims=True) / 1536 + EPS)
-        mixed[rows, :] = low(hidden + branch[rows, :].astype(jnp.float32))
-        store(mixed.at[rows], mixed_out.at[rows])
-        scaled = dx[rows, :].astype(jnp.float32) * norm_gain[...].reshape(1, 1536)
-        along = jnp.sum(scaled * hidden, 1, keepdims=True) * (inverse * inverse * inverse / 1536)
-        grad_tokens[rows, :] = cot[rows, :].astype(jnp.float32) + inverse * scaled - hidden * along
+    mixed_load.wait()
+    store(mixed, mixed_out)
+    for n in range(4):
+        loads[4 + n][0].wait()
+        rows = pl.ds(n * 256, 256)
+        grad_tokens[rows, :] = dx[n].astype(jnp.float32)
         store(grad_tokens.at[rows], tokens_out.at[rows])
     for cp in stores:
         cp.wait()
 
 
-def finished(tokens, cot, norm_gain, *sums):
+def finished(*sums):
     f32, bf16 = jnp.float32, jnp.bfloat16
     large = [((1024, 1536), bf16), ((1024, 1536), f32), ((1536, 768), f32), ((1536, 768), f32), ((768, 1536), f32), ((3, 512, 256), f32)]
     rest = [((12, 1536), f32), ((4, 768), f32), ((768,), f32), ((4, 256), f32), ((256,), f32)] + [((12,), f32)] * 3
     rest += [((1536,), f32), ((768,), f32)]
-    scratch = [((1024, 1536), bf16)] * 4 + [((2, 4, 4, 96, 384), bf16)] * 3 + [((2, 4, 4, 32, 384), bf16)] + large
+    scratch = [((4, 256, 1536), bf16)] + [((2, 4, 4, 96, 384), bf16)] * 3 + [((2, 4, 4, 32, 384), bf16)] + large
     vmem, hbm = pl.BlockSpec(memory_space=pltpu.VMEM), pl.BlockSpec(memory_space=pl.ANY)
     return pl.pallas_call(
         finish_kernel,
         out_shape=[jax.ShapeDtypeStruct(shape, kind) for shape, kind in large + rest],
-        in_specs=[hbm, hbm, vmem, hbm, hbm, hbm, hbm, vmem, vmem, hbm, hbm],
+        in_specs=[hbm, hbm, hbm, hbm, vmem, vmem, hbm, hbm],
         out_specs=[hbm] * len(large) + [vmem] * len(rest),
         scratch_shapes=[pltpu.VMEM(shape, kind) for shape, kind in scratch]
         + [pltpu.SemaphoreType.DMA((20,)), pltpu.SemaphoreType.DMA((19,))],
         compiler_params=pltpu.CompilerParams(vmem_limit_bytes=60 * 2**20),
         name="finish",
-    )(tokens, cot, norm_gain, *sums)
+    )(*sums)
 
 
 def local(
@@ -973,15 +1016,16 @@
     out_proj,
     cotangent,
 ):
-    *sums, branch, dx = layer(
+    sum_gate, sum_out, sum_value, sum_state, small, shared, branch, dx = layer(
         tokens, cotangent.reshape(2, 2, 256, 1536), gate_proj, value_proj, state_proj, out_proj.reshape(3, 256, 1536), segment, step_proj.T,
         value_conv, value_conv_bias, state_conv, state_conv_bias, norm_gain, gated_norm_gain, step_bias, log_rate, bypass_gain,
     )
-    rows = tokens.shape
     (
         mixed_out, grad_tokens, grad_gate, grad_value, grad_out, grad_state, grad_step, grad_value_conv, grad_value_bias,
         grad_state_conv, grad_state_bias, grad_step_bias, grad_log_rate, grad_bypass, grad_gain, grad_mixer_gain,
-    ) = finished(tokens, cotangent, norm_gain, *sums, branch.reshape(rows), dx.reshape(rows))
+    ) = finished(
+        sum_gate, sum_out, sum_value, sum_state, small, shared, branch.reshape(tokens.shape), dx.reshape(4, 256, 1536)
+    )
     return (
         mixed_out,
         grad_tokens,

time: 176 us -> 173 us (0.983)
  Pallas kernels: 175 us -> 171 us
    pallas_call x1, Pallas kernels: 17.9 us -> 16 us  [finished(): pl.pallas_call(finish_kernel, out_shape=[jax.ShapeDtypeStruct(shape, kind...]
where the time goes in v5:
time: 173 us; the launch traced here: 172 us
  Pallas kernels  171 us (99%)
    pallas_call x1, Pallas kernels, layer(): pl.pallas_call(functools.partial(layer_kernel, remote), out_shape=[jax.Sh...  155 us
    pallas_call x1, Pallas kernels, finished(): pl.pallas_call(finish_kernel, out_shape=[jax.ShapeDtypeStruct(shape, kind...  16 us

profile of v5, /device:TPU:0, one launch (start us, length us, event | category | flops | bytes accessed | tf_op | source)
XLA Modules:
  0.0 172.0 jit_solution(10434838769977016709)
XLA Ops:
  0.7 155.2 %layer.1 = (bf16[2,4,4,96,384]{4,3,2,1,0:T(8,128)(2,1)}, bf16[2,4,4,96,384]{4,3,2,1,0:T(8,128)(2,1)}, bf16[2,4,4,96,384]{4,3,2,1,0:T(8,128)(2,1)}, bf16[2,4,4,32...) custom-call(bf16[1024,1536]{1,0:T(8,128)(2,1)} %tokens.1, ...), custom_call_target="tpu_custom_call" | custom-call | tf_op jit(solution)/shard_map/layer/pallas_call | solution.py:888
  155.9 16.0 %finish.1 = (bf16[1024,1536]{1,0:T(8,128)(2,1)}, f32[1024,1536]{1,0:T(8,128)}, f32[1536,768]{1,0:T(8,128)}, f32[1536,768]{1,0:T(8,128)}, f32[768,1536]{1,0:T(8,1...) custom-call(bf16[2,4,4,96,384]{4,3,2,1,0:T(8,128)(2,1)} %get-tuple-e, ...), custom_call_target="tpu_custom_call" | custom-call | tf_op jit(solution)/shard_map/finish/pallas_call | solution.py:988

commit v6 on v5

--- a/solution.py
+++ b/solution.py
@@ -53,33 +53,35 @@
     def __init__(self, send, recv, first):
         self.send, self.recv, self.first = send, recv, first
 
-    def made(self, stage):
-        at = self.first + sum(self.counts[:stage])
-        for n, (src, dst, peer) in enumerate(self.copies(stage)):
+    def start(self, stage):
+        send, recv = self.send.at[self.first + stage], self.recv.at[self.first + stage]
+        for src, dst, peer in self.copies(stage):
             if peer is None:
-                yield pltpu.make_async_copy(src, dst, self.recv.at[at + n])
+                pltpu.make_async_copy(src, dst, recv).start()
             else:
-                yield pltpu.make_async_remote_copy(
-                    src_ref=src,
-                    dst_ref=dst,
-                    send_sem=self.send.at[at + n],
-                    recv_sem=self.recv.at[at + n],
-                    device_id=peer,
-                    device_id_type=MESH_ID,
-                )
-
-    def start(self, stage):
-        for cp in self.made(stage):
-            cp.start()
+                pltpu.make_async_remote_copy(
+                    src_ref=src, dst_ref=dst, send_sem=send, recv_sem=recv, device_id=peer, device_id_type=MESH_ID
+                ).start()
 
     def finish(self, stage):
-        for cp in self.made(stage):
-            cp.wait()
+        send, recv = self.send.at[self.first + stage], self.recv.at[self.first + stage]
+        arrived, sent = self.totals(stage)
+        peer = self.copies(stage)[0][2]
+        for ref in (sent, arrived):
+            copy = pltpu.make_async_remote_copy(
+                src_ref=ref, dst_ref=ref, send_sem=send, recv_sem=recv, device_id=peer, device_id_type=MESH_ID
+            )
+            if ref is sent:
+                copy.wait_send()
+            if ref is arrived:
+                copy.wait_recv()
+            if sent is arrived:
+                break
         self.settle(stage)
 
 
 class SumOverDp(Staged):
-    counts = (3, 2, 3, 1, 3, 4, 3, 2)
+    stages = 8
 
     def __init__(self, at, order, buf, res, scratch, sems, across=None, direct=False):
         super().__init__(*sems)
@@ -122,6 +124,20 @@
             (res.at[self.a_up, far], res.at[self.a_up, far], self.a_left),
         ]
 
+    def totals(self, stage):
+        res, a = self.res, self.a
+        if stage == 5:
+            return res.at[a], res.at[a, pl.ds(0, 3)]
+        if stage == 6:
+            both = res.at[pl.ds(0, 3 if self.direct else 2)]
+        elif stage == 7:
+            both = res.at[0]
+        elif stage == 4:
+            both = self.tt.at[pl.ds(0, 3)]
+        else:
+            both = (self.ta1, self.ta2, self.tb, self.ty)[stage]
+        return both, both
+
     def settle(self, stage):
         buf, a, b, own = self.buf, self.a, self.b, self.own
         if stage == 0 and self.direct:
@@ -143,7 +159,7 @@
             own[self.across] = added(*(self.tt.at[n] for n in range(4)))
 
 
-DP_SEMS = sum(SumOverDp.counts)
+DP_SEMS = SumOverDp.stages
 
 
 def dp_scratch(rows, width, across=16, direct=False):
@@ -153,7 +169,7 @@
 
 
 class SumOverTensor(Staged):
-    counts = (1, 1, 2, 1)
+    stages = 4
 
     def __init__(self, at, rows, buf, res, scratch, sems, ending):
         super().__init__(*sems)
@@ -174,6 +190,13 @@
             return [(mine, theirs, self.partner), (mine, theirs, None)]
         return [(res.at[c, :, rows], res.at[c, :, rows], self.sibling)]
 
+    def totals(self, stage):
+        res, c, h, rows = self.res, self.c, self.h, self.rows
+        if stage == 2:
+            return res.at[c, :, rows], res.at[c, h, rows]
+        both = (self.t0.at[:, rows], self.t1.at[rows], None, res.at[c, :, rows])[stage]
+        return both, both
+
     def settle(self, stage):
         buf, c, h, rows = self.buf, self.c, self.h, self.rows
         if stage == 0:
@@ -184,11 +207,11 @@
             buf[c, h, rows] = self.ending(total, rows)
 
 
-TENSOR_SEMS = sum(SumOverTensor.counts)
+TENSOR_SEMS = SumOverTensor.stages
 
 
 class SumState(Staged):
-    counts = (1, 3, 3, 1, 1, 4, 3, 1)
+    stages = 8
 
     def __init__(self, at, buf, res, scratch, sems):
         super().__init__(*sems)
@@ -221,6 +244,18 @@
             return [(res.at[c, a], res.at[c, a], peer) for peer in self.a_peers]
         return [(res.at[c], res.at[c], self.sibling)]
 
+    def totals(self, stage):
+        res, a, c = self.res, self.a, self.c
+        if stage == 5:
+            return res.at[c, a], res.at[c, a, pl.ds(0, 3)]
+        if stage == 6:
+            both = res.at[c, pl.ds(0, 3)]
+        elif stage == 7:
+            both = res.at[c]
+        else:
+            both = (self.t0, self.ta, self.tb, self.ty, self.tt)[stage]
+        return both, both
+
     def settle(self, stage):
         buf, a, b, c = self.buf, self.a, self.b, self.c
         if stage == 0:
@@ -238,7 +273,7 @@
             self.own[...] = added(self.own, self.tt)
 
 
-STATE_SEMS = sum(SumState.counts)
+STATE_SEMS = SumState.stages
 
 
 def state_scratch(rows, width):

time: 173 us -> 171 us (0.988)
  Pallas kernels: 171 us -> 169 us
    pallas_call x1, Pallas kernels: 155 us -> 153 us  [layer(): pl.pallas_call(functools.partial(layer_kernel, remote), out_shape=[jax.Sh...]
where the time goes in v6:
time: 171 us; the launch traced here: 170 us
  Pallas kernels  169 us (99%)
    pallas_call x1, Pallas kernels, layer(): pl.pallas_call(functools.partial(layer_kernel, remote), out_shape=[jax.Sh...  153 us
    pallas_call x1, Pallas kernels, finished(): pl.pallas_call(finish_kernel, out_shape=[jax.ShapeDtypeStruct(shape, kind...  16 us

profile of v6, /device:TPU:0, one launch (start us, length us, event | category | flops | bytes accessed | tf_op | source)
XLA Modules:
  0.0 169.9 jit_solution(11786792859547403834)
XLA Ops:
  0.7 153.1 %layer.1 = (bf16[2,4,4,96,384]{4,3,2,1,0:T(8,128)(2,1)}, bf16[2,4,4,96,384]{4,3,2,1,0:T(8,128)(2,1)}, bf16[2,4,4,96,384]{4,3,2,1,0:T(8,128)(2,1)}, bf16[2,4,4,32...) custom-call(bf16[1024,1536]{1,0:T(8,128)(2,1)} %tokens.1, ...), custom_call_target="tpu_custom_call" | custom-call | tf_op jit(solution)/shard_map/layer/pallas_call | solution.py:923
  153.7 16.0 %finish.1 = (bf16[1024,1536]{1,0:T(8,128)(2,1)}, f32[1024,1536]{1,0:T(8,128)}, f32[1536,768]{1,0:T(8,128)}, f32[1536,768]{1,0:T(8,128)}, f32[768,1536]{1,0:T(8,1...) custom-call(bf16[2,4,4,96,384]{4,3,2,1,0:T(8,128)(2,1)} %get-tuple-e, ...), custom_call_target="tpu_custom_call" | custom-call | tf_op jit(solution)/shard_map/finish/pallas_call | solution.py:1023

commit v7 on v6

--- a/solution.py
+++ b/solution.py
@@ -43,6 +43,8 @@
 
 
 def added(*refs):
+    if len(refs) == 2:
+        return refs[0][...] + refs[1][...]
     total = refs[0][...].astype(jnp.float32)
     for ref in refs[1:]:
         total = total + ref[...].astype(jnp.float32)

time: 171 us -> 170 us (level)
  no operation moved by 1% of the time
where the time goes in v7:
time: 170 us; the launch traced here: 169 us
  Pallas kernels  169 us (99%)
    pallas_call x1, Pallas kernels, layer(): pl.pallas_call(functools.partial(layer_kernel, remote), out_shape=[jax.Sh...  153 us
    pallas_call x1, Pallas kernels, finished(): pl.pallas_call(finish_kernel, out_shape=[jax.ShapeDtypeStruct(shape, kind...  16 us

profile of v7, /device:TPU:0, one launch (start us, length us, event | category | flops | bytes accessed | tf_op | source)
XLA Modules:
  0.0 169.4 jit_solution(9364179661234525778)
XLA Ops:
  0.7 152.6 %layer.1 = (bf16[2,4,4,96,384]{4,3,2,1,0:T(8,128)(2,1)}, bf16[2,4,4,96,384]{4,3,2,1,0:T(8,128)(2,1)}, bf16[2,4,4,96,384]{4,3,2,1,0:T(8,128)(2,1)}, bf16[2,4,4,32...) custom-call(bf16[1024,1536]{1,0:T(8,128)(2,1)} %tokens.1, ...), custom_call_target="tpu_custom_call" | custom-call | tf_op jit(solution)/shard_map/layer/pallas_call | solution.py:925
  153.3 16.0 %finish.1 = (bf16[1024,1536]{1,0:T(8,128)(2,1)}, f32[1024,1536]{1,0:T(8,128)}, f32[1536,768]{1,0:T(8,128)}, f32[1536,768]{1,0:T(8,128)}, f32[768,1536]{1,0:T(8,1...) custom-call(bf16[2,4,4,96,384]{4,3,2,1,0:T(8,128)(2,1)} %get-tuple-e, ...), custom_call_target="tpu_custom_call" | custom-call | tf_op jit(solution)/shard_map/finish/pallas_call | solution.py:1025
